TPU v7x, 768 devices: a whole 4x8x12 slice. The times are simulated.
768 devices in a mesh: node: 16 (over y, core), local: 48 (over x, z).
Axes of the slice: x: 4, y: 8, z: 12, core: 2. Of those that a mesh axis runs over, the one named last changes fastest.
Arguments:
- cotangent: float32 [6144, 3584], P('local', 'node'), may hold values from -6 to 6
- probs: float32 [6144, 8], P('local'), may hold values from 0.1 to 0.8
- routes: int32 [6144, 8], P('local'), may hold values from 0 to 143, all different within a row; in each aligned block of 128 rows (0 to 127, 128 to 255, ...) at most 9 rows name the same one
- gate_pre: bfloat16 [144, 432, 1024], P('local'), may hold values from -3 to 3
- up_pre: bfloat16 [144, 432, 1024], P('local'), may hold values from -3 to 3
- w_gate: bfloat16 [144, 3584, 1024], P('local', 'node'), may hold values from -0.1875 to 0.1875
- w_up: bfloat16 [144, 3584, 1024], P('local', 'node'), may hold values from -0.1875 to 0.1875
- w_down: bfloat16 [144, 3584, 1024], P('local', 'node'), may hold values from -0.1875 to 0.1875
Outputs:
- grad_tokens: float32 [6144, 3584], P('local', 'node')
- grad_probs: float32 [6144, 8], P('local')
Inputs may be any that keep to these rules, and one draw needn't show every extreme that they name: `routes`: each row names 8 different experts; in each aligned block of 128 rows (the tokens of one local shard) no expert is named more than 9 times, a bound that some block reaches.
All inputs are finite; a program needn't handle non-finite values.
Results may differ from a plain program's by a relative error of at most 0.0049.
Values may be sent and summed in bfloat16 or wider, within the bound.
No kernel may reach another device: no remote copies, remote signals or barrier semaphores. Data moves between devices by JAX's collectives and lax.ppermute only.
A program may use at most 64 MiB of HBM per device.

v0:
```python
import jax
import jax.numpy as jnp
from jax import lax
from jax.sharding import PartitionSpec as P

TOPK = 8
MOST = 9


def activation_grads(grad_full, gate_raw, up_raw, route_scale):
    gate_value = gate_raw.astype(jnp.float32)
    up_value = up_raw.astype(jnp.float32)
    sigmoid_gate = jax.nn.sigmoid(gate_value)
    silu_gate = gate_value * sigmoid_gate
    hidden_act = silu_gate * up_value
    score_rows = jnp.sum(hidden_act * grad_full, axis=2)
    scaled = route_scale.astype(jnp.float32)[:, :, None] * grad_full
    grad_up = (scaled * silu_gate).astype(jnp.bfloat16)
    grad_gate = (
        scaled * up_value * sigmoid_gate * (1.0 + gate_value * (1.0 - sigmoid_gate))
    ).astype(jnp.bfloat16)
    return (grad_gate, grad_up, score_rows)


def on_device(cotangent, probs, routes, gate_pre, up_pre, w_gate, w_up, w_down):
    tok_local = cotangent.shape[0]
    local_experts = w_gate.shape[0]
    home_count = lax.axis_size("local")
    experts_all = local_experts * home_count
    width_total = experts_all * MOST
    capacity = home_count * MOST
    flat_routes = routes.reshape(-1)
    onehot = (flat_routes[:, None] == jnp.arange(experts_all, dtype=jnp.int32)).astype(jnp.int32)
    before = jnp.cumsum(onehot, axis=0) - onehot
    slot_rank = jnp.sum(before * onehot, axis=1)
    column = (
        flat_routes % local_experts * home_count + flat_routes // local_experts
    ) * MOST + slot_rank
    picker = (column[:, None] == jnp.arange(width_total, dtype=jnp.int32)).astype(jnp.float32)
    per_token = picker.reshape(tok_local, TOPK, width_total).sum(axis=1)
    cotan_low = cotangent.astype(jnp.bfloat16)
    contract_rows = (((0,), (0,)), ((), ()))
    send_rows = lax.dot_general(
        per_token.astype(jnp.bfloat16), cotan_low, contract_rows, preferred_element_type=jnp.float32
    ).astype(jnp.bfloat16)
    send_weight = lax.dot_general(
        picker, probs.reshape(-1), contract_rows, precision=lax.Precision.HIGHEST
    ).astype(jnp.bfloat16)
    send_rows = send_rows.reshape(local_experts, home_count, MOST, -1)
    send_weight = send_weight.reshape(local_experts, home_count, MOST)
    rows_in, weight_in = (
        lax.all_to_all(send_rows, "local", split_axis=1, concat_axis=1, tiled=True),
        lax.all_to_all(send_weight, "local", split_axis=1, concat_axis=1, tiled=True),
    )
    rows_in = rows_in.reshape(local_experts, capacity, -1)
    weight_in = weight_in.reshape(local_experts, capacity)
    partial_value = jnp.einsum("ecd,edh->ech", rows_in, w_down, preferred_element_type=jnp.float32)
    grad_share = lax.psum_scatter(partial_value, "node", scatter_dimension=1, tiled=True)
    grad_full = lax.all_gather(grad_share, "node", axis=1, tiled=True)
    grad_gate, grad_up, score_rows = activation_grads(grad_full, gate_pre, up_pre, weight_in)
    back_rows = jnp.einsum("ech,edh->ecd", grad_gate, w_gate, preferred_element_type=jnp.float32)
    back_rows = back_rows + jnp.einsum(
        "ech,edh->ecd", grad_up, w_up, preferred_element_type=jnp.float32
    )
    back_rows = back_rows.reshape(local_experts, home_count, MOST, -1)
    score_rows = score_rows.reshape(local_experts, home_count, MOST)
    back_in, score_in = (
        lax.all_to_all(back_rows, "local", split_axis=1, concat_axis=1, tiled=True),
        lax.all_to_all(score_rows, "local", split_axis=1, concat_axis=1, tiled=True),
    )
    back_flat = back_in.reshape(width_total, -1)
    score_flat = score_in.reshape(width_total)
    grad_tokens = jnp.dot(per_token, back_flat, precision=lax.Precision.HIGHEST)
    grad_probs = jnp.dot(picker, score_flat, precision=lax.Precision.HIGHEST).reshape(
        tok_local, TOPK
    )
    return (grad_tokens, grad_probs)


def solution(mesh):
    return jax.shard_map(
        on_device,
        mesh=mesh,
        in_specs=(
            P("local", "node"),
            P("local", None),
            P("local", None),
            P("local", None, None),
            P("local", None, None),
            P("local", "node", None),
            P("local", "node", None),
            P("local", "node", None),
        ),
        out_specs=(P("local", "node"), P("local", None)),
        check_vma=False,
    )
```

profile of v0, /device:TPU:6, one launch (start us, length us, event | category | flops | bytes accessed | tf_op | source)
XLA Modules:
  0.0 389.2 jit_solution(15051302563446866002)
XLA Ops:
  7.2 0.0 all-reduce.3.cloned.1.call-start
  7.2 0.9 copy.114
  8.1 0.1 eq.69
  8.2 0.1 eq.73
  8.3 0.1 copy.116
  8.4 0.2 fusion.24
  8.7 0.1 broadcast_add_fusion
  8.7 0.5 copy.117
  9.3 0.2 fusion.30
  9.4 0.1 reduce_sum.30
  9.6 0.7 convert_reduce_fusion
  10.3 0.8 copy-done.1
  11.1 1.2 convolution_convert_fusion
  12.4 0.2 copy.123
  12.6 0.3 reshape.119
  12.9 0.6 copy.124
  13.6 54.7 %all_to_all.20 = bf16[3,48,9,224]{3,0,2,1:T(4,128)(2,1)S(1)} all-to-all(bf16[3,48,9,224]{3,0,2,1:T(4,128)(2,1)S(1)} %copy.124), channel_id=1, replica_groups=mesh['node'=16,'local'=48] {'local'}, dimensions={1} | all-to-all | bytes 1161216 | tf_op jit(solution)/shard_map/all_to_all | solution.py:52
  68.3 3.2 fusion.26
  71.5 0.0 all-reduce.3.cloned.1.call-update
  71.5 0.0 all-gather.2.cloned.1.call-start
  71.6 1.3 dynamic-slice
  73.5 128.5 %all-reduce.3.cloned.1.call-done = f32[3,432,1024]{2,1,0:T(8,128)} async-done(((f32[3,432,1024]{2,1,0:T(8,128)}), f32[3,432,1024]{2,1,0:T(8,128)}) %all-reduce.3.cloned.1.call-update) | async-done | bytes 5308432
  202.0 1.1 constant_dynamic-slice_fusion
  203.1 1.0 copy.126
  204.1 0.0 all-gather.2.cloned.1.call-update
  204.2 0.1 copy.119
  204.3 0.1 reshape.126
  204.4 1.8 fusion.23
  206.2 0.2 reshape.118
  206.4 24.1 %all_to_all.21 = bf16[3,48,9]{2,0,1:T(4,128)(2,1)S(1)} all-to-all(bf16[3,48,9]{2,0,1:T(4,128)(2,1)S(1)} %copy.120), channel_id=1, replica_groups=mesh['node'=16,'local'=48] {'local'}, dimensions={1} | all-to-all | bytes 5184 | tf_op jit(solution)/shard_map/all_to_all | solution.py:53
  230.5 0.1 copy.121
  230.7 0.1 copy.122
  230.8 0.1 reshape.125
  230.9 29.0 %all-gather.2.cloned.1.call-done = f32[3,432,1024]{2,0,1:T(4,128)} async-done(((f32[3,27,1024]{2,0,1:T(4,128)}), f32[3,432,1024]{2,0,1:T(4,128)}) %all-gather.2.cloned.1.call-update) | async-done | bytes 5308432 | tf_op jit(solution)/shard_map/all_gather | solution.py:59
  260.0 6.0 %fusion.5 = f32[3,432]{1,0:T(4,128)S(1)} fusion(bf16[3,432,1024]{2,1,0:T(8,128)(2,1)} %param.12, f32[3,432,1024]{2,0,1:T(4,128)} %all-gather.2.cloned.1.call-done, bf16[3,432,1024]{2,1,0:T(8,128)(2,1)} %param.11), kind=kLoop, calls=%fused_computation.11 | loop fusion | flops 11942640 | bytes 10622016 | tf_op jit(solution)/shard_map/reduce_sum | solution.py:16
  266.0 0.1 reshape.123
  266.1 0.7 copy.133
  266.8 13.6 %all-to-all-start.3 = ((f32[3,48,9]{2,0,1:T(4,128)}), f32[3,48,9]{2,0,1:T(4,128)S(1)}, u32[]{:S(2)}, u32[]{:S(2)}) async-start(f32[3,48,9]{2,0,1:T(4,128)} %copy.133), calls=%async_computation.3 | async-start | bytes 196608 | tf_op jit(solution)/shard_map/all_to_all | solution.py:69
  280.4 7.6 %fusion.15 = f32[3,432,224]{2,1,0:T(8,128)S(1)} fusion(bf16[3,224,1024]{2,1,0:T(8,128)(2,1)S(1)} %copy-done.6, f32[3,432,1024]{2,0,1:T(4,128)} %all-gather.2.cloned.1.call-done, f32[3,432]{1,0:T(4,128)S(1)} %reshape.125, bf16[3,432,1024]{2,1,0:T(8,128)(2,1)} %param.11), kind=kOutput, calls=%fused_computation.24 | convolution fusion | flops 605159424 | bytes 10505280 | tf_op jit(solution)/shard_map/ech,edh->ecd/dot_general | solution.py:62
  288.1 7.3 %fusion.20 = f32[3,432,224]{2,1,0:T(8,128)S(1)} fusion(f32[3,432,224]{2,1,0:T(8,128)S(1)} %fusion.15, bf16[3,224,1024]{2,1,0:T(8,128)(2,1)S(1)} %copy-done.7, bf16[3,432,1024]{2,1,0:T(8,128)(2,1)S(1)} %copy-done.3, bf16[3,432,1024]{2,1,0:T(8,128)(2,1)S(1)} %copy-done.2, f32[3,432,1024]{2,0,1:T(4,128)} %all-gather.2.cloned.1.call-done, ...), kind=kOutput, calls=%fused_computation.29 | convolution fusion | flops 612085248 | bytes 14320704 | tf_op jit(solution)/shard_map/ech,edh->ecd/dot_general | solution.py:61
  295.4 2.1 copy.128
  297.5 12.5 %all-to-all-start.2 = ((f32[3,48,9,224]{3,0,2,1:T(4,128)}), f32[3,48,9,224]{3,0,2,1:T(4,128)S(1)}, u32[]{:S(2)}, u32[]{:S(2)}) async-start(f32[3,48,9,224]{3,0,2,1:T(4,128)} %bitcast.3), calls=%async_computation.2 | async-start | bytes 3538944 | tf_op jit(solution)/shard_map/all_to_all | solution.py:68
  310.0 0.2 reshape.128
  310.2 1.9 fusion.13
  312.1 62.5 %all-to-all-done.2 = f32[3,48,9,224]{3,0,2,1:T(4,128)S(1)} async-done(((f32[3,48,9,224]{3,0,2,1:T(4,128)}), f32[3,48,9,224]{3,0,2,1:T(4,128)S(1)}, u32[]{:S(2)}, u32[]{:S(2)}) %all-to-all-start.2) | async-done | bytes 1161248 | tf_op jit(solution)/shard_map/all_to_all | solution.py:68
  374.7 1.8 copy.129
  376.4 1.7 reshape.122
  378.2 4.2 %fusion.46 = f32[128,224]{0,1:T(8,128)} fusion(f32[128,1296]{0,1:T(8,128)} %copy-done.1, f32[1296,224]{1,0:T(8,128)S(1)} %reshape.122), kind=kOutput, calls=%fused_computation.67 | convolution fusion | flops 445906944 | bytes 1939456 | tf_op jit(solution)/shard_map/dot_general | solution.py:73
  (24 shorter events, 0.2 us)
Async XLA Ops:
  7.2 61.1 %copy-start = (bf16[3,224,1024]{2,1,0:T(8,128)(2,1)S(1)}, bf16[3,224,1024]{2,1,0:T(8,128)(2,1)}, u32[]{:S(2)}) copy-start(bf16[3,224,1024]{2,1,0:T(8,128)(2,1)} %param.15) | copy-start | bytes 4128772
  7.2 2.4 copy-start.4
  7.2 194.9 %all-reduce.3.cloned.1.call-start = ((), (), s32[]{:S(2)}) async-start(), calls=%async_computation.5 | async-start | bytes 10616832
  10.3 0.8 copy-start.1
  71.5 132.6 %copy-start.5 = (f32[128,8]{0,1:T(8,128)S(1)}, f32[128,8]{0,1:T(8,128)}, u32[]{:S(2)}) copy-start(f32[128,8]{0,1:T(8,128)} %param.9) | copy-start | bytes 12292
  71.5 188.4 %all-gather.2.cloned.1.call-start = ((), (), s32[]{:S(2)}) async-start(), calls=%async_computation.4 | async-start | bytes 7520256 | tf_op jit(solution)/shard_map/all_gather | solution.py:59
  230.9 49.5 %copy-start.6 = (bf16[3,224,1024]{2,1,0:T(8,128)(2,1)S(1)}, bf16[3,224,1024]{2,1,0:T(8,128)(2,1)}, u32[]{:S(2)}) copy-start(bf16[3,224,1024]{2,1,0:T(8,128)(2,1)} %param.14) | copy-start | bytes 4128772
  266.8 30.7 %all-to-all-start.3 = ((f32[3,48,9]{2,0,1:T(4,128)}), f32[3,48,9]{2,0,1:T(4,128)S(1)}, u32[]{:S(2)}, u32[]{:S(2)}) async-start(f32[3,48,9]{2,0,1:T(4,128)} %copy.133), calls=%async_computation.3 | async-start | bytes 196608 | tf_op jit(solution)/shard_map/all_to_all | solution.py:69
  280.4 7.6 %copy-start.2 = (bf16[3,432,1024]{2,1,0:T(8,128)(2,1)S(1)}, bf16[3,432,1024]{2,1,0:T(8,128)(2,1)}, u32[]{:S(2)}) copy-start(bf16[3,432,1024]{2,1,0:T(8,128)(2,1)} %param.11) | copy-start | bytes 7962628
  280.4 7.6 %copy-start.3 = (bf16[3,432,1024]{2,1,0:T(8,128)(2,1)S(1)}, bf16[3,432,1024]{2,1,0:T(8,128)(2,1)}, u32[]{:S(2)}) copy-start(bf16[3,432,1024]{2,1,0:T(8,128)(2,1)} %param.12) | copy-start | bytes 7962628
  280.4 7.6 %copy-start.7 = (bf16[3,224,1024]{2,1,0:T(8,128)(2,1)S(1)}, bf16[3,224,1024]{2,1,0:T(8,128)(2,1)}, u32[]{:S(2)}) copy-start(bf16[3,224,1024]{2,1,0:T(8,128)(2,1)} %param.13) | copy-start | bytes 4128772
  297.5 77.1 %all-to-all-start.2 = ((f32[3,48,9,224]{3,0,2,1:T(4,128)}), f32[3,48,9,224]{3,0,2,1:T(4,128)S(1)}, u32[]{:S(2)}, u32[]{:S(2)}) async-start(f32[3,48,9,224]{3,0,2,1:T(4,128)} %bitcast.3), calls=%async_computation.2 | async-start | bytes 3538944 | tf_op jit(solution)/shard_map/all_to_all | solution.py:68
Sparse Core Ops, SparseCore 0:
  71.7 130.3 all-reduce.2
  204.5 55.4 all-gather.1
where the time goes:
time: 390 us; the launch traced here: 389 us
  waiting for transfers between devices  220 us (56%)
  blocking collectives  78.8 us (20%)
  matrix products  27.2 us (7%)
  starting transfers between devices  26.2 us (7%)
  between operations  15 us (4%)
  local copies, waits for them, and re-layouts  14.7 us (4%)
  other arithmetic  7.21 us (2%)
    unnamed x3, waiting for transfers between devices  129 us
    all_to_all x1, waiting for transfers between devices, on_device(): lax.all_to_all(back_rows, 'local', split_axis=1, concat_axis=1, tiled=True)  62.5 us
    all_to_all x1, blocking collectives, on_device(): lax.all_to_all(send_rows, 'local', split_axis=1, concat_axis=1, tiled=True)  54.7 us
    all_gather x1, waiting for transfers between devices, on_device(): grad_full = lax.all_gather(grad_share, 'node', axis=1, tiled=True)  29 us
    all_to_all x1, blocking collectives, on_device(): lax.all_to_all(send_weight, 'local', split_axis=1, concat_axis=1, tiled=T...  24.1 us
    all_to_all x1, starting transfers between devices, on_device(): lax.all_to_all(score_rows, 'local', split_axis=1, concat_axis=1, tiled=True)  13.6 us
    all_to_all x1, starting transfers between devices, on_device(): lax.all_to_all(back_rows, 'local', split_axis=1, concat_axis=1, tiled=True)  12.5 us
  transfers between devices with their start and end apart: 4, of which 3 were waited for; matrix products, arithmetic and copies ran while one was open for 6% of the time, Pallas kernels for 0%

commit v1 on v0

v1 whole, which is shorter than its diff:
```python
import functools

import jax
import jax.numpy as jnp
import numpy as np
from jax import lax
from jax.experimental import pallas as pl
from jax.experimental.pallas import tpu as pltpu
from jax.sharding import Mesh, PartitionSpec as P

MOST = 9
OWN = 3
SLOTS = 28
PAIR = 2 * SLOTS
LANE = 128
GROUP = 16
F32 = jnp.float32
BF16 = jnp.bfloat16
NT = (((1,), (1,)), ((), ()))
VMEM = pl.BlockSpec(memory_space=pltpu.VMEM)
SMEM = pl.BlockSpec(memory_space=pltpu.SMEM)
PARAMS = pltpu.CompilerParams(vmem_limit_bytes=48 * 1024 * 1024)


def dot(a, b):
    return jnp.dot(a, b, preferred_element_type=F32)


def dot_nt(a, b):
    return lax.dot_general(a, b, NT, preferred_element_type=F32)


def decode(row):
    second = (row >= SLOTS).astype(jnp.int32)
    place = row - SLOTS * second
    expert = (place >= MOST).astype(jnp.int32) + (place >= 2 * MOST).astype(jnp.int32)
    expert = jnp.minimum(expert, OWN - 1)
    return second, expert, place - MOST * expert


def rank_table(routes, experts):
    tokens, top = routes.shape
    lane = lax.broadcasted_iota(jnp.int32, (tokens, experts), 1)
    hits = [routes[:, k : k + 1] == lane for k in range(top)]
    named = sum(hit.astype(F32) for hit in hits)
    square = (tokens, tokens)
    earlier = lax.broadcasted_iota(jnp.int32, square, 0) > lax.broadcasted_iota(jnp.int32, square, 1)
    rank = dot(earlier.astype(F32).astype(BF16), named.astype(BF16))
    return hits, jnp.where(named > 0.0, rank, 31.0).astype(BF16)


def expert_rows(first, homes, experts):
    shape = (homes, PAIR, experts)
    _, expert, _ = decode(lax.broadcasted_iota(jnp.int32, shape, 1))
    wanted = (lax.broadcasted_iota(jnp.int32, shape, 0) + first) * OWN + expert
    return (lax.broadcasted_iota(jnp.int32, shape, 2) == wanted).reshape(homes * PAIR, experts)


def send_kernel(homes, routes_ref, probs_ref, cot_ref, out_ref, right):
    tokens, width = cot_ref.shape
    experts = homes * OWN
    routes = routes_ref[...]
    hits, ranks = rank_table(routes, experts)
    probs = probs_ref[...]
    weight = sum(jnp.where(hit, probs[:, k : k + 1], 0.0) for k, hit in enumerate(hits)).astype(BF16)
    right[...] = jnp.zeros_like(right)
    right[0:tokens, :] = cot_ref[:, 0:LANE].astype(BF16)
    right[tokens : 2 * tokens, 0 : width - LANE] = cot_ref[:, LANE:width].astype(BF16)
    mark = lax.broadcasted_iota(jnp.int32, (tokens, LANE), 1) == width - LANE
    right[2 * tokens : 3 * tokens, :] = mark.astype(F32).astype(BF16)
    step = 8 if homes % 8 == 0 else homes
    for first in range(0, homes, step):
        pick = expert_rows(first, step, experts).astype(F32).astype(BF16)
        rank_of = dot_nt(pick, ranks)
        weight_of = dot_nt(pick, weight)
        shape = (step, PAIR, tokens)
        second, _, slot = decode(lax.broadcasted_iota(jnp.int32, shape, 1))
        second = second.reshape(step * PAIR, tokens) > 0
        here = rank_of == slot.astype(F32).reshape(step * PAIR, tokens)
        left = jnp.concatenate(
            [
                jnp.where(here & ~second, 1.0, 0.0).astype(BF16),
                jnp.where(here & second, 1.0, 0.0).astype(BF16),
                jnp.where(here & second, weight_of, 0.0).astype(BF16),
            ],
            axis=1,
        )
        out_ref[first * PAIR : (first + step) * PAIR, :] = dot(left, right[...]).astype(BF16)


def down_half(half, share, rows_ref, w_ref, out_ref):
    capacity = out_ref.shape[1] - share
    whole = half * (OWN - 1)
    width = w_ref.shape[1]
    hidden = w_ref.shape[2]
    left = rows_ref[whole, 0:capacity, 0:width]
    part = rows_ref[1, pl.ds(pl.multiple_of(half * share, 16), share), 0:width]
    tile = 2 * LANE
    for n in range(hidden // tile):
        columns = slice(n * tile, (n + 1) * tile)
        for a, top, count in (
            (dot(left, w_ref[whole, :, columns]), 0, capacity),
            (dot(part, w_ref[1, :, columns]), capacity, share),
        ):
            out_ref[2 * n, top : top + count, :] = a[:, :LANE].astype(BF16)
            out_ref[2 * n + 1, top : top + count, :] = a[:, LANE:].astype(BF16)


def unpack_kernel(share, half_ref, got_ref, w_ref, rows_ref, out_ref):
    sources = got_ref.shape[0] // PAIR
    capacity = sources * MOST
    rows, columns = GROUP * MOST, GROUP * PAIR
    at = lax.broadcasted_iota(jnp.int32, (1, columns), 1)
    source = jnp.floor((at.astype(F32) + 0.5) * (1.0 / PAIR)).astype(jnp.int32)
    second, expert, slot = decode(at - PAIR * source)
    goal = jnp.where(slot < MOST, (2 * expert + second) * rows + source * MOST + slot, -1)
    select = lax.broadcasted_iota(jnp.int32, (2 * OWN * rows, columns), 0) == goal
    select = select.astype(F32).astype(BF16)
    rows_ref[:, capacity:, :] = jnp.zeros((OWN, rows_ref.shape[1] - capacity, 2 * LANE), BF16)
    for g in range(sources // GROUP):
        piece = dot(select, got_ref[g * columns : (g + 1) * columns, :]).astype(BF16)
        for e in range(OWN):
            for second in range(2):
                top = (2 * e + second) * rows
                rows_ref[e, g * rows : (g + 1) * rows, second * LANE : (second + 1) * LANE] = piece[top : top + rows]
    down_half(1 - half_ref[0], share, rows_ref, w_ref, out_ref)


def down_kernel(share, half_ref, rows_ref, w_ref, out_ref):
    down_half(half_ref[0], share, rows_ref, w_ref, out_ref)


def back_kernel(share, grad_ref, rows_ref, gate_ref, up_ref, wg_ref, wu_ref, out_ref, gate_grad, up_grad, weight, score, back):
    sources = out_ref.shape[0] // PAIR
    capacity = sources * MOST
    width = wg_ref.shape[1]
    blocks = gate_ref.shape[2] // LANE
    rows, columns = GROUP * MOST, GROUP * PAIR
    tail = capacity - share
    for e, low, count, half, top in (
        (0, 0, capacity, 0, 0),
        (OWN - 1, 0, capacity, 1, 0),
        (1, 0, share, 0, capacity),
        (1, share, tail, 1, capacity),
    ):
        here = slice(0, count)
        weight[here] = jnp.broadcast_to(
            rows_ref[e, low : low + count, LANE:].astype(F32)[:, width - LANE : width - LANE + 1], (count, LANE)
        )
        score[here] = jnp.zeros((count, LANE), F32)

        def block(b, carry, e=e, low=low, count=count, half=half, top=top, here=here):
            columns = pl.ds(pl.multiple_of(b * LANE, LANE), LANE)
            grad = grad_ref[2 * b + half, top : top + count, :].astype(F32)
            gate = gate_ref[e, low : low + count, columns].astype(F32)
            up = up_ref[e, low : low + count, columns].astype(F32)
            sig = lax.logistic(gate)
            silu = gate * sig
            score[here] += silu * up * grad
            scaled = weight[here] * grad
            up_grad[here, columns] = (scaled * silu).astype(BF16)
            gate_grad[here, columns] = (scaled * up * sig * (1.0 + gate * (1.0 - sig))).astype(BF16)
            return carry

        lax.fori_loop(0, blocks, block, 0)
        total = dot_nt(gate_grad[here], wg_ref[e]) + dot_nt(up_grad[here], wu_ref[e])
        sums = jnp.sum(score[here], axis=1, keepdims=True)
        high = sums.astype(BF16).astype(F32)
        at = lax.broadcasted_iota(jnp.int32, (count, 2 * LANE - width), 1)
        ends = jnp.where(at == 0, high, jnp.where(at == 1, sums - high, 0.0)).astype(BF16)
        total = total.astype(BF16)
        done = 0
        while done < count:
            group, inner = divmod(low + done, rows)
            n = min(rows - inner, count - done)
            first = group * 2 * OWN * rows + 2 * e * rows + inner
            back[first : first + n, :] = total[done : done + n, 0:LANE]
            back[first + rows : first + rows + n, 0 : width - LANE] = total[done : done + n, LANE:width]
            back[first + rows : first + rows + n, width - LANE :] = ends[done : done + n]
            done += n
    shape = (GROUP, PAIR, 2 * OWN * rows)
    second, expert, slot = decode(lax.broadcasted_iota(jnp.int32, shape, 1))
    goal = (2 * expert + second) * rows + lax.broadcasted_iota(jnp.int32, shape, 0) * MOST + slot
    select = (lax.broadcasted_iota(jnp.int32, shape, 2) == goal) & (slot < MOST)
    select = select.reshape(columns, 2 * OWN * rows).astype(F32).astype(BF16)
    for g in range(sources // GROUP):
        piece = dot(select, back[g * 2 * OWN * rows : (g + 1) * 2 * OWN * rows, :])
        out_ref[g * columns : (g + 1) * columns, :] = piece.astype(BF16)


def combine_kernel(homes, routes_ref, slots_ref, got_ref, tokens_ref, probs_ref):
    tokens, width = tokens_ref.shape
    experts = homes * OWN
    hits, ranks = rank_table(routes_ref[...], experts)
    pick = expert_rows(0, homes, experts)
    rank_of = dot_nt(ranks, pick.astype(F32).astype(BF16))
    first = (rank_of == slots_ref[0:1, :]).astype(F32).astype(BF16)
    second = (rank_of == slots_ref[1:2, :]).astype(F32).astype(BF16)
    tokens_ref[:, 0:LANE] = dot(first, got_ref[...])
    tokens_ref[:, LANE:width] = dot(second, got_ref[...])[:, : width - LANE]
    ends = got_ref[...].astype(F32)
    high = jnp.where(pick, ends[:, width - LANE : width - LANE + 1], 0.0).astype(BF16)
    low = jnp.where(pick, ends[:, width - LANE + 1 : width - LANE + 2], 0.0).astype(BF16)
    table = dot(second, high) + dot(second, low)
    at = lax.broadcasted_iota(jnp.int32, probs_ref.shape, 1)
    result = jnp.zeros(probs_ref.shape, F32)
    for k, hit in enumerate(hits):
        mine = jnp.sum(jnp.where(hit, table, 0.0), axis=1, keepdims=True)
        result = jnp.where(at == k, mine, result)
    probs_ref[...] = result


def cost(flops, nbytes):
    return pl.CostEstimate(flops=flops, bytes_accessed=nbytes, transcendentals=0)


def on_device(cotangent, probs, routes, gate_pre, up_pre, w_gate, w_up, w_down):
    tokens, width = cotangent.shape
    hidden = w_gate.shape[2]
    homes = lax.axis_size("x") * lax.axis_size("z")
    ring = lax.axis_size("y")
    capacity = homes * MOST
    share = -(-capacity // 32) * 16
    blocks = hidden // LANE
    packed = homes * PAIR
    here = lax.axis_index("core").astype(jnp.int32)[None]
    half_shape = jax.ShapeDtypeStruct((blocks, capacity + share, LANE), BF16)
    rows_shape = jax.ShapeDtypeStruct((OWN, 2 * share, 2 * LANE), BF16)

    with jax.named_scope("send_rows"):
        send = pl.pallas_call(
            functools.partial(send_kernel, homes),
            out_shape=jax.ShapeDtypeStruct((packed, LANE), BF16),
            in_specs=[VMEM] * 3,
            out_specs=VMEM,
            scratch_shapes=[pltpu.VMEM((3 * tokens, LANE), BF16)],
            compiler_params=PARAMS,
            cost_estimate=cost(10**9, 10**6),
        )(routes, probs, cotangent)
    with jax.named_scope("dispatch"):
        got = lax.all_to_all(send.reshape(homes, PAIR, LANE), ("x", "z"), 0, 0, tiled=True).reshape(packed, LANE)
    with jax.named_scope("down_other"):
        rows, other = pl.pallas_call(
            functools.partial(unpack_kernel, share),
            out_shape=(rows_shape, half_shape),
            in_specs=[SMEM, VMEM, VMEM],
            out_specs=(VMEM, VMEM),
            compiler_params=PARAMS,
            cost_estimate=cost(10**9, 4 * 10**6),
        )(here, got, w_down)
    with jax.named_scope("swap_cores"):
        swapped = lax.ppermute(other, "core", [(0, 1), (1, 0)])
    with jax.named_scope("down_own"):
        own = pl.pallas_call(
            functools.partial(down_kernel, share),
            out_shape=half_shape,
            in_specs=[SMEM, VMEM, VMEM],
            out_specs=VMEM,
            compiler_params=PARAMS,
            cost_estimate=cost(10**9, 4 * 10**6),
        )(here, rows, w_down)
    with jax.named_scope("add_cores"):
        chip = (own.astype(F32) + swapped.astype(F32)).astype(BF16)
    with jax.named_scope("sum_over_y"):
        parts = lax.all_to_all(chip, "y", 0, 0, tiled=True)
        share_sum = jnp.sum(parts.astype(F32), axis=0).astype(BF16)
    with jax.named_scope("gather_hidden"):
        grad = lax.all_gather(share_sum, ("y", "core"), axis=0)
    with jax.named_scope("back"):
        back = pl.pallas_call(
            functools.partial(back_kernel, share),
            out_shape=jax.ShapeDtypeStruct((packed, LANE), BF16),
            in_specs=[VMEM] * 6,
            out_specs=VMEM,
            scratch_shapes=[
                pltpu.VMEM((capacity, hidden), BF16),
                pltpu.VMEM((capacity, hidden), BF16),
                pltpu.VMEM((capacity, LANE), F32),
                pltpu.VMEM((capacity, LANE), F32),
                pltpu.VMEM((homes * MOST * 2 * OWN, LANE), BF16),
            ],
            compiler_params=PARAMS,
            cost_estimate=cost(2 * 10**9, 10**7),
        )(grad, rows, gate_pre, up_pre, w_gate, w_up)
    with jax.named_scope("way_back"):
        home = lax.all_to_all(back.reshape(homes, PAIR, LANE), ("x", "z"), 0, 0, tiled=True).reshape(packed, LANE)
    row = np.arange(packed) % PAIR
    place = row % SLOTS
    slot = np.where(place < OWN * MOST, place % MOST, 99)
    slots = np.stack([np.where(row < SLOTS, slot, 99), np.where(row < SLOTS, 99, slot)]).astype(np.float32)
    with jax.named_scope("combine"):
        return pl.pallas_call(
            functools.partial(combine_kernel, homes),
            out_shape=(
                jax.ShapeDtypeStruct((tokens, width), F32),
                jax.ShapeDtypeStruct(probs.shape, F32),
            ),
            in_specs=[VMEM] * 3,
            out_specs=(VMEM, VMEM),
            compiler_params=PARAMS,
            cost_estimate=cost(10**9, 10**6),
        )(routes, jnp.asarray(slots), home)


def solution(mesh):
    node, local = ("y", "core"), ("x", "z")
    y, x = mesh.devices.shape[0] // 2, 4
    parts = Mesh(mesh.devices.reshape(y, 2, x, -1), node + local)
    return jax.shard_map(
        on_device,
        mesh=parts,
        in_specs=(
            P(local, node),
            P(local, None),
            P(local, None),
            P(local, None, None),
            P(local, None, None),
            P(local, node, None),
            P(local, node, None),
            P(local, node, None),
        ),
        out_specs=(P(local, node), P(local, None)),
        check_vma=False,
    )
```

time: 390 us -> 217 us (0.56)
  waiting for transfers between devices: 220 us -> 67.6 us
  matrix products: 27.2 us -> 0 us
  Pallas kernels: 0 us -> 21.4 us
  local copies, waits for them, and re-layouts: 14.7 us -> 4 us
  blocking collectives: 78.8 us -> 86.4 us
  starting transfers between devices: 26.2 us -> 20.6 us
  other arithmetic: 7.21 us -> 2.68 us
    unnamed x3 -> x1, waiting for transfers between devices: 129 us -> 0.02 us
    all_to_all x2 -> x1, waiting for transfers between devices: 62.5 us -> 30 us  [on_device(): lax.all_to_all(send.reshape(homes, PAIR, LANE), ('x', 'z'), 0, 0, tiled=T...]
    dot_general x7 -> x0, matrix products: 27.2 us -> none  [the longest x1 7.6 us: on_device(): jnp.einsum('ech,edh->ecd', grad_up, w_up, preferred_element_type=jnp.floa...]
    pallas_call x0 -> x5, Pallas kernels: none -> 21.4 us  [the longest x1 13.1 us: on_device(): pl.pallas_call(functools.partial(back_kernel, share), out_shape=jax.Shape...]
    all_to_all x2, blocking collectives: 78.8 us -> 86.4 us  [the longest x1 43.9 us: on_device(): lax.all_to_all(back.reshape(homes, PAIR, LANE), ('x', 'z'), 0, 0, tiled=T...]
    all_to_all x2 -> x1, starting transfers between devices: 26.1 us -> 18.7 us  [on_device(): lax.all_to_all(send.reshape(homes, PAIR, LANE), ('x', 'z'), 0, 0, tiled=T...]
    all_gather x1, waiting for transfers between devices: 29 us -> 35.1 us  [on_device(): grad = lax.all_gather(share_sum, ('y', 'core'), axis=0)]
    reduce_sum x3 -> x1, other arithmetic: 6.86 us -> 2.33 us  [on_device(): share_sum = jnp.sum(parts.astype(F32), axis=0).astype(BF16)]
  transfers between devices with their start and end apart: 4 -> 3, of which waited for: 3 -> 3; matrix products, arithmetic and copies ran while one was open for 6% -> 0% of each run, Pallas kernels for 0% -> 0%
where the time goes in v1:
time: 217 us
  blocking collectives  86.4 us (40%)
  waiting for transfers between devices  67.6 us (31%)
  Pallas kernels  21.4 us (10%)
  starting transfers between devices  20.6 us (9%)
  between operations  14.1 us (6%)
  local copies, waits for them, and re-layouts  4 us (2%)
  other arithmetic  2.68 us (1%)
    all_to_all x1, blocking collectives, on_device(): lax.all_to_all(back.reshape(homes, PAIR, LANE), ('x', 'z'), 0, 0, tiled=T...  43.9 us
    all_to_all x1, blocking collectives, on_device(): parts = lax.all_to_all(chip, 'y', 0, 0, tiled=True)  42.5 us
    all_gather x1, waiting for transfers between devices, on_device(): grad = lax.all_gather(share_sum, ('y', 'core'), axis=0)  35.1 us
    all_to_all x1, waiting for transfers between devices, on_device(): lax.all_to_all(send.reshape(homes, PAIR, LANE), ('x', 'z'), 0, 0, tiled=T...  30 us
    all_to_all x1, starting transfers between devices, on_device(): lax.all_to_all(send.reshape(homes, PAIR, LANE), ('x', 'z'), 0, 0, tiled=T...  18.7 us
    pallas_call x1, Pallas kernels, on_device(): pl.pallas_call(functools.partial(back_kernel, share), out_shape=jax.Shape...  13.1 us
  transfers between devices with their start and end apart: 3, of which 3 were waited for; matrix products, arithmetic and copies ran while one was open for 0% of the time, Pallas kernels for 0%

profile of v1, /device:TPU:6, one launch (start us, length us, event | category | flops | bytes accessed | tf_op | source)
XLA Modules:
  0.0 216.8 jit_solution(8532706358056229639)
XLA Ops:
  7.2 0.8 copy.14.routes_ref
  8.0 0.8 copy.12.probs_ref
  8.7 1.0 copy.13.cot_ref
  9.7 2.9 %send_rows.1 = bf16[2688,128]{1,0:T(8,128)(2,1)} custom-call(s32[128,8]{1,0:T(8,128)S(1)} %copy.14.routes_ref, f32[128,8]{1,0:T(8,128)S(1)} %copy.12.probs_ref, f32[128,224]{1,0:T(8,128)S(1)} %copy.13.cot_ref), custom_call_target="tpu_custom_call" | custom-call | flops 1000000000 | bytes 1000000 | tf_op jit(solution)/shard_map/send_rows/pallas_call | solution.py:231
  12.7 0.0 copy-start.2
  12.7 18.7 %all-to-all-start = ((bf16[48,56,128]{2,1,0:T(8,128)(2,1)}), bf16[48,56,128]{2,1,0:T(8,128)(2,1)S(1)}, u32[]{:S(2)}, u32[]{:S(2)}) async-start(bf16[48,56,128]{2,1,0:T(8,128)(2,1)} %bitcast.1), calls=%async_computation | async-start | bytes 1376256 | tf_op jit(solution)/shard_map/dispatch/all_to_all | solution.py:241
  31.4 0.0 all-gather.3.cloned.1.call-start
  31.4 30.0 %all-to-all-done = bf16[48,56,128]{2,1,0:T(8,128)(2,1)S(1)} async-done(((bf16[48,56,128]{2,1,0:T(8,128)(2,1)}), bf16[48,56,128]{2,1,0:T(8,128)(2,1)S(1)}, u32[]{:S(2)}, u32[]{:S(2)}) %all-to-all-start) | async-done | bytes 688160 | tf_op jit(solution)/shard_map/dispatch/all_to_all | solution.py:241
  61.4 0.0 copy-done.2
  61.4 2.4 %down_other.1 = (bf16[3,448,256]{2,1,0:T(8,128)(2,1)S(1)}, bf16[8,656,128]{2,1,0:T(8,128)(2,1)S(1)}) custom-call(s32[1]{0:T(128)} %bitcast.half_ref, bf16[2688,128]{1,0:T(8,128)(2,1)S(1)} %bitcast.7, bf16[3,224,1024]{2,1,0:T(8,128)(2,1)S(1)} %copy-done.2), custom_call_target="tpu_custom_call" | custom-call | flops 1000000000 | bytes 4000000 | tf_op jit(solution)/shard_map/down_other/pallas_call | solution.py:243
  63.8 1.9 collective-permute-start
  65.8 0.5 down_own.1
  66.3 2.5 %collective-permute-done = bf16[8,656,128]{2,1,0:T(8,128)(2,1)S(1)} collective-permute-done((bf16[8,656,128]{2,1,0:T(8,128)(2,1)S(1)}, bf16[8,656,128]{2,1,0:T(8,128)(2,1)S(1)}, u32[]{:S(2)}, u32[]{:S(2)}) %collective-permute-start) | collective-permute-done | bytes 1343520 | tf_op jit(solution)/shard_map/swap_cores/ppermute | solution.py:252
  68.8 0.3 add_convert_fusion
  69.2 0.0 copy-start.1
  69.2 42.5 %all_to_all.15 = bf16[8,656,128]{2,1,0:T(8,128)(2,1)} all-to-all(bf16[8,656,128]{2,1,0:T(8,128)(2,1)S(1)} %add_convert_fusion), channel_id=1, replica_groups=mesh['y'=8,'core'=2,'x'=4,'z'=12] {'y'}, dimensions={0} | all-to-all | bytes 2686976 | tf_op jit(solution)/shard_map/sum_over_y/all_to_all | solution.py:265
  111.7 0.0 copy-start
  111.7 2.3 %reduce_sum.12 = bf16[656,128]{1,0:T(8,128)(2,1)} reduce(bf16[8,656,128]{2,1,0:T(8,128)(2,1)} %all_to_all.15, bf16[]{:T(256)} %constant.9.clone.1), dimensions={0}, to_apply=%region_0.0 | reduce | flops 587776 | bytes 1511426 | tf_op jit(solution)/shard_map/sum_over_y/reduce_sum | solution.py:266
  114.0 0.0 all-gather.3.cloned.1.call-update
  114.0 35.1 %all-gather.3.cloned.1.call-done = bf16[10496,128]{1,0:T(8,128)(2,1)} async-done(((bf16[656,128]{1,0:T(8,128)(2,1)}), bf16[10496,128]{1,0:T(8,128)(2,1)}) %all-gather.3.cloned.1.call-update) | async-done | bytes 2686992 | tf_op jit(solution)/shard_map/gather_hidden/all_gather | solution.py:268
  149.1 0.0 copy-done.1
  149.1 0.0 copy-done
  149.1 13.1 %back.1 = bf16[2688,128]{1,0:T(8,128)(2,1)S(1)} custom-call(bf16[16,656,128]{2,1,0:T(8,128)(2,1)} %bitcast.9, bf16[3,448,256]{2,1,0:T(8,128)(2,1)S(1)} %get-tuple-element.4.rows_ref, bf16[3,432,1024]{2,1,0:T(8,128)(2,1)} %gate_ref.1, bf16[3,432,1024]{2,1,0:T(8,128)(2,1)} %up_ref.1, bf16[3,224,1024]{2,1,0:T(8,128)(2,1)S(1)} %copy-done, ...), custom_call_target="tpu_custom_call" | custom-call | flops 2000000000 | bytes 10000000 | tf_op jit(solution)/shard_map/back/pallas_call | solution.py:270
  162.2 0.0 copy-start.3
  162.2 43.9 %all_to_all.16 = bf16[48,56,128]{2,1,0:T(8,128)(2,1)S(1)} all-to-all(bf16[48,56,128]{2,1,0:T(8,128)(2,1)S(1)} %bitcast.6), channel_id=1, replica_groups=mesh['y'=8,'core'=2,'x'=4,'z'=12] {'x','z'}, dimensions={0} | all-to-all | bytes 1376256 | tf_op jit(solution)/shard_map/way_back/all_to_all | solution.py:286
  206.1 0.0 copy-done.3
  206.1 2.5 %combine.1 = (f32[128,224]{1,0:T(8,128)S(1)}, f32[128,8]{1,0:T(8,128)S(1)}) custom-call(s32[128,8]{1,0:T(8,128)S(1)} %copy.14.routes_ref, f32[2,2688]{1,0:T(2,128)S(1)} %copy-done.3, bf16[2688,128]{1,0:T(8,128)(2,1)S(1)} %bitcast.8), custom_call_target="tpu_custom_call" | custom-call | flops 1000000000 | bytes 1000000 | tf_op jit(solution)/shard_map/combine/pallas_call | solution.py:292
  208.6 0.7 copy.15
  209.3 0.7 copy.16
Async XLA Ops:
  12.7 48.7 %copy-start.2 = (bf16[3,224,1024]{2,1,0:T(8,128)(2,1)S(1)}, bf16[3,224,1024]{2,1,0:T(8,128)(2,1)}, u32[]{:S(2)}) copy-start(bf16[3,224,1024]{2,1,0:T(8,128)(2,1)} %w_ref.3) | copy-start | bytes 4128772
  12.7 48.7 %all-to-all-start = ((bf16[48,56,128]{2,1,0:T(8,128)(2,1)}), bf16[48,56,128]{2,1,0:T(8,128)(2,1)S(1)}, u32[]{:S(2)}, u32[]{:S(2)}) async-start(bf16[48,56,128]{2,1,0:T(8,128)(2,1)} %bitcast.1), calls=%async_computation | async-start | bytes 1376256 | tf_op jit(solution)/shard_map/dispatch/all_to_all | solution.py:241
  31.4 117.8 %all-gather.3.cloned.1.call-start = ((), (), s32[]{:S(2)}) async-start(), calls=%async_computation.3 | async-start | bytes 2854912 | tf_op jit(solution)/shard_map/gather_hidden/all_gather | solution.py:268
  63.8 5.0 %collective-permute-start = (bf16[8,656,128]{2,1,0:T(8,128)(2,1)S(1)}, bf16[8,656,128]{2,1,0:T(8,128)(2,1)S(1)}, u32[]{:S(2)}, u32[]{:S(2)}) collective-permute-start(bf16[8,656,128]{2,1,0:T(8,128)(2,1)S(1)} %get-tuple-element.5), channel_id=1, source_target_pairs={{0,48},{48,0},{1,49},{49,1},{2,50},{50,2},{3,51},{51,3},{4,52},{52... | collective-permute-start | bytes 4030472 | tf_op jit(solution)/shard_map/swap_cores/ppermute | solution.py:252
  69.2 79.9 %copy-start.1 = (bf16[3,224,1024]{2,1,0:T(8,128)(2,1)S(1)}, bf16[3,224,1024]{2,1,0:T(8,128)(2,1)}, u32[]{:S(2)}) copy-start(bf16[3,224,1024]{2,1,0:T(8,128)(2,1)} %wu_ref.1) | copy-start | bytes 4128772
  111.7 37.4 %copy-start = (bf16[3,224,1024]{2,1,0:T(8,128)(2,1)S(1)}, bf16[3,224,1024]{2,1,0:T(8,128)(2,1)}, u32[]{:S(2)}) copy-start(bf16[3,224,1024]{2,1,0:T(8,128)(2,1)} %wg_ref.1) | copy-start | bytes 4128772
  162.2 43.9 %copy-start.3 = (f32[2,2688]{1,0:T(2,128)S(1)}, f32[2,2688]{1,0:T(2,128)}, u32[]{:S(2)}) copy-start(f32[2,2688]{1,0:T(2,128)} %constant.10.clone.slots_ref) | copy-start | bytes 64516
Sparse Core Ops, SparseCore 0:
  114.1 34.9 all-gather.2

commit v2 on v1

--- a/solution.py
+++ b/solution.py
@@ -19,7 +19,7 @@
 NT = (((1,), (1,)), ((), ()))
 VMEM = pl.BlockSpec(memory_space=pltpu.VMEM)
 SMEM = pl.BlockSpec(memory_space=pltpu.SMEM)
-PARAMS = pltpu.CompilerParams(vmem_limit_bytes=48 * 1024 * 1024)
+PARAMS = pltpu.CompilerParams(vmem_limit_bytes=32 * 1024 * 1024)
 
 
 def dot(a, b):
@@ -57,17 +57,17 @@
 
 
 def send_kernel(homes, routes_ref, probs_ref, cot_ref, out_ref, right):
-    tokens, width = cot_ref.shape
+    width, tokens = cot_ref.shape
     experts = homes * OWN
-    routes = routes_ref[...]
+    routes = routes_ref[...].astype(F32).T.astype(jnp.int32)
     hits, ranks = rank_table(routes, experts)
-    probs = probs_ref[...]
+    probs = probs_ref[...].T
     weight = sum(jnp.where(hit, probs[:, k : k + 1], 0.0) for k, hit in enumerate(hits)).astype(BF16)
     right[...] = jnp.zeros_like(right)
-    right[0:tokens, :] = cot_ref[:, 0:LANE].astype(BF16)
-    right[tokens : 2 * tokens, 0 : width - LANE] = cot_ref[:, LANE:width].astype(BF16)
-    mark = lax.broadcasted_iota(jnp.int32, (tokens, LANE), 1) == width - LANE
-    right[2 * tokens : 3 * tokens, :] = mark.astype(F32).astype(BF16)
+    right[:, 0:tokens] = cot_ref[0:LANE, :].astype(BF16)
+    right[0 : width - LANE, tokens : 2 * tokens] = cot_ref[LANE:width, :].astype(BF16)
+    mark = lax.broadcasted_iota(jnp.int32, (LANE, tokens), 0) == width - LANE
+    right[:, 2 * tokens : 3 * tokens] = mark.astype(F32).astype(BF16)
     step = 8 if homes % 8 == 0 else homes
     for first in range(0, homes, step):
         pick = expert_rows(first, step, experts).astype(F32).astype(BF16)
@@ -85,10 +85,10 @@
             ],
             axis=1,
         )
-        out_ref[first * PAIR : (first + step) * PAIR, :] = dot(left, right[...]).astype(BF16)
-
-
-def down_half(half, share, rows_ref, w_ref, out_ref):
+        out_ref[first * PAIR : (first + step) * PAIR, :] = dot_nt(left, right[...]).astype(BF16)
+
+
+def down_half(half, share, rows_ref, w_ref, out_ref, plus_ref=None):
     capacity = out_ref.shape[1] - share
     whole = half * (OWN - 1)
     width = w_ref.shape[1]
@@ -102,8 +102,10 @@
             (dot(left, w_ref[whole, :, columns]), 0, capacity),
             (dot(part, w_ref[1, :, columns]), capacity, share),
         ):
-            out_ref[2 * n, top : top + count, :] = a[:, :LANE].astype(BF16)
-            out_ref[2 * n + 1, top : top + count, :] = a[:, LANE:].astype(BF16)
+            for m, piece in ((2 * n, a[:, :LANE]), (2 * n + 1, a[:, LANE:])):
+                if plus_ref is not None:
+                    piece = piece + plus_ref[m, top : top + count, :].astype(F32)
+                out_ref[m, top : top + count, :] = piece.astype(BF16)
 
 
 def unpack_kernel(share, half_ref, got_ref, w_ref, rows_ref, out_ref):
@@ -126,15 +128,48 @@
     down_half(1 - half_ref[0], share, rows_ref, w_ref, out_ref)
 
 
-def down_kernel(share, half_ref, rows_ref, w_ref, out_ref):
-    down_half(half_ref[0], share, rows_ref, w_ref, out_ref)
-
-
-def back_kernel(share, grad_ref, rows_ref, gate_ref, up_ref, wg_ref, wu_ref, out_ref, gate_grad, up_grad, weight, score, back):
+def down_kernel(share, half_ref, rows_ref, w_ref, plus_ref, out_ref):
+    down_half(half_ref[0], share, rows_ref, w_ref, out_ref, plus_ref)
+
+
+def factor_kernel(gate_ref, up_ref, up_factor_ref, gate_factor_ref):
+    experts, capacity, hidden = gate_ref.shape
+    step = 48
+    for e in range(experts):
+
+        def part(i, carry, e=e):
+            rows = pl.ds(pl.multiple_of(i * step, step), step)
+            for b in range(0, hidden, LANE):
+                gate = gate_ref[e, rows, b : b + LANE].astype(F32)
+                up = up_ref[e, rows, b : b + LANE].astype(F32)
+                sig = lax.logistic(gate)
+                up_factor_ref[e, rows, b : b + LANE] = gate * sig
+                gate_factor_ref[e, rows, b : b + LANE] = up * sig * (1.0 + gate * (1.0 - sig))
+            return carry
+
+        lax.fori_loop(0, capacity // step, part, 0)
+
+
+def sum_kernel(parts_ref, out_ref):
+    sources, rows, _ = parts_ref.shape
+    total = parts_ref[0].astype(F32)
+    for i in range(1, sources):
+        total = total + parts_ref[i].astype(F32)
+    largest = jnp.max(jnp.max(jnp.abs(total), axis=0, keepdims=True), axis=1, keepdims=True)
+    largest = jnp.broadcast_to(jnp.maximum(largest, 1e-35), (16, LANE))
+    power = jnp.clip(jnp.floor(jnp.log2(largest)), -100.0, 100.0)
+    out_ref[0:rows, :] = total * jnp.exp2(-power)[0:1]
+    out_ref[rows:, :] = power
+
+
+def back_kernel(
+    share, grad_ref, rows_ref, up_ref, up_factor_ref, gate_factor_ref, wg_ref, wu_ref, out_ref,
+    gate_grad, up_grad, score, back,
+):
     sources = out_ref.shape[0] // PAIR
     capacity = sources * MOST
     width = wg_ref.shape[1]
-    blocks = gate_ref.shape[2] // LANE
+    blocks = up_ref.shape[2] // LANE
     rows, columns = GROUP * MOST, GROUP * PAIR
     tail = capacity - share
     for e, low, count, half, top in (
@@ -144,26 +179,22 @@
         (1, share, tail, 1, capacity),
     ):
         here = slice(0, count)
-        weight[here] = jnp.broadcast_to(
-            rows_ref[e, low : low + count, LANE:].astype(F32)[:, width - LANE : width - LANE + 1], (count, LANE)
-        )
         score[here] = jnp.zeros((count, LANE), F32)
 
         def block(b, carry, e=e, low=low, count=count, half=half, top=top, here=here):
             columns = pl.ds(pl.multiple_of(b * LANE, LANE), LANE)
-            grad = grad_ref[2 * b + half, top : top + count, :].astype(F32)
-            gate = gate_ref[e, low : low + count, columns].astype(F32)
-            up = up_ref[e, low : low + count, columns].astype(F32)
-            sig = lax.logistic(gate)
-            silu = gate * sig
-            score[here] += silu * up * grad
-            scaled = weight[here] * grad
-            up_grad[here, columns] = (scaled * silu).astype(BF16)
-            gate_grad[here, columns] = (scaled * up * sig * (1.0 + gate * (1.0 - sig))).astype(BF16)
+            scale = jnp.exp2(grad_ref[2 * b + half, capacity + share : capacity + share + 1, :])
+            grad = grad_ref[2 * b + half, top : top + count, :] * scale
+            by_up = grad * up_factor_ref[e, low : low + count, columns]
+            score[here] += by_up * up_ref[e, low : low + count, columns].astype(F32)
+            up_grad[here, columns] = by_up.astype(BF16)
+            gate_grad[here, columns] = (grad * gate_factor_ref[e, low : low + count, columns]).astype(BF16)
             return carry
 
         lax.fori_loop(0, blocks, block, 0)
+        weight = rows_ref[e, low : low + count, LANE:].astype(F32)[:, width - LANE : width - LANE + 1]
         total = dot_nt(gate_grad[here], wg_ref[e]) + dot_nt(up_grad[here], wu_ref[e])
+        total = total * weight
         sums = jnp.sum(score[here], axis=1, keepdims=True)
         high = sums.astype(BF16).astype(F32)
         at = lax.broadcasted_iota(jnp.int32, (count, 2 * LANE - width), 1)
@@ -189,25 +220,25 @@
 
 
 def combine_kernel(homes, routes_ref, slots_ref, got_ref, tokens_ref, probs_ref):
-    tokens, width = tokens_ref.shape
+    width, tokens = tokens_ref.shape
     experts = homes * OWN
-    hits, ranks = rank_table(routes_ref[...], experts)
+    hits, ranks = rank_table(routes_ref[...].astype(F32).T.astype(jnp.int32), experts)
     pick = expert_rows(0, homes, experts)
     rank_of = dot_nt(ranks, pick.astype(F32).astype(BF16))
     first = (rank_of == slots_ref[0:1, :]).astype(F32).astype(BF16)
     second = (rank_of == slots_ref[1:2, :]).astype(F32).astype(BF16)
-    tokens_ref[:, 0:LANE] = dot(first, got_ref[...])
-    tokens_ref[:, LANE:width] = dot(second, got_ref[...])[:, : width - LANE]
+    tokens_ref[0:LANE, :] = dot(first, got_ref[...]).T
+    tokens_ref[LANE:width, :] = dot(second, got_ref[...]).T[: width - LANE]
     ends = got_ref[...].astype(F32)
     high = jnp.where(pick, ends[:, width - LANE : width - LANE + 1], 0.0).astype(BF16)
     low = jnp.where(pick, ends[:, width - LANE + 1 : width - LANE + 2], 0.0).astype(BF16)
     table = dot(second, high) + dot(second, low)
-    at = lax.broadcasted_iota(jnp.int32, probs_ref.shape, 1)
-    result = jnp.zeros(probs_ref.shape, F32)
+    at = lax.broadcasted_iota(jnp.int32, (tokens, len(hits)), 1)
+    result = jnp.zeros((tokens, len(hits)), F32)
     for k, hit in enumerate(hits):
         mine = jnp.sum(jnp.where(hit, table, 0.0), axis=1, keepdims=True)
         result = jnp.where(at == k, mine, result)
-    probs_ref[...] = result
+    probs_ref[...] = result.T
 
 
 def cost(flops, nbytes):
@@ -233,12 +264,23 @@
             out_shape=jax.ShapeDtypeStruct((packed, LANE), BF16),
             in_specs=[VMEM] * 3,
             out_specs=VMEM,
-            scratch_shapes=[pltpu.VMEM((3 * tokens, LANE), BF16)],
+            scratch_shapes=[pltpu.VMEM((LANE, 3 * tokens), BF16)],
             compiler_params=PARAMS,
             cost_estimate=cost(10**9, 10**6),
-        )(routes, probs, cotangent)
+        )(routes.T, probs.T, cotangent.T)
+    with jax.named_scope("factors"):
+        factor = jax.ShapeDtypeStruct(gate_pre.shape, F32)
+        up_factor, gate_factor = pl.pallas_call(
+            factor_kernel,
+            out_shape=(factor, factor),
+            in_specs=[VMEM] * 2,
+            out_specs=(VMEM, VMEM),
+            compiler_params=PARAMS,
+            cost_estimate=pl.CostEstimate(flops=2 * 10**7, bytes_accessed=2 * 10**7, transcendentals=10**6),
+        )(gate_pre, up_pre)
     with jax.named_scope("dispatch"):
         got = lax.all_to_all(send.reshape(homes, PAIR, LANE), ("x", "z"), 0, 0, tiled=True).reshape(packed, LANE)
+        got, up_factor, gate_factor = lax.optimization_barrier((got, up_factor, gate_factor))
     with jax.named_scope("down_other"):
         rows, other = pl.pallas_call(
             functools.partial(unpack_kernel, share),
@@ -251,37 +293,41 @@
     with jax.named_scope("swap_cores"):
         swapped = lax.ppermute(other, "core", [(0, 1), (1, 0)])
     with jax.named_scope("down_own"):
-        own = pl.pallas_call(
+        chip = pl.pallas_call(
             functools.partial(down_kernel, share),
             out_shape=half_shape,
-            in_specs=[SMEM, VMEM, VMEM],
+            in_specs=[SMEM, VMEM, VMEM, VMEM],
             out_specs=VMEM,
             compiler_params=PARAMS,
             cost_estimate=cost(10**9, 4 * 10**6),
-        )(here, rows, w_down)
-    with jax.named_scope("add_cores"):
-        chip = (own.astype(F32) + swapped.astype(F32)).astype(BF16)
+        )(here, rows, w_down, swapped)
     with jax.named_scope("sum_over_y"):
         parts = lax.all_to_all(chip, "y", 0, 0, tiled=True)
-        share_sum = jnp.sum(parts.astype(F32), axis=0).astype(BF16)
+        scaled = pl.pallas_call(
+            sum_kernel,
+            out_shape=jax.ShapeDtypeStruct((capacity + share + 16, LANE), F32),
+            in_specs=[VMEM],
+            out_specs=VMEM,
+            compiler_params=PARAMS,
+            cost_estimate=cost(10**6, 3 * 10**6),
+        )(parts)
     with jax.named_scope("gather_hidden"):
-        grad = lax.all_gather(share_sum, ("y", "core"), axis=0)
+        grad = lax.all_gather(scaled.astype(jnp.float16), ("y", "core"), axis=0).astype(F32)
     with jax.named_scope("back"):
         back = pl.pallas_call(
             functools.partial(back_kernel, share),
             out_shape=jax.ShapeDtypeStruct((packed, LANE), BF16),
-            in_specs=[VMEM] * 6,
+            in_specs=[VMEM] * 7,
             out_specs=VMEM,
             scratch_shapes=[
                 pltpu.VMEM((capacity, hidden), BF16),
                 pltpu.VMEM((capacity, hidden), BF16),
                 pltpu.VMEM((capacity, LANE), F32),
-                pltpu.VMEM((capacity, LANE), F32),
                 pltpu.VMEM((homes * MOST * 2 * OWN, LANE), BF16),
             ],
             compiler_params=PARAMS,
             cost_estimate=cost(2 * 10**9, 10**7),
-        )(grad, rows, gate_pre, up_pre, w_gate, w_up)
+        )(grad, rows, up_pre, up_factor, gate_factor, w_gate, w_up)
     with jax.named_scope("way_back"):
         home = lax.all_to_all(back.reshape(homes, PAIR, LANE), ("x", "z"), 0, 0, tiled=True).reshape(packed, LANE)
     row = np.arange(packed) % PAIR
@@ -289,17 +335,18 @@
     slot = np.where(place < OWN * MOST, place % MOST, 99)
     slots = np.stack([np.where(row < SLOTS, slot, 99), np.where(row < SLOTS, 99, slot)]).astype(np.float32)
     with jax.named_scope("combine"):
-        return pl.pallas_call(
+        grad_tokens, grad_probs = pl.pallas_call(
             functools.partial(combine_kernel, homes),
             out_shape=(
-                jax.ShapeDtypeStruct((tokens, width), F32),
-                jax.ShapeDtypeStruct(probs.shape, F32),
+                jax.ShapeDtypeStruct((width, tokens), F32),
+                jax.ShapeDtypeStruct(probs.shape[::-1], F32),
             ),
             in_specs=[VMEM] * 3,
             out_specs=(VMEM, VMEM),
             compiler_params=PARAMS,
             cost_estimate=cost(10**9, 10**6),
-        )(routes, jnp.asarray(slots), home)
+        )(routes.T, jnp.asarray(slots), home)
+        return grad_tokens.T, grad_probs.T
 
 
 def solution(mesh):

time: 217 us -> 182 us (0.84)
  waiting for transfers between devices: 67.6 us -> 24.6 us
  blocking collectives: 86.4 us -> 104 us
  between operations: 14.1 us -> 0.81 us
  local copies, waits for them, and re-layouts: 4 us -> 12.5 us
  Pallas kernels: 21.4 us -> 18.7 us
    all_gather x1 -> x0, waiting for transfers between devices: 35.1 us -> none  [on_device(): grad = lax.all_gather(share_sum, ('y', 'core'), axis=0)]
    all_gather x0 -> x1, blocking collectives: none -> 25.1 us  [on_device(): lax.all_gather(scaled.astype(jnp.float16), ('y', 'core'), axis=0)]
    unnamed x11 -> x36, local copies, waits for them, and re-layouts: 2.59 us -> 12.5 us
    all_to_all x1, waiting for transfers between devices: 30 us -> 21.6 us  [on_device(): lax.all_to_all(send.reshape(homes, PAIR, LANE), ('x', 'z'), 0, 0, tiled=T...]
    all_to_all x1, blocking collectives: 43.9 us -> 36.9 us  [on_device(): lax.all_to_all(back.reshape(homes, PAIR, LANE), ('x', 'z'), 0, 0, tiled=T...]
    pallas_call x1, Pallas kernels: 13.1 us -> 8.14 us  [on_device(): pl.pallas_call(functools.partial(back_kernel, share), out_shape=jax.Shape...]
    reduce_sum x1 -> x0, other arithmetic: 2.33 us -> none  [on_device(): share_sum = jnp.sum(parts.astype(F32), axis=0).astype(BF16)]
    pallas_call x0 -> x2, Pallas kernels: none -> 2.25 us  [the longest x1 1.96 us: on_device(): pl.pallas_call(factor_kernel, out_shape=(factor, factor), in_specs=[VMEM]...]
  transfers between devices with their start and end apart: 3 -> 2, of which waited for: 3 -> 2; matrix products, arithmetic and copies ran while one was open for 0% -> 0% of each run, Pallas kernels for 0% -> 1%
where the time goes in v2:
time: 182 us
  blocking collectives  104 us (57%)
  waiting for transfers between devices  24.6 us (14%)
  starting transfers between devices  20.5 us (11%)
  Pallas kernels  18.7 us (10%)
  local copies, waits for them, and re-layouts  12.5 us (7%)
    all_to_all x1, blocking collectives, on_device(): parts = lax.all_to_all(chip, 'y', 0, 0, tiled=True)  42.2 us
    all_to_all x1, blocking collectives, on_device(): lax.all_to_all(back.reshape(homes, PAIR, LANE), ('x', 'z'), 0, 0, tiled=T...  36.9 us
    all_gather x1, blocking collectives, on_device(): lax.all_gather(scaled.astype(jnp.float16), ('y', 'core'), axis=0)  25.1 us
    all_to_all x1, waiting for transfers between devices, on_device(): lax.all_to_all(send.reshape(homes, PAIR, LANE), ('x', 'z'), 0, 0, tiled=T...  21.6 us
    all_to_all x1, starting transfers between devices, on_device(): lax.all_to_all(send.reshape(homes, PAIR, LANE), ('x', 'z'), 0, 0, tiled=T...  18.5 us
    unnamed x36, local copies, waits for them, and re-layouts  12.5 us
    pallas_call x1, Pallas kernels, on_device(): pl.pallas_call(functools.partial(back_kernel, share), out_shape=jax.Shape...  8.14 us
  transfers between devices with their start and end apart: 2, of which 2 were waited for; matrix products, arithmetic and copies ran while one was open for 0% of the time, Pallas kernels for 1%

profile of v2, /device:TPU:6, one launch (start us, length us, event | category | flops | bytes accessed | tf_op | source)
XLA Modules:
  0.0 181.8 jit_solution(12053512345770785772)
XLA Ops:
  0.6 0.0 copy-start.9
  0.6 0.9 copy-done.9
  1.5 0.0 copy-start.10
  1.5 0.7 copy-done.10
  2.2 0.0 copy-start.11
  2.2 0.7 copy-done.11
  2.9 0.0 copy-start
  2.9 2.1 %send_rows.1 = bf16[2688,128]{1,0:T(8,128)(2,1)S(1)} custom-call(s32[8,128]{1,0:T(8,128)S(1)} %bitcast.22, f32[8,128]{1,0:T(8,128)S(1)} %bitcast.21, f32[224,128]{1,0:T(8,128)S(1)} %bitcast.20), custom_call_target="tpu_custom_call" | custom-call | flops 1000000000 | bytes 1000000 | tf_op jit(solution)/shard_map/send_rows/pallas_call | solution.py:262
  5.0 0.0 copy-start.8
  5.0 0.8 copy-done.8
  5.9 18.5 %all-to-all-start = ((bf16[48,56,128]{2,1,0:T(8,128)(2,1)}), bf16[48,56,128]{2,1,0:T(8,128)(2,1)S(1)}, u32[]{:S(2)}, u32[]{:S(2)}) async-start(bf16[48,56,128]{2,1,0:T(8,128)(2,1)} %bitcast.18), calls=%async_computation | async-start | bytes 1376256 | tf_op jit(solution)/shard_map/dispatch/all_to_all | solution.py:282
  24.5 0.0 copy-done
  24.5 0.0 copy-start.3
  24.5 1.7 copy-done.3
  26.2 2.0 %factors.1 = (f32[3,432,1024]{2,1,0:T(8,128)S(1)}, f32[3,432,1024]{2,1,0:T(8,128)S(1)}) custom-call(bf16[3,432,1024]{2,1,0:T(8,128)(2,1)S(1)} %copy-done.3, bf16[3,432,1024]{2,1,0:T(8,128)(2,1)S(1)} %copy-done), custom_call_target="tpu_custom_call" | custom-call | flops 20000000 | bytes 20000000 | tf_op jit(solution)/shard_map/factors/pallas_call | solution.py:273
  28.2 0.0 copy-start.1
  28.2 2.3 %copy-done.1 = f32[3,432,1024]{2,1,0:T(8,128)} copy-done((f32[3,432,1024]{2,1,0:T(8,128)}, f32[3,432,1024]{2,1,0:T(8,128)S(1)}, u32[]{:S(2)}) %copy-start.1) | copy-done | bytes 5308440
  30.5 0.0 copy-start.2
  30.5 2.4 %copy-done.2 = f32[3,432,1024]{2,1,0:T(8,128)} copy-done((f32[3,432,1024]{2,1,0:T(8,128)}, f32[3,432,1024]{2,1,0:T(8,128)S(1)}, u32[]{:S(2)}) %copy-start.2) | copy-done | bytes 5308440
  32.9 21.6 %all-to-all-done = bf16[48,56,128]{2,1,0:T(8,128)(2,1)S(1)} async-done(((bf16[48,56,128]{2,1,0:T(8,128)(2,1)}), bf16[48,56,128]{2,1,0:T(8,128)(2,1)S(1)}, u32[]{:S(2)}, u32[]{:S(2)}) %all-to-all-start) | async-done | bytes 688160 | tf_op jit(solution)/shard_map/dispatch/all_to_all | solution.py:282
  54.5 0.0 copy-start.4
  54.5 1.3 copy-done.4
  55.8 0.0 copy-start.5
  55.8 0.0 slice-start.2
  55.8 2.4 %down_other.1 = (bf16[3,448,256]{2,1,0:T(8,128)(2,1)S(1)}, bf16[8,656,128]{2,1,0:T(8,128)(2,1)S(1)}) custom-call(s32[1]{0:T(128)} %bitcast.1.half_ref, bf16[2688,128]{1,0:T(8,128)(2,1)S(1)} %bitcast.17, bf16[3,224,1024]{2,1,0:T(8,128)(2,1)S(1)} %copy-done.4), custom_call_target="tpu_custom_call" | custom-call | flops 1000000000 | bytes 4000000 | tf_op jit(solution)/shard_map/down_other/pallas_call | solution.py:285
  58.3 1.9 %collective-permute-start = (bf16[8,656,128]{2,1,0:T(8,128)(2,1)S(1)}, bf16[8,656,128]{2,1,0:T(8,128)(2,1)S(1)}, u32[]{:S(2)}, u32[]{:S(2)}) collective-permute-start(bf16[8,656,128]{2,1,0:T(8,128)(2,1)S(1)} %get-tuple-element.15), channel_id=1, source_target_pairs={{0,48},{48,0},{1,49},{49,1},{2,50},{50,2},{3,51},{51,3},{4,52},{52... | collective-permute-start | bytes 4030472 | tf_op jit(solution)/shard_map/swap_cores/ppermute | solution.py:294
  60.2 3.0 %collective-permute-done.plus_ref = bf16[8,656,128]{2,1,0:T(8,128)(2,1)S(1)} collective-permute-done((bf16[8,656,128]{2,1,0:T(8,128)(2,1)S(1)}, bf16[8,656,128]{2,1,0:T(8,128)(2,1)S(1)}, u32[]{:S(2)}, u32[]{:S(2)}) %collective-permute-start) | collective-permute-done | bytes 1343520 | tf_op jit(solution)/shard_map/swap_cores/ppermute | solution.py:294
  63.2 0.0 copy-done.5
  63.3 0.5 down_own.1
  63.8 42.2 %all_to_all.15.parts_ref = bf16[8,656,128]{2,1,0:T(8,128)(2,1)S(1)} all-to-all(bf16[8,656,128]{2,1,0:T(8,128)(2,1)S(1)} %down_own.1), channel_id=1, replica_groups=mesh['y'=8,'core'=2,'x'=4,'z'=12] {'y'}, dimensions={0} | all-to-all | bytes 2686976 | tf_op jit(solution)/shard_map/sum_over_y/all_to_all | solution.py:305
  106.0 0.0 slice-start.3
  106.0 0.3 sum_over_y.1
  106.4 0.0 slice-start
  106.4 25.1 %all-gather.2 = f16[10752,128]{1,0:T(8,128)(2,1)S(1)} all-gather(f16[672,128]{1,0:T(8,128)(2,1)S(1)} %convert_element_type.6), channel_id=2, replica_groups=mesh['y'=8,'core'=2,'x'=4,'z'=12] {'y','core'}, dimensions={0}, use_global_device_ids=true | all-gather | bytes 2924544 | tf_op jit(solution)/shard_map/gather_hidden/all_gather | solution.py:315
  131.5 0.5 convert.grad_ref
  132.0 0.0 slice-done.2
  132.1 0.0 slice-done.3
  132.1 0.0 slice-done
  132.1 0.7 slice-done.1
  132.7 0.4 copy-done.6
  133.2 0.4 copy-done.7
  133.6 8.1 %back.1 = bf16[2688,128]{1,0:T(8,128)(2,1)S(1)} custom-call(f32[16,672,128]{2,1,0:T(8,128)S(1)} %convert.grad_ref, bf16[3,448,256]{2,1,0:T(8,128)(2,1)S(1)} %get-tuple-element.14.rows_ref, bf16[3,432,1024]{2,1,0:T(8,128)(2,1)S(1)} %copy-done, f32[3,432,1024]{2,1,0:T(8,128)S(1)} %bitcast.13, f32[3,432,1024]{2,1,0:T(8,128)S(1)} %bitcast.15, ...), custom_call_target="tpu_custom_call" | custom-call | flops 2000000000 | bytes 10000000 | tf_op jit(solution)/shard_map/back/pallas_call | solution.py:317
  141.7 0.0 copy-start.12
  141.7 0.0 copy-start.13
  141.7 36.9 %all_to_all.16 = bf16[48,56,128]{2,1,0:T(8,128)(2,1)S(1)} all-to-all(bf16[48,56,128]{2,1,0:T(8,128)(2,1)S(1)} %bitcast.16), channel_id=1, replica_groups=mesh['y'=8,'core'=2,'x'=4,'z'=12] {'x','z'}, dimensions={0} | all-to-all | bytes 1376256 | tf_op jit(solution)/shard_map/way_back/all_to_all | solution.py:332
  178.6 0.0 copy-done.12
  178.6 0.0 copy-done.13
  178.6 3.2 %combine.1 = (f32[224,128]{1,0:T(8,128)}, f32[8,128]{1,0:T(8,128)}) custom-call(s32[8,128]{1,0:T(8,128)S(1)} %bitcast.23, f32[2,2688]{1,0:T(2,128)S(1)} %copy-done.13, bf16[2688,128]{1,0:T(8,128)(2,1)S(1)} %bitcast.19), custom_call_target="tpu_custom_call" | custom-call | flops 1000000000 | bytes 1000000 | tf_op jit(solution)/shard_map/combine/pallas_call | solution.py:338
  (6 shorter events, 0.0 us)
Async XLA Ops:
  0.6 0.9 copy-start.9
  1.5 0.7 copy-start.10
  2.2 0.7 copy-start.11
  2.9 21.6 %copy-start = (bf16[3,432,1024]{2,1,0:T(8,128)(2,1)S(1)}, bf16[3,432,1024]{2,1,0:T(8,128)(2,1)}, u32[]{:S(2)}) copy-start(bf16[3,432,1024]{2,1,0:T(8,128)(2,1)} %up_ref.3) | copy-start | bytes 7962628
  5.0 0.9 copy-start.8
  5.9 48.6 %all-to-all-start = ((bf16[48,56,128]{2,1,0:T(8,128)(2,1)}), bf16[48,56,128]{2,1,0:T(8,128)(2,1)S(1)}, u32[]{:S(2)}, u32[]{:S(2)}) async-start(bf16[48,56,128]{2,1,0:T(8,128)(2,1)} %bitcast.18), calls=%async_computation | async-start | bytes 1376256 | tf_op jit(solution)/shard_map/dispatch/all_to_all | solution.py:282
  24.5 1.8 copy-start.3
  28.2 2.3 %copy-start.1 = (f32[3,432,1024]{2,1,0:T(8,128)}, f32[3,432,1024]{2,1,0:T(8,128)S(1)}, u32[]{:S(2)}) copy-start(f32[3,432,1024]{2,1,0:T(8,128)S(1)} %get-tuple-element.16.up_factor_ref) | copy-start | bytes 15925252
  30.5 2.4 %copy-start.2 = (f32[3,432,1024]{2,1,0:T(8,128)}, f32[3,432,1024]{2,1,0:T(8,128)S(1)}, u32[]{:S(2)}) copy-start(f32[3,432,1024]{2,1,0:T(8,128)S(1)} %get-tuple-element.17.gate_factor_ref) | copy-start | bytes 15925252
  54.5 1.3 copy-start.4
  55.8 7.4 %copy-start.5 = (bf16[3,224,1024]{2,1,0:T(8,128)(2,1)S(1)}, bf16[3,224,1024]{2,1,0:T(8,128)(2,1)}, u32[]{:S(2)}) copy-start(bf16[3,224,1024]{2,1,0:T(8,128)(2,1)} %w_ref.3) | copy-start | bytes 4128772
  55.8 76.2 %slice-start.2 = ((s8[5308416]{0:T(1024)(128)(4,1)}), s8[1114112]{0:T(1024)(128)(4,1)S(1)}, s32[]{:S(2)}) async-start(s8[5308416]{0:T(1024)(128)(4,1)} %bitcast.14), calls=%async_computation.5 | async-start | bytes 2228224
  58.3 5.0 %collective-permute-start = (bf16[8,656,128]{2,1,0:T(8,128)(2,1)S(1)}, bf16[8,656,128]{2,1,0:T(8,128)(2,1)S(1)}, u32[]{:S(2)}, u32[]{:S(2)}) collective-permute-start(bf16[8,656,128]{2,1,0:T(8,128)(2,1)S(1)} %get-tuple-element.15), channel_id=1, source_target_pairs={{0,48},{48,0},{1,49},{49,1},{2,50},{50,2},{3,51},{51,3},{4,52},{52... | collective-permute-start | bytes 4030472 | tf_op jit(solution)/shard_map/swap_cores/ppermute | solution.py:294
  106.0 26.0 %slice-start.3 = ((s8[5308416]{0:T(1024)(128)(4,1)}), s8[4194304]{0:T(1024)(128)(4,1)S(1)}, s32[]{:S(2)}) async-start(s8[5308416]{0:T(1024)(128)(4,1)} %bitcast.14), calls=%async_computation.6 | async-start | bytes 8388608
  106.4 25.7 %slice-start = ((s8[5308416]{0:T(1024)(128)(4,1)}), s8[4194304]{0:T(1024)(128)(4,1)S(1)}, s32[]{:S(2)}) async-start(s8[5308416]{0:T(1024)(128)(4,1)} %bitcast.12), calls=%async_computation.3 | async-start | bytes 8388608
  131.5 1.2 slice-start.1
  131.5 1.7 copy-start.6
  131.5 2.1 %copy-start.7 = (bf16[3,224,1024]{2,1,0:T(8,128)(2,1)S(1)}, bf16[3,224,1024]{2,1,0:T(8,128)(2,1)}, u32[]{:S(2)}) copy-start(bf16[3,224,1024]{2,1,0:T(8,128)(2,1)} %wu_ref.1) | copy-start | bytes 4128772
  141.7 36.9 %copy-start.12 = (s32[128,8]{0,1:T(8,128)S(1)}, s32[128,8]{0,1:T(8,128)}, u32[]{:S(2)}) copy-start(s32[128,8]{0,1:T(8,128)} %param.11) | copy-start | bytes 12292
  141.7 36.9 %copy-start.13 = (f32[2,2688]{1,0:T(2,128)S(1)}, f32[2,2688]{1,0:T(2,128)}, u32[]{:S(2)}) copy-start(f32[2,2688]{1,0:T(2,128)} %constant.7.clone.slots_ref) | copy-start | bytes 64516

commit v3 on v2

--- a/solution.py
+++ b/solution.py
@@ -19,7 +19,7 @@
 NT = (((1,), (1,)), ((), ()))
 VMEM = pl.BlockSpec(memory_space=pltpu.VMEM)
 SMEM = pl.BlockSpec(memory_space=pltpu.SMEM)
-PARAMS = pltpu.CompilerParams(vmem_limit_bytes=32 * 1024 * 1024)
+PARAMS = pltpu.CompilerParams(vmem_limit_bytes=24 * 1024 * 1024)
 
 
 def dot(a, b):
@@ -108,19 +108,13 @@
                 out_ref[m, top : top + count, :] = piece.astype(BF16)
 
 
-def unpack_kernel(share, half_ref, got_ref, w_ref, rows_ref, out_ref):
+def unpack_kernel(share, half_ref, got_ref, select_ref, w_ref, rows_ref, out_ref):
     sources = got_ref.shape[0] // PAIR
     capacity = sources * MOST
     rows, columns = GROUP * MOST, GROUP * PAIR
-    at = lax.broadcasted_iota(jnp.int32, (1, columns), 1)
-    source = jnp.floor((at.astype(F32) + 0.5) * (1.0 / PAIR)).astype(jnp.int32)
-    second, expert, slot = decode(at - PAIR * source)
-    goal = jnp.where(slot < MOST, (2 * expert + second) * rows + source * MOST + slot, -1)
-    select = lax.broadcasted_iota(jnp.int32, (2 * OWN * rows, columns), 0) == goal
-    select = select.astype(F32).astype(BF16)
     rows_ref[:, capacity:, :] = jnp.zeros((OWN, rows_ref.shape[1] - capacity, 2 * LANE), BF16)
     for g in range(sources // GROUP):
-        piece = dot(select, got_ref[g * columns : (g + 1) * columns, :]).astype(BF16)
+        piece = dot(select_ref[...], got_ref[g * columns : (g + 1) * columns, :]).astype(BF16)
         for e in range(OWN):
             for second in range(2):
                 top = (2 * e + second) * rows
@@ -132,10 +126,14 @@
     down_half(half_ref[0], share, rows_ref, w_ref, out_ref, plus_ref)
 
 
-def factor_kernel(gate_ref, up_ref, up_factor_ref, gate_factor_ref):
-    experts, capacity, hidden = gate_ref.shape
+def prepare_kernel(
+    homes, routes_ref, slots_ref, gate_ref, up_ref,
+    up_factor_ref, gate_factor_ref, select_in_ref, select_out_ref, first_ref, second_ref, pick_ref,
+):
+    capacity, hidden = gate_ref.shape[1:]
+    experts = homes * OWN
     step = 48
-    for e in range(experts):
+    for e in range(OWN):
 
         def part(i, carry, e=e):
             rows = pl.ds(pl.multiple_of(i * step, step), step)
@@ -148,6 +146,23 @@
             return carry
 
         lax.fori_loop(0, capacity // step, part, 0)
+    rows, columns = GROUP * MOST, GROUP * PAIR
+    at = lax.broadcasted_iota(jnp.int32, (1, columns), 1)
+    source = jnp.floor((at.astype(F32) + 0.5) * (1.0 / PAIR)).astype(jnp.int32)
+    second, expert, slot = decode(at - PAIR * source)
+    goal = jnp.where(slot < MOST, (2 * expert + second) * rows + source * MOST + slot, -1)
+    select = lax.broadcasted_iota(jnp.int32, (2 * OWN * rows, columns), 0) == goal
+    select_in_ref[...] = select.astype(F32).astype(BF16)
+    shape = (GROUP, PAIR, 2 * OWN * rows)
+    second, expert, slot = decode(lax.broadcasted_iota(jnp.int32, shape, 1))
+    goal = (2 * expert + second) * rows + lax.broadcasted_iota(jnp.int32, shape, 0) * MOST + slot
+    select = (lax.broadcasted_iota(jnp.int32, shape, 2) == goal) & (slot < MOST)
+    select_out_ref[...] = select.reshape(columns, 2 * OWN * rows).astype(F32).astype(BF16)
+    _, ranks = rank_table(routes_ref[...].astype(F32).T.astype(jnp.int32), experts)
+    pick_ref[...] = expert_rows(0, homes, experts).astype(F32).astype(BF16)
+    rank_of = dot_nt(ranks, pick_ref[...])
+    first_ref[...] = (rank_of == slots_ref[0:1, :]).astype(F32).astype(BF16)
+    second_ref[...] = (rank_of == slots_ref[1:2, :]).astype(F32).astype(BF16)
 
 
 def sum_kernel(parts_ref, out_ref):
@@ -163,7 +178,7 @@
 
 
 def back_kernel(
-    share, grad_ref, rows_ref, up_ref, up_factor_ref, gate_factor_ref, wg_ref, wu_ref, out_ref,
+    share, grad_ref, rows_ref, up_ref, up_factor_ref, gate_factor_ref, wg_ref, wu_ref, select_ref, out_ref,
     gate_grad, up_grad, score, back,
 ):
     sources = out_ref.shape[0] // PAIR
@@ -209,34 +224,28 @@
             back[first + rows : first + rows + n, 0 : width - LANE] = total[done : done + n, LANE:width]
             back[first + rows : first + rows + n, width - LANE :] = ends[done : done + n]
             done += n
-    shape = (GROUP, PAIR, 2 * OWN * rows)
-    second, expert, slot = decode(lax.broadcasted_iota(jnp.int32, shape, 1))
-    goal = (2 * expert + second) * rows + lax.broadcasted_iota(jnp.int32, shape, 0) * MOST + slot
-    select = (lax.broadcasted_iota(jnp.int32, shape, 2) == goal) & (slot < MOST)
-    select = select.reshape(columns, 2 * OWN * rows).astype(F32).astype(BF16)
     for g in range(sources // GROUP):
-        piece = dot(select, back[g * 2 * OWN * rows : (g + 1) * 2 * OWN * rows, :])
+        piece = dot(select_ref[...], back[g * 2 * OWN * rows : (g + 1) * 2 * OWN * rows, :])
         out_ref[g * columns : (g + 1) * columns, :] = piece.astype(BF16)
 
 
-def combine_kernel(homes, routes_ref, slots_ref, got_ref, tokens_ref, probs_ref):
+def combine_kernel(routes_ref, first_ref, second_ref, pick_ref, got_ref, tokens_ref, probs_ref):
     width, tokens = tokens_ref.shape
-    experts = homes * OWN
-    hits, ranks = rank_table(routes_ref[...].astype(F32).T.astype(jnp.int32), experts)
-    pick = expert_rows(0, homes, experts)
-    rank_of = dot_nt(ranks, pick.astype(F32).astype(BF16))
-    first = (rank_of == slots_ref[0:1, :]).astype(F32).astype(BF16)
-    second = (rank_of == slots_ref[1:2, :]).astype(F32).astype(BF16)
-    tokens_ref[0:LANE, :] = dot(first, got_ref[...]).T
-    tokens_ref[LANE:width, :] = dot(second, got_ref[...]).T[: width - LANE]
-    ends = got_ref[...].astype(F32)
-    high = jnp.where(pick, ends[:, width - LANE : width - LANE + 1], 0.0).astype(BF16)
-    low = jnp.where(pick, ends[:, width - LANE + 1 : width - LANE + 2], 0.0).astype(BF16)
-    table = dot(second, high) + dot(second, low)
-    at = lax.broadcasted_iota(jnp.int32, (tokens, len(hits)), 1)
-    result = jnp.zeros((tokens, len(hits)), F32)
-    for k, hit in enumerate(hits):
-        mine = jnp.sum(jnp.where(hit, table, 0.0), axis=1, keepdims=True)
+    experts = pick_ref.shape[1]
+    tokens_ref[0:LANE, :] = dot(first_ref[...], got_ref[...]).T
+    tokens_ref[LANE:width, :] = dot(second_ref[...], got_ref[...]).T[: width - LANE]
+    at = lax.broadcasted_iota(jnp.int32, (16, LANE), 1) - lax.broadcasted_iota(jnp.int32, (16, LANE), 0)
+    ends = dot_nt((at == width - LANE).astype(F32).astype(BF16), got_ref[...])
+    second = second_ref[...].astype(F32)
+    table = dot((second * ends[0:1, :]).astype(BF16), pick_ref[...])
+    table = table + dot((second * ends[1:2, :]).astype(BF16), pick_ref[...])
+    routes = routes_ref[...].astype(F32).T.astype(jnp.int32)
+    top = routes.shape[1]
+    lane = lax.broadcasted_iota(jnp.int32, (tokens, experts), 1)
+    at = lax.broadcasted_iota(jnp.int32, (tokens, top), 1)
+    result = jnp.zeros((tokens, top), F32)
+    for k in range(top):
+        mine = jnp.sum(jnp.where(routes[:, k : k + 1] == lane, table, 0.0), axis=1, keepdims=True)
         result = jnp.where(at == k, mine, result)
     probs_ref[...] = result.T
 
@@ -268,28 +277,42 @@
             compiler_params=PARAMS,
             cost_estimate=cost(10**9, 10**6),
         )(routes.T, probs.T, cotangent.T)
-    with jax.named_scope("factors"):
+    row = np.arange(packed) % PAIR
+    place = row % SLOTS
+    slot = np.where(place < OWN * MOST, place % MOST, 99)
+    slots = np.stack([np.where(row < SLOTS, slot, 99), np.where(row < SLOTS, 99, slot)]).astype(np.float32)
+    with jax.named_scope("prepare"):
         factor = jax.ShapeDtypeStruct(gate_pre.shape, F32)
-        up_factor, gate_factor = pl.pallas_call(
-            factor_kernel,
-            out_shape=(factor, factor),
-            in_specs=[VMEM] * 2,
-            out_specs=(VMEM, VMEM),
+        there, column = 2 * OWN * GROUP * MOST, GROUP * PAIR
+        mask = jax.ShapeDtypeStruct((tokens, packed), BF16)
+        ready = pl.pallas_call(
+            functools.partial(prepare_kernel, homes),
+            out_shape=(
+                factor,
+                factor,
+                jax.ShapeDtypeStruct((there, column), BF16),
+                jax.ShapeDtypeStruct((column, there), BF16),
+                mask,
+                mask,
+                jax.ShapeDtypeStruct((packed, homes * OWN), BF16),
+            ),
+            in_specs=[VMEM] * 4,
+            out_specs=(VMEM,) * 7,
             compiler_params=PARAMS,
             cost_estimate=pl.CostEstimate(flops=2 * 10**7, bytes_accessed=2 * 10**7, transcendentals=10**6),
-        )(gate_pre, up_pre)
+        )(routes.T, jnp.asarray(slots), gate_pre, up_pre)
     with jax.named_scope("dispatch"):
         got = lax.all_to_all(send.reshape(homes, PAIR, LANE), ("x", "z"), 0, 0, tiled=True).reshape(packed, LANE)
-        got, up_factor, gate_factor = lax.optimization_barrier((got, up_factor, gate_factor))
+    up_factor, gate_factor, select_in, select_out, first, second, pick = ready
     with jax.named_scope("down_other"):
         rows, other = pl.pallas_call(
             functools.partial(unpack_kernel, share),
             out_shape=(rows_shape, half_shape),
-            in_specs=[SMEM, VMEM, VMEM],
+            in_specs=[SMEM, VMEM, VMEM, VMEM],
             out_specs=(VMEM, VMEM),
             compiler_params=PARAMS,
             cost_estimate=cost(10**9, 4 * 10**6),
-        )(here, got, w_down)
+        )(here, got, select_in, w_down)
     with jax.named_scope("swap_cores"):
         swapped = lax.ppermute(other, "core", [(0, 1), (1, 0)])
     with jax.named_scope("down_own"):
@@ -317,7 +340,7 @@
         back = pl.pallas_call(
             functools.partial(back_kernel, share),
             out_shape=jax.ShapeDtypeStruct((packed, LANE), BF16),
-            in_specs=[VMEM] * 7,
+            in_specs=[VMEM] * 8,
             out_specs=VMEM,
             scratch_shapes=[
                 pltpu.VMEM((capacity, hidden), BF16),
@@ -327,25 +350,21 @@
             ],
             compiler_params=PARAMS,
             cost_estimate=cost(2 * 10**9, 10**7),
-        )(grad, rows, up_pre, up_factor, gate_factor, w_gate, w_up)
+        )(grad, rows, up_pre, up_factor, gate_factor, w_gate, w_up, select_out)
     with jax.named_scope("way_back"):
         home = lax.all_to_all(back.reshape(homes, PAIR, LANE), ("x", "z"), 0, 0, tiled=True).reshape(packed, LANE)
-    row = np.arange(packed) % PAIR
-    place = row % SLOTS
-    slot = np.where(place < OWN * MOST, place % MOST, 99)
-    slots = np.stack([np.where(row < SLOTS, slot, 99), np.where(row < SLOTS, 99, slot)]).astype(np.float32)
     with jax.named_scope("combine"):
         grad_tokens, grad_probs = pl.pallas_call(
-            functools.partial(combine_kernel, homes),
+            combine_kernel,
             out_shape=(
                 jax.ShapeDtypeStruct((width, tokens), F32),
                 jax.ShapeDtypeStruct(probs.shape[::-1], F32),
             ),
-            in_specs=[VMEM] * 3,
+            in_specs=[VMEM] * 5,
             out_specs=(VMEM, VMEM),
             compiler_params=PARAMS,
             cost_estimate=cost(10**9, 10**6),
-        )(routes.T, jnp.asarray(slots), home)
+        )(routes.T, first, second, pick, home)
         return grad_tokens.T, grad_probs.T
 
 

time: 182 us -> 184 us (1.011)
  waiting for transfers between devices: 24.6 us -> 17.2 us
  local copies, waits for them, and re-layouts: 12.5 us -> 19.4 us
    all_to_all x1, waiting for transfers between devices: 21.6 us -> 14.2 us  [on_device(): lax.all_to_all(send.reshape(homes, PAIR, LANE), ('x', 'z'), 0, 0, tiled=T...]
    unnamed x36 -> x54, local copies, waits for them, and re-layouts: 12.5 us -> 19.4 us
  transfers between devices with their start and end apart: 2 -> 2, of which waited for: 2 -> 2; matrix products, arithmetic and copies ran while one was open for 0% -> 0% of each run, Pallas kernels for 1% -> 2%
where the time goes in v3:
time: 184 us; the launch traced here: 183 us
  blocking collectives  104 us (57%)
  starting transfers between devices  20.5 us (11%)
  Pallas kernels  20.3 us (11%)
  local copies, waits for them, and re-layouts  19.4 us (11%)
  waiting for transfers between devices  17.2 us (9%)
    all_to_all x1, blocking collectives, on_device(): parts = lax.all_to_all(chip, 'y', 0, 0, tiled=True)  42.2 us
    all_to_all x1, blocking collectives, on_device(): lax.all_to_all(back.reshape(homes, PAIR, LANE), ('x', 'z'), 0, 0, tiled=T...  36.9 us
    all_gather x1, blocking collectives, on_device(): lax.all_gather(scaled.astype(jnp.float16), ('y', 'core'), axis=0)  25.3 us
    unnamed x54, local copies, waits for them, and re-layouts  19.4 us
    all_to_all x1, starting transfers between devices, on_device(): lax.all_to_all(send.reshape(homes, PAIR, LANE), ('x', 'z'), 0, 0, tiled=T...  18.6 us
    all_to_all x1, waiting for transfers between devices, on_device(): lax.all_to_all(send.reshape(homes, PAIR, LANE), ('x', 'z'), 0, 0, tiled=T...  14.2 us
    pallas_call x1, Pallas kernels, on_device(): pl.pallas_call(functools.partial(back_kernel, share), out_shape=jax.Shape...  8.13 us
    pallas_call x1, Pallas kernels, on_device(): pl.pallas_call(functools.partial(prepare_kernel, homes), out_shape=(facto...  4.29 us
  transfers between devices with their start and end apart: 2, of which 2 were waited for; matrix products, arithmetic and copies ran while one was open for 0% of the time, Pallas kernels for 2%

profile of v3, /device:TPU:6, one launch (start us, length us, event | category | flops | bytes accessed | tf_op | source)
XLA Modules:
  0.0 183.2 jit_solution(1987349984931349207)
XLA Ops:
  0.6 0.0 copy-start.11
  0.6 0.7 copy-done.11
  1.3 0.0 copy-start.21
  1.3 0.9 copy-done.21
  2.2 0.7 copy-done.22
  2.9 2.1 %send_rows.1 = bf16[2688,128]{1,0:T(8,128)(2,1)S(1)} custom-call(s32[8,128]{1,0:T(8,128)S(1)} %bitcast.20, f32[8,128]{1,0:T(8,128)S(1)} %bitcast.24, f32[224,128]{1,0:T(8,128)S(1)} %bitcast.23), custom_call_target="tpu_custom_call" | custom-call | flops 1000000000 | bytes 1000000 | tf_op jit(solution)/shard_map/send_rows/pallas_call | solution.py:271
  5.0 0.0 copy-start.9
  5.0 0.9 copy-done.9
  5.9 18.6 %all-to-all-start = ((bf16[48,56,128]{2,1,0:T(8,128)(2,1)}), bf16[48,56,128]{2,1,0:T(8,128)(2,1)S(1)}, u32[]{:S(2)}, u32[]{:S(2)}) async-start(bf16[48,56,128]{2,1,0:T(8,128)(2,1)} %bitcast.18), calls=%async_computation | async-start | bytes 1376256 | tf_op jit(solution)/shard_map/dispatch/all_to_all | solution.py:305
  24.5 0.0 copy-done
  24.5 0.0 copy-done.10
  24.5 0.0 copy-done.12
  24.5 0.0 copy-start.3
  24.5 1.7 copy-done.3
  26.2 4.3 %prepare.1 = (f32[3,432,1024]{2,1,0:T(8,128)S(1)}, f32[3,432,1024]{2,1,0:T(8,128)S(1)}, bf16[864,896]{1,0:T(8,128)(2,1)S(1)}, bf16[896,864]{1,0:T(8,128)(2,1)S(1...) custom-call(s32[8,128]{1,0:T(8,128)S(1)} %bitcast.21, ...), custom_call_target="tpu_custom_call" | custom-call | flops 20000000 | bytes 20000000 | tf_op jit(solution)/shard_map/prepare/pallas_call | solution.py:288
  30.5 0.0 copy-start.1
  30.6 2.3 %copy-done.1 = f32[3,432,1024]{2,1,0:T(8,128)} copy-done((f32[3,432,1024]{2,1,0:T(8,128)}, f32[3,432,1024]{2,1,0:T(8,128)S(1)}, u32[]{:S(2)}) %copy-start.1) | copy-done | bytes 5308440
  32.9 2.3 %copy-done.2 = f32[3,432,1024]{2,1,0:T(8,128)} copy-done((f32[3,432,1024]{2,1,0:T(8,128)}, f32[3,432,1024]{2,1,0:T(8,128)S(1)}, u32[]{:S(2)}) %copy-start.2) | copy-done | bytes 5308440
  35.2 1.2 copy-done.4
  36.4 1.1 copy-done.13
  37.5 1.1 copy-done.15
  38.6 0.8 copy-done.17
  39.5 0.8 copy-done.19
  40.3 14.2 %all-to-all-done = bf16[48,56,128]{2,1,0:T(8,128)(2,1)S(1)} async-done(((bf16[48,56,128]{2,1,0:T(8,128)(2,1)}), bf16[48,56,128]{2,1,0:T(8,128)(2,1)S(1)}, u32[]{:S(2)}, u32[]{:S(2)}) %all-to-all-start) | async-done | bytes 688160 | tf_op jit(solution)/shard_map/dispatch/all_to_all | solution.py:305
  54.5 1.3 copy-done.6
  55.9 1.4 copy-done.14
  57.3 2.4 %down_other.1 = (bf16[3,448,256]{2,1,0:T(8,128)(2,1)S(1)}, bf16[8,656,128]{2,1,0:T(8,128)(2,1)S(1)}) custom-call(s32[1]{0:T(128)} %bitcast.1.half_ref, bf16[2688,128]{1,0:T(8,128)(2,1)S(1)} %bitcast.17, bf16[864,896]{1,0:T(8,128)(2,1)S(1)} %copy-done.14, bf16[3,224,1024]{2,1,0:T(8,128)(2,1)S(1)} %copy-done.6), custom_call_target="tpu_custom_call" | custom-call | flops 1000000000 | bytes 4000000 | tf_op jit(solution)/shard_map/down_other/pallas_call | solution.py:308
  59.7 1.9 %collective-permute-start = (bf16[8,656,128]{2,1,0:T(8,128)(2,1)S(1)}, bf16[8,656,128]{2,1,0:T(8,128)(2,1)S(1)}, u32[]{:S(2)}, u32[]{:S(2)}) collective-permute-start(bf16[8,656,128]{2,1,0:T(8,128)(2,1)S(1)} %get-tuple-element.18), channel_id=1, source_target_pairs={{0,48},{48,0},{1,49},{49,1},{2,50},{50,2},{3,51},{51,3},{4,52},{52... | collective-permute-start | bytes 4030472 | tf_op jit(solution)/shard_map/swap_cores/ppermute | solution.py:317
  61.6 3.0 %collective-permute-done.plus_ref = bf16[8,656,128]{2,1,0:T(8,128)(2,1)S(1)} collective-permute-done((bf16[8,656,128]{2,1,0:T(8,128)(2,1)S(1)}, bf16[8,656,128]{2,1,0:T(8,128)(2,1)S(1)}, u32[]{:S(2)}, u32[]{:S(2)}) %collective-permute-start) | collective-permute-done | bytes 1343520 | tf_op jit(solution)/shard_map/swap_cores/ppermute | solution.py:317
  64.6 0.5 down_own.1
  65.2 42.2 %all_to_all.15.parts_ref = bf16[8,656,128]{2,1,0:T(8,128)(2,1)S(1)} all-to-all(bf16[8,656,128]{2,1,0:T(8,128)(2,1)S(1)} %down_own.1), channel_id=1, replica_groups=mesh['y'=8,'core'=2,'x'=4,'z'=12] {'y'}, dimensions={0} | all-to-all | bytes 2686976 | tf_op jit(solution)/shard_map/sum_over_y/all_to_all | solution.py:328
  107.4 0.3 sum_over_y.1
  107.7 0.0 slice-start
  107.8 25.3 %all-gather.2 = f16[10752,128]{1,0:T(8,128)(2,1)S(1)} all-gather(f16[672,128]{1,0:T(8,128)(2,1)S(1)} %convert_element_type.6), channel_id=2, replica_groups=mesh['y'=8,'core'=2,'x'=4,'z'=12] {'y','core'}, dimensions={0}, use_global_device_ids=true | all-gather | bytes 2924544 | tf_op jit(solution)/shard_map/gather_hidden/all_gather | solution.py:338
  133.0 0.5 convert.grad_ref
  133.6 0.0 slice-done.2
  133.6 0.0 slice-done.3
  133.6 0.0 slice-done
  133.6 0.7 slice-done.1
  134.3 0.5 copy-done.5
  134.8 0.4 copy-done.7
  135.2 0.4 copy-done.8
  135.6 8.1 %back.1 = bf16[2688,128]{1,0:T(8,128)(2,1)S(1)} custom-call(f32[16,672,128]{2,1,0:T(8,128)S(1)} %convert.grad_ref, bf16[3,448,256]{2,1,0:T(8,128)(2,1)S(1)} %get-tuple-element.17.rows_ref, bf16[3,432,1024]{2,1,0:T(8,128)(2,1)S(1)} %copy-done, f32[3,432,1024]{2,1,0:T(8,128)S(1)} %bitcast.13, f32[3,432,1024]{2,1,0:T(8,128)S(1)} %bitcast.15, ...), custom_call_target="tpu_custom_call" | custom-call | flops 2000000000 | bytes 10000000 | tf_op jit(solution)/shard_map/back/pallas_call | solution.py:340
  143.7 36.9 %all_to_all.16 = bf16[48,56,128]{2,1,0:T(8,128)(2,1)S(1)} all-to-all(bf16[48,56,128]{2,1,0:T(8,128)(2,1)S(1)} %bitcast.16), channel_id=1, replica_groups=mesh['y'=8,'core'=2,'x'=4,'z'=12] {'x','z'}, dimensions={0} | all-to-all | bytes 1376256 | tf_op jit(solution)/shard_map/way_back/all_to_all | solution.py:355
  180.6 0.0 copy-done.16
  180.6 0.0 copy-done.18
  180.6 0.0 copy-done.20
  180.6 2.6 %combine.1 = (f32[224,128]{1,0:T(8,128)}, f32[8,128]{1,0:T(8,128)}) custom-call(s32[8,128]{1,0:T(8,128)S(1)} %bitcast.22, bf16[128,2688]{1,0:T(8,128)(2,1)S(1)} %copy-done.18, bf16[128,2688]{1,0:T(8,128)(2,1)S(1)} %copy-done.20, bf16[2688,144]{1,0:T(8,128)(2,1)S(1)} %copy-done.16, bf16[2688,128]{1,0:T(8,128)(2,1)S(1)} %bitcast.19), custom_call_target="tpu_custom_call" | custom-call | flops 1000000000 | bytes 1000000 | tf_op jit(solution)/shard_map/combine/pallas_call | solution.py:357
  (24 shorter events, 0.1 us)
Async XLA Ops:
  0.6 0.7 copy-start.11
  1.3 0.9 copy-start.21
  2.2 0.7 copy-start.22
  2.9 21.6 %copy-start = (bf16[3,432,1024]{2,1,0:T(8,128)(2,1)S(1)}, bf16[3,432,1024]{2,1,0:T(8,128)(2,1)}, u32[]{:S(2)}) copy-start(bf16[3,432,1024]{2,1,0:T(8,128)(2,1)} %up_ref.3) | copy-start | bytes 7962628
  2.9 21.6 %copy-start.10 = (f32[2,2688]{1,0:T(2,128)S(1)}, f32[2,2688]{1,0:T(2,128)}, u32[]{:S(2)}) copy-start(f32[2,2688]{1,0:T(2,128)} %constant.7.clone.slots_ref) | copy-start | bytes 64516
  2.9 21.6 %copy-start.12 = (s32[128,8]{0,1:T(8,128)S(1)}, s32[128,8]{0,1:T(8,128)}, u32[]{:S(2)}) copy-start(s32[128,8]{0,1:T(8,128)} %param.11) | copy-start | bytes 12292
  5.0 0.9 copy-start.9
  5.9 48.6 %all-to-all-start = ((bf16[48,56,128]{2,1,0:T(8,128)(2,1)}), bf16[48,56,128]{2,1,0:T(8,128)(2,1)S(1)}, u32[]{:S(2)}, u32[]{:S(2)}) async-start(bf16[48,56,128]{2,1,0:T(8,128)(2,1)} %bitcast.18), calls=%async_computation | async-start | bytes 1376256 | tf_op jit(solution)/shard_map/dispatch/all_to_all | solution.py:305
  24.5 1.8 copy-start.3
  30.5 2.3 %copy-start.1 = (f32[3,432,1024]{2,1,0:T(8,128)}, f32[3,432,1024]{2,1,0:T(8,128)S(1)}, u32[]{:S(2)}) copy-start(f32[3,432,1024]{2,1,0:T(8,128)S(1)} %get-tuple-element.19.up_factor_ref) | copy-start | bytes 15925252
  32.9 2.3 %copy-start.2 = (f32[3,432,1024]{2,1,0:T(8,128)}, f32[3,432,1024]{2,1,0:T(8,128)S(1)}, u32[]{:S(2)}) copy-start(f32[3,432,1024]{2,1,0:T(8,128)S(1)} %get-tuple-element.20.gate_factor_ref) | copy-start | bytes 15925252
  35.2 1.2 copy-start.4
  36.4 1.1 copy-start.13
  37.5 1.1 copy-start.15
  38.6 0.8 copy-start.17
  39.5 0.8 copy-start.19
  54.5 1.3 copy-start.6
  55.9 1.4 copy-start.14
  57.3 76.3 %slice-start.2 = ((s8[5308416]{0:T(1024)(128)(4,1)}), s8[4194304]{0:T(1024)(128)(4,1)S(1)}, s32[]{:S(2)}) async-start(s8[5308416]{0:T(1024)(128)(4,1)} %bitcast.14), calls=%async_computation.5 | async-start | bytes 8388608
  59.7 5.0 %collective-permute-start = (bf16[8,656,128]{2,1,0:T(8,128)(2,1)S(1)}, bf16[8,656,128]{2,1,0:T(8,128)(2,1)S(1)}, u32[]{:S(2)}, u32[]{:S(2)}) collective-permute-start(bf16[8,656,128]{2,1,0:T(8,128)(2,1)S(1)} %get-tuple-element.18), channel_id=1, source_target_pairs={{0,48},{48,0},{1,49},{49,1},{2,50},{50,2},{3,51},{51,3},{4,52},{52... | collective-permute-start | bytes 4030472 | tf_op jit(solution)/shard_map/swap_cores/ppermute | solution.py:317
  107.4 26.2 %slice-start.3 = ((s8[5308416]{0:T(1024)(128)(4,1)}), s8[1114112]{0:T(1024)(128)(4,1)S(1)}, s32[]{:S(2)}) async-start(s8[5308416]{0:T(1024)(128)(4,1)} %bitcast.14), calls=%async_computation.6 | async-start | bytes 2228224
  107.7 25.9 %slice-start = ((s8[5308416]{0:T(1024)(128)(4,1)}), s8[4194304]{0:T(1024)(128)(4,1)S(1)}, s32[]{:S(2)}) async-start(s8[5308416]{0:T(1024)(128)(4,1)} %bitcast.12), calls=%async_computation.3 | async-start | bytes 8388608
  133.0 1.2 slice-start.1
  133.0 1.8 copy-start.5
  133.0 2.2 %copy-start.7 = (bf16[3,224,1024]{2,1,0:T(8,128)(2,1)S(1)}, bf16[3,224,1024]{2,1,0:T(8,128)(2,1)}, u32[]{:S(2)}) copy-start(bf16[3,224,1024]{2,1,0:T(8,128)(2,1)} %wg_ref.1) | copy-start | bytes 4128772
  133.0 2.6 %copy-start.8 = (bf16[3,224,1024]{2,1,0:T(8,128)(2,1)S(1)}, bf16[3,224,1024]{2,1,0:T(8,128)(2,1)}, u32[]{:S(2)}) copy-start(bf16[3,224,1024]{2,1,0:T(8,128)(2,1)} %wu_ref.1) | copy-start | bytes 4128772
  135.6 45.0 %copy-start.16 = (bf16[2688,144]{1,0:T(8,128)(2,1)S(1)}, bf16[2688,144]{1,0:T(8,128)(2,1)}, u32[]{:S(2)}) copy-start(bf16[2688,144]{1,0:T(8,128)(2,1)} %copy-done.15) | copy-start | bytes 2322436
  135.6 45.0 %copy-start.18 = (bf16[128,2688]{1,0:T(8,128)(2,1)S(1)}, bf16[128,2688]{1,0:T(8,128)(2,1)}, u32[]{:S(2)}) copy-start(bf16[128,2688]{1,0:T(8,128)(2,1)} %copy-done.17) | copy-start | bytes 2064388
  135.6 45.0 %copy-start.20 = (bf16[128,2688]{1,0:T(8,128)(2,1)S(1)}, bf16[128,2688]{1,0:T(8,128)(2,1)}, u32[]{:S(2)}) copy-start(bf16[128,2688]{1,0:T(8,128)(2,1)} %copy-done.19) | copy-start | bytes 2064388

commit v4 on v3

--- a/solution.py
+++ b/solution.py
@@ -18,7 +18,9 @@
 BF16 = jnp.bfloat16
 NT = (((1,), (1,)), ((), ()))
 VMEM = pl.BlockSpec(memory_space=pltpu.VMEM)
+HBM = pl.BlockSpec(memory_space=pltpu.HBM)
 SMEM = pl.BlockSpec(memory_space=pltpu.SMEM)
+WIDE = pltpu.CompilerParams(vmem_limit_bytes=62 * 1024 * 1024)
 PARAMS = pltpu.CompilerParams(vmem_limit_bytes=24 * 1024 * 1024)
 
 
@@ -56,19 +58,30 @@
     return (lax.broadcasted_iota(jnp.int32, shape, 2) == wanted).reshape(homes * PAIR, experts)
 
 
-def send_kernel(homes, routes_ref, probs_ref, cot_ref, out_ref, right):
+def send_kernel(
+    homes, routes_in, probs_in, cot_in, out_hbm, right, routes_ref, probs_ref, cot_ref, out_ref, in_sems, out_sems
+):
     width, tokens = cot_ref.shape
+    arriving = [
+        pltpu.make_async_copy(a, b, in_sems.at[i])
+        for i, (a, b) in enumerate(((routes_in, routes_ref), (probs_in, probs_ref), (cot_in, cot_ref)))
+    ]
+    for copy in arriving:
+        copy.start()
+    right[...] = jnp.zeros_like(right)
+    for copy in arriving:
+        copy.wait()
     experts = homes * OWN
     routes = routes_ref[...].astype(F32).T.astype(jnp.int32)
     hits, ranks = rank_table(routes, experts)
     probs = probs_ref[...].T
     weight = sum(jnp.where(hit, probs[:, k : k + 1], 0.0) for k, hit in enumerate(hits)).astype(BF16)
-    right[...] = jnp.zeros_like(right)
     right[:, 0:tokens] = cot_ref[0:LANE, :].astype(BF16)
     right[0 : width - LANE, tokens : 2 * tokens] = cot_ref[LANE:width, :].astype(BF16)
     mark = lax.broadcasted_iota(jnp.int32, (LANE, tokens), 0) == width - LANE
     right[:, 2 * tokens : 3 * tokens] = mark.astype(F32).astype(BF16)
-    step = 8 if homes % 8 == 0 else homes
+    step = 8
+    leaving = []
     for first in range(0, homes, step):
         pick = expert_rows(first, step, experts).astype(F32).astype(BF16)
         rank_of = dot_nt(pick, ranks)
@@ -85,14 +98,18 @@
             ],
             axis=1,
         )
-        out_ref[first * PAIR : (first + step) * PAIR, :] = dot_nt(left, right[...]).astype(BF16)
+        there = slice(first * PAIR, (first + step) * PAIR)
+        out_ref[there, :] = dot_nt(left, right[...]).astype(BF16)
+        leaving.append(pltpu.make_async_copy(out_ref.at[there], out_hbm.at[there], out_sems.at[first // step]))
+        leaving[-1].start()
+    for copy in leaving:
+        copy.wait()
 
 
 def down_half(half, share, rows_ref, w_ref, out_ref, plus_ref=None):
     capacity = out_ref.shape[1] - share
     whole = half * (OWN - 1)
-    width = w_ref.shape[1]
-    hidden = w_ref.shape[2]
+    width, hidden = w_ref.shape[1:]
     left = rows_ref[whole, 0:capacity, 0:width]
     part = rows_ref[1, pl.ds(pl.multiple_of(half * share, 16), share), 0:width]
     tile = 2 * LANE
@@ -108,13 +125,19 @@
                 out_ref[m, top : top + count, :] = piece.astype(BF16)
 
 
-def unpack_kernel(share, half_ref, got_ref, select_ref, w_ref, rows_ref, out_ref):
+def unpack_kernel(share, half_ref, got_ref, w_ref, rows_ref, out_ref):
     sources = got_ref.shape[0] // PAIR
     capacity = sources * MOST
     rows, columns = GROUP * MOST, GROUP * PAIR
+    at = lax.broadcasted_iota(jnp.int32, (1, columns), 1)
+    source = jnp.floor((at.astype(F32) + 0.5) * (1.0 / PAIR)).astype(jnp.int32)
+    second, expert, slot = decode(at - PAIR * source)
+    goal = jnp.where(slot < MOST, (2 * expert + second) * rows + source * MOST + slot, -1)
+    select = lax.broadcasted_iota(jnp.int32, (2 * OWN * rows, columns), 0) == goal
+    select = select.astype(F32).astype(BF16)
     rows_ref[:, capacity:, :] = jnp.zeros((OWN, rows_ref.shape[1] - capacity, 2 * LANE), BF16)
     for g in range(sources // GROUP):
-        piece = dot(select_ref[...], got_ref[g * columns : (g + 1) * columns, :]).astype(BF16)
+        piece = dot(select, got_ref[g * columns : (g + 1) * columns, :]).astype(BF16)
         for e in range(OWN):
             for second in range(2):
                 top = (2 * e + second) * rows
@@ -128,7 +151,7 @@
 
 def prepare_kernel(
     homes, routes_ref, slots_ref, gate_ref, up_ref,
-    up_factor_ref, gate_factor_ref, select_in_ref, select_out_ref, first_ref, second_ref, pick_ref,
+    up_factor_ref, gate_factor_ref, select_out_ref, masks_ref, pick_ref,
 ):
     capacity, hidden = gate_ref.shape[1:]
     experts = homes * OWN
@@ -147,12 +170,6 @@
 
         lax.fori_loop(0, capacity // step, part, 0)
     rows, columns = GROUP * MOST, GROUP * PAIR
-    at = lax.broadcasted_iota(jnp.int32, (1, columns), 1)
-    source = jnp.floor((at.astype(F32) + 0.5) * (1.0 / PAIR)).astype(jnp.int32)
-    second, expert, slot = decode(at - PAIR * source)
-    goal = jnp.where(slot < MOST, (2 * expert + second) * rows + source * MOST + slot, -1)
-    select = lax.broadcasted_iota(jnp.int32, (2 * OWN * rows, columns), 0) == goal
-    select_in_ref[...] = select.astype(F32).astype(BF16)
     shape = (GROUP, PAIR, 2 * OWN * rows)
     second, expert, slot = decode(lax.broadcasted_iota(jnp.int32, shape, 1))
     goal = (2 * expert + second) * rows + lax.broadcasted_iota(jnp.int32, shape, 0) * MOST + slot
@@ -161,8 +178,9 @@
     _, ranks = rank_table(routes_ref[...].astype(F32).T.astype(jnp.int32), experts)
     pick_ref[...] = expert_rows(0, homes, experts).astype(F32).astype(BF16)
     rank_of = dot_nt(ranks, pick_ref[...])
-    first_ref[...] = (rank_of == slots_ref[0:1, :]).astype(F32).astype(BF16)
-    second_ref[...] = (rank_of == slots_ref[1:2, :]).astype(F32).astype(BF16)
+    tokens = rank_of.shape[0]
+    masks_ref[0:tokens] = (rank_of == slots_ref[0:1, :]).astype(F32).astype(BF16)
+    masks_ref[tokens:] = (rank_of == slots_ref[1:2, :]).astype(F32).astype(BF16)
 
 
 def sum_kernel(parts_ref, out_ref):
@@ -179,66 +197,64 @@
 
 def back_kernel(
     share, grad_ref, rows_ref, up_ref, up_factor_ref, gate_factor_ref, wg_ref, wu_ref, select_ref, out_ref,
-    gate_grad, up_grad, score, back,
+    gate_grad, up_grad, back,
 ):
     sources = out_ref.shape[0] // PAIR
     capacity = sources * MOST
     width = wg_ref.shape[1]
     blocks = up_ref.shape[2] // LANE
     rows, columns = GROUP * MOST, GROUP * PAIR
-    tail = capacity - share
-    for e, low, count, half, top in (
-        (0, 0, capacity, 0, 0),
-        (OWN - 1, 0, capacity, 1, 0),
-        (1, 0, share, 0, capacity),
-        (1, share, tail, 1, capacity),
-    ):
-        here = slice(0, count)
-        score[here] = jnp.zeros((count, LANE), F32)
-
-        def block(b, carry, e=e, low=low, count=count, half=half, top=top, here=here):
-            columns = pl.ds(pl.multiple_of(b * LANE, LANE), LANE)
-            scale = jnp.exp2(grad_ref[2 * b + half, capacity + share : capacity + share + 1, :])
-            grad = grad_ref[2 * b + half, top : top + count, :] * scale
-            by_up = grad * up_factor_ref[e, low : low + count, columns]
-            score[here] += by_up * up_ref[e, low : low + count, columns].astype(F32)
-            up_grad[here, columns] = by_up.astype(BF16)
-            gate_grad[here, columns] = (grad * gate_factor_ref[e, low : low + count, columns]).astype(BF16)
-            return carry
-
-        lax.fori_loop(0, blocks, block, 0)
-        weight = rows_ref[e, low : low + count, LANE:].astype(F32)[:, width - LANE : width - LANE + 1]
-        total = dot_nt(gate_grad[here], wg_ref[e]) + dot_nt(up_grad[here], wu_ref[e])
-        total = total * weight
-        sums = jnp.sum(score[here], axis=1, keepdims=True)
-        high = sums.astype(BF16).astype(F32)
-        at = lax.broadcasted_iota(jnp.int32, (count, 2 * LANE - width), 1)
-        ends = jnp.where(at == 0, high, jnp.where(at == 1, sums - high, 0.0)).astype(BF16)
-        total = total.astype(BF16)
-        done = 0
-        while done < count:
-            group, inner = divmod(low + done, rows)
-            n = min(rows - inner, count - done)
-            first = group * 2 * OWN * rows + 2 * e * rows + inner
-            back[first : first + n, :] = total[done : done + n, 0:LANE]
-            back[first + rows : first + rows + n, 0 : width - LANE] = total[done : done + n, LANE:width]
-            back[first + rows : first + rows + n, width - LANE :] = ends[done : done + n]
-            done += n
+    last = capacity + share
+    scales = [jnp.exp2(grad_ref[i, last : last + 1, :]) for i in range(2 * blocks)]
+    for e in range(OWN):
+        cuts = sorted({*range(0, capacity + 1, rows), *((share,) if e == 1 else ())})
+        pieces = []
+        for low, high in zip(cuts, cuts[1:]):
+            half = {0: 0, OWN - 1: 1}.get(e, int(low >= share))
+            top = low if e != 1 else capacity + low - half * share
+            pieces.append((low, high, half, top))
+        for low, high, half, top in pieces:
+            score = jnp.zeros((high - low, LANE), F32)
+            for b in range(blocks):
+                at = slice(b * LANE, (b + 1) * LANE)
+                grad = grad_ref[2 * b + half, top : top + high - low, :] * scales[2 * b + half]
+                by_up = grad * up_factor_ref[e, low:high, at]
+                score = score + by_up * up_ref[e, low:high, at].astype(F32)
+                up_grad[e, low:high, at] = by_up.astype(BF16)
+                gate_grad[e, low:high, at] = (grad * gate_factor_ref[e, low:high, at]).astype(BF16)
+            sums = jnp.sum(score, axis=1, keepdims=True)
+            near = sums.astype(BF16).astype(F32)
+            lane = lax.broadcasted_iota(jnp.int32, (high - low, 2 * LANE - width), 1)
+            ends = jnp.where(lane == 0, near, jnp.where(lane == 1, sums - near, 0.0)).astype(BF16)
+            group, inner = divmod(low, rows)
+            first = (group * OWN + e) * 2 * rows + rows + inner
+            back[first : first + high - low, width - LANE :] = ends
+        total = dot_nt(gate_grad[e], wg_ref[e]) + dot_nt(up_grad[e], wu_ref[e])
+        weight = rows_ref[e, 0:capacity, LANE:].astype(F32)[:, width - LANE : width - LANE + 1]
+        total = (total * weight).astype(BF16)
+        for group in range(sources // GROUP):
+            first = (group * OWN + e) * 2 * rows
+            piece = total[group * rows : (group + 1) * rows]
+            back[first : first + rows, :] = piece[:, 0:LANE]
+            back[first + rows : first + 2 * rows, 0 : width - LANE] = piece[:, LANE:width]
     for g in range(sources // GROUP):
         piece = dot(select_ref[...], back[g * 2 * OWN * rows : (g + 1) * 2 * OWN * rows, :])
         out_ref[g * columns : (g + 1) * columns, :] = piece.astype(BF16)
 
 
-def combine_kernel(routes_ref, first_ref, second_ref, pick_ref, got_ref, tokens_ref, probs_ref):
+def combine_kernel(routes_ref, masks_ref, pick_ref, got_ref, tokens_ref, probs_ref, both):
     width, tokens = tokens_ref.shape
     experts = pick_ref.shape[1]
-    tokens_ref[0:LANE, :] = dot(first_ref[...], got_ref[...]).T
-    tokens_ref[LANE:width, :] = dot(second_ref[...], got_ref[...]).T[: width - LANE]
+    sums = dot(masks_ref[...], got_ref[...])
+    tokens_ref[0:LANE, :] = sums[0:tokens].T
+    tokens_ref[LANE:width, :] = sums[tokens:].T[: width - LANE]
     at = lax.broadcasted_iota(jnp.int32, (16, LANE), 1) - lax.broadcasted_iota(jnp.int32, (16, LANE), 0)
     ends = dot_nt((at == width - LANE).astype(F32).astype(BF16), got_ref[...])
-    second = second_ref[...].astype(F32)
-    table = dot((second * ends[0:1, :]).astype(BF16), pick_ref[...])
-    table = table + dot((second * ends[1:2, :]).astype(BF16), pick_ref[...])
+    second = masks_ref[tokens:, :].astype(F32)
+    both[0:tokens] = (second * ends[0:1, :]).astype(BF16)
+    both[tokens:] = (second * ends[1:2, :]).astype(BF16)
+    table = dot(both[...], pick_ref[...])
+    table = table[0:tokens] + table[tokens:]
     routes = routes_ref[...].astype(F32).T.astype(jnp.int32)
     top = routes.shape[1]
     lane = lax.broadcasted_iota(jnp.int32, (tokens, experts), 1)
@@ -271,10 +287,18 @@
         send = pl.pallas_call(
             functools.partial(send_kernel, homes),
             out_shape=jax.ShapeDtypeStruct((packed, LANE), BF16),
-            in_specs=[VMEM] * 3,
-            out_specs=VMEM,
-            scratch_shapes=[pltpu.VMEM((LANE, 3 * tokens), BF16)],
-            compiler_params=PARAMS,
+            in_specs=[HBM] * 3,
+            out_specs=HBM,
+            scratch_shapes=[
+                pltpu.VMEM((LANE, 3 * tokens), BF16),
+                pltpu.VMEM(routes.shape[::-1], jnp.int32),
+                pltpu.VMEM(probs.shape[::-1], F32),
+                pltpu.VMEM((width, tokens), F32),
+                pltpu.VMEM((packed, LANE), BF16),
+                pltpu.SemaphoreType.DMA((3,)),
+                pltpu.SemaphoreType.DMA((homes // 8,)),
+            ],
+            compiler_params=WIDE,
             cost_estimate=cost(10**9, 10**6),
         )(routes.T, probs.T, cotangent.T)
     row = np.arange(packed) % PAIR
@@ -284,35 +308,32 @@
     with jax.named_scope("prepare"):
         factor = jax.ShapeDtypeStruct(gate_pre.shape, F32)
         there, column = 2 * OWN * GROUP * MOST, GROUP * PAIR
-        mask = jax.ShapeDtypeStruct((tokens, packed), BF16)
         ready = pl.pallas_call(
             functools.partial(prepare_kernel, homes),
             out_shape=(
                 factor,
                 factor,
-                jax.ShapeDtypeStruct((there, column), BF16),
                 jax.ShapeDtypeStruct((column, there), BF16),
-                mask,
-                mask,
+                jax.ShapeDtypeStruct((2 * tokens, packed), BF16),
                 jax.ShapeDtypeStruct((packed, homes * OWN), BF16),
             ),
             in_specs=[VMEM] * 4,
-            out_specs=(VMEM,) * 7,
+            out_specs=(VMEM,) * 5,
             compiler_params=PARAMS,
             cost_estimate=pl.CostEstimate(flops=2 * 10**7, bytes_accessed=2 * 10**7, transcendentals=10**6),
         )(routes.T, jnp.asarray(slots), gate_pre, up_pre)
     with jax.named_scope("dispatch"):
         got = lax.all_to_all(send.reshape(homes, PAIR, LANE), ("x", "z"), 0, 0, tiled=True).reshape(packed, LANE)
-    up_factor, gate_factor, select_in, select_out, first, second, pick = ready
+        got, (up_factor, gate_factor, select_out, masks, pick) = lax.optimization_barrier((got, ready))
     with jax.named_scope("down_other"):
         rows, other = pl.pallas_call(
             functools.partial(unpack_kernel, share),
             out_shape=(rows_shape, half_shape),
-            in_specs=[SMEM, VMEM, VMEM, VMEM],
+            in_specs=[SMEM, VMEM, VMEM],
             out_specs=(VMEM, VMEM),
             compiler_params=PARAMS,
             cost_estimate=cost(10**9, 4 * 10**6),
-        )(here, got, select_in, w_down)
+        )(here, got, w_down)
     with jax.named_scope("swap_cores"):
         swapped = lax.ppermute(other, "core", [(0, 1), (1, 0)])
     with jax.named_scope("down_own"):
@@ -343,9 +364,8 @@
             in_specs=[VMEM] * 8,
             out_specs=VMEM,
             scratch_shapes=[
-                pltpu.VMEM((capacity, hidden), BF16),
-                pltpu.VMEM((capacity, hidden), BF16),
-                pltpu.VMEM((capacity, LANE), F32),
+                pltpu.VMEM((OWN, capacity, hidden), BF16),
+                pltpu.VMEM((OWN, capacity, hidden), BF16),
                 pltpu.VMEM((homes * MOST * 2 * OWN, LANE), BF16),
             ],
             compiler_params=PARAMS,
@@ -360,11 +380,12 @@
                 jax.ShapeDtypeStruct((width, tokens), F32),
                 jax.ShapeDtypeStruct(probs.shape[::-1], F32),
             ),
-            in_specs=[VMEM] * 5,
+            in_specs=[VMEM] * 4,
             out_specs=(VMEM, VMEM),
+            scratch_shapes=[pltpu.VMEM((2 * tokens, packed), BF16)],
             compiler_params=PARAMS,
             cost_estimate=cost(10**9, 10**6),
-        )(routes.T, first, second, pick, home)
+        )(routes.T, masks, pick, home)
         return grad_tokens.T, grad_probs.T
 
 

time: 184 us -> 177 us (0.962)
  local copies, waits for them, and re-layouts: 19.4 us -> 11.6 us
    unnamed x54 -> x34, local copies, waits for them, and re-layouts: 19.4 us -> 11.6 us
    pallas_call x1, Pallas kernels: 8.13 us -> 4.45 us  [on_device(): pl.pallas_call(functools.partial(back_kernel, share), out_shape=jax.Shape...]
where the time goes in v4:
time: 177 us; the launch traced here: 176 us
  blocking collectives  105 us (59%)
  starting transfers between devices  20.6 us (12%)
  waiting for transfers between devices  19 us (11%)
  Pallas kernels  18.7 us (11%)
  local copies, waits for them, and re-layouts  11.6 us (7%)
    all_to_all x1, blocking collectives, on_device(): parts = lax.all_to_all(chip, 'y', 0, 0, tiled=True)  42.5 us
    all_to_all x1, blocking collectives, on_device(): lax.all_to_all(back.reshape(homes, PAIR, LANE), ('x', 'z'), 0, 0, tiled=T...  37 us
    all_gather x1, blocking collectives, on_device(): lax.all_gather(scaled.astype(jnp.float16), ('y', 'core'), axis=0)  25.3 us
    all_to_all x1, starting transfers between devices, on_device(): lax.all_to_all(send.reshape(homes, PAIR, LANE), ('x', 'z'), 0, 0, tiled=T...  18.7 us
    all_to_all x1, waiting for transfers between devices, on_device(): lax.all_to_all(send.reshape(homes, PAIR, LANE), ('x', 'z'), 0, 0, tiled=T...  16 us
    unnamed x34, local copies, waits for them, and re-layouts  11.6 us
    pallas_call x1, Pallas kernels, on_device(): pl.pallas_call(functools.partial(back_kernel, share), out_shape=jax.Shape...  4.45 us
    pallas_call x1, Pallas kernels, on_device(): pl.pallas_call(functools.partial(send_kernel, homes), out_shape=jax.Shape...  3.78 us
  transfers between devices with their start and end apart: 2, of which 2 were waited for; matrix products, arithmetic and copies ran while one was open for 0% of the time, Pallas kernels for 2%

profile of v4, /device:TPU:6, one launch (start us, length us, event | category | flops | bytes accessed | tf_op | source)
XLA Modules:
  0.0 176.1 jit_solution(5202731213383120220)
XLA Ops:
  0.6 3.8 %send_rows.1 = bf16[2688,128]{1,0:T(8,128)(2,1)} custom-call(s32[8,128]{1,0:T(8,128)} %bitcast.16, f32[8,128]{1,0:T(8,128)} %bitcast.22, f32[224,128]{1,0:T(8,128)} %bitcast.21), custom_call_target="tpu_custom_call" | custom-call | flops 1000000000 | bytes 1000000 | tf_op jit(solution)/shard_map/send_rows/pallas_call | solution.py:287
  4.4 0.0 copy-start.9
  4.4 0.0 copy-start.10
  4.4 18.7 %all-to-all-start = ((bf16[48,56,128]{2,1,0:T(8,128)(2,1)}), bf16[48,56,128]{2,1,0:T(8,128)(2,1)}, u32[]{:S(2)}, u32[]{:S(2)}) async-start(bf16[48,56,128]{2,1,0:T(8,128)(2,1)} %bitcast.20), calls=%async_computation | async-start | bytes 1376256 | tf_op jit(solution)/shard_map/dispatch/all_to_all | solution.py:326
  23.1 0.0 copy-done.9
  23.1 0.0 copy-done.10
  23.1 0.0 copy-start
  23.2 1.7 copy-done
  24.9 0.0 copy-start.5
  24.9 1.7 copy-done.5
  26.7 0.0 copy-start.6
  26.7 3.6 %prepare.1 = (f32[3,432,1024]{2,1,0:T(8,128)S(1)}, f32[3,432,1024]{2,1,0:T(8,128)S(1)}, bf16[896,864]{1,0:T(8,128)(2,1)S(1)}, bf16[256,2688]{1,0:T(8,128)(2,1)S(1)}, bf16[2688,144]{1,0:T(8,128)(2,1)S(1)}) custom-call(s32[8,128]{1,0:T(8,128)S(1)} %bitcast.17, f32[2,2688]{1,0:T(2,128)S(1)} %copy-done.9, bf16[3,432,1024]{2,1,0:T(8,128)(2,1)S(1)} %copy-done.5, ...), custom_call_target="tpu_custom_call" | custom-call | flops 20000000 | bytes 20000000 | tf_op jit(solution)/shard_map/prepare/pallas_call | solution.py:311
  30.2 0.0 copy-start.2
  30.3 2.3 %copy-done.2 = f32[3,432,1024]{2,1,0:T(8,128)} copy-done((f32[3,432,1024]{2,1,0:T(8,128)}, f32[3,432,1024]{2,1,0:T(8,128)S(1)}, u32[]{:S(2)}) %copy-start.2) | copy-done | bytes 5308440
  32.6 0.0 copy-start.3
  32.6 2.4 %copy-done.3 = f32[3,432,1024]{2,1,0:T(8,128)} copy-done((f32[3,432,1024]{2,1,0:T(8,128)}, f32[3,432,1024]{2,1,0:T(8,128)S(1)}, u32[]{:S(2)}) %copy-start.3) | copy-done | bytes 5308440
  35.0 0.0 copy-start.11
  35.0 1.1 copy-done.11
  36.1 0.0 copy-start.13
  36.1 1.1 copy-done.13
  37.2 16.0 %all-to-all-done = bf16[48,56,128]{2,1,0:T(8,128)(2,1)} async-done(((bf16[48,56,128]{2,1,0:T(8,128)(2,1)}), bf16[48,56,128]{2,1,0:T(8,128)(2,1)}, u32[]{:S(2)}, u32[]{:S(2)}) %all-to-all-start) | async-done | bytes 688160 | tf_op jit(solution)/shard_map/dispatch/all_to_all | solution.py:326
  53.2 0.0 copy-done.6
  53.2 3.5 %down_other.1 = (bf16[3,448,256]{2,1,0:T(8,128)(2,1)S(1)}, bf16[8,656,128]{2,1,0:T(8,128)(2,1)S(1)}) custom-call(s32[1]{0:T(128)} %bitcast.5.half_ref, bf16[2688,128]{1,0:T(8,128)(2,1)} %bitcast.4.got_ref, bf16[3,224,1024]{2,1,0:T(8,128)(2,1)S(1)} %copy-done.6), custom_call_target="tpu_custom_call" | custom-call | flops 1000000000 | bytes 4000000 | tf_op jit(solution)/shard_map/down_other/pallas_call | solution.py:329
  56.7 1.9 %collective-permute-start = (bf16[8,656,128]{2,1,0:T(8,128)(2,1)S(1)}, bf16[8,656,128]{2,1,0:T(8,128)(2,1)S(1)}, u32[]{:S(2)}, u32[]{:S(2)}) collective-permute-start(bf16[8,656,128]{2,1,0:T(8,128)(2,1)S(1)} %get-tuple-element.26), channel_id=1, source_target_pairs={{0,48},{48,0},{1,49},{49,1},{2,50},{50,2},{3,51},{51,3},{4,52},{52... | collective-permute-start | bytes 4030472 | tf_op jit(solution)/shard_map/swap_cores/ppermute | solution.py:338
  58.6 3.0 %collective-permute-done.plus_ref = bf16[8,656,128]{2,1,0:T(8,128)(2,1)S(1)} collective-permute-done((bf16[8,656,128]{2,1,0:T(8,128)(2,1)S(1)}, bf16[8,656,128]{2,1,0:T(8,128)(2,1)S(1)}, u32[]{:S(2)}, u32[]{:S(2)}) %collective-permute-start) | collective-permute-done | bytes 1343520 | tf_op jit(solution)/shard_map/swap_cores/ppermute | solution.py:338
  61.7 0.0 slice-start
  61.7 0.5 down_own.1
  62.2 0.0 copy-start.7
  62.2 0.0 copy-start.8
  62.2 42.5 %all_to_all.15.parts_ref = bf16[8,656,128]{2,1,0:T(8,128)(2,1)S(1)} all-to-all(bf16[8,656,128]{2,1,0:T(8,128)(2,1)S(1)} %down_own.1), channel_id=1, replica_groups=mesh['y'=8,'core'=2,'x'=4,'z'=12] {'y'}, dimensions={0} | all-to-all | bytes 2686976 | tf_op jit(solution)/shard_map/sum_over_y/all_to_all | solution.py:349
  104.8 0.3 sum_over_y.1
  105.1 0.0 slice-start.1
  105.1 25.3 %all-gather.2 = f16[10752,128]{1,0:T(8,128)(2,1)S(1)} all-gather(f16[672,128]{1,0:T(8,128)(2,1)S(1)} %convert_element_type.6), channel_id=2, replica_groups=mesh['y'=8,'core'=2,'x'=4,'z'=12] {'y','core'}, dimensions={0}, use_global_device_ids=true | all-gather | bytes 2924544 | tf_op jit(solution)/shard_map/gather_hidden/all_gather | solution.py:359
  130.4 0.0 copy-start.1
  130.4 0.5 convert.grad_ref
  130.9 0.0 slice-done
  130.9 0.0 copy-done.7
  131.0 0.0 copy-done.8
  131.0 0.0 copy-done.4
  131.0 0.0 slice-done.1
  131.0 1.1 copy-done.1
  132.1 0.0 copy-start.14
  132.1 4.4 %back.1 = bf16[2688,128]{1,0:T(8,128)(2,1)S(1)} custom-call(f32[16,672,128]{2,1,0:T(8,128)S(1)} %convert.grad_ref, bf16[3,448,256]{2,1,0:T(8,128)(2,1)S(1)} %get-tuple-element.25.rows_ref, bf16[3,432,1024]{2,1,0:T(8,128)(2,1)S(1)} %copy-done.1, f32[3,432,1024]{2,1,0:T(8,128)S(1)} %bitcast.13, f32[3,432,1024]{2,1,0:T(8,128)S(1)} %copy-done.4, ...), custom_call_target="tpu_custom_call" | custom-call | flops 2000000000 | bytes 10000000 | tf_op jit(solution)/shard_map/back/pallas_call | solution.py:361
  136.6 0.0 copy-start.12
  136.6 37.0 %all_to_all.16 = bf16[48,56,128]{2,1,0:T(8,128)(2,1)S(1)} all-to-all(bf16[48,56,128]{2,1,0:T(8,128)(2,1)S(1)} %bitcast.14), channel_id=1, replica_groups=mesh['y'=8,'core'=2,'x'=4,'z'=12] {'x','z'}, dimensions={0} | all-to-all | bytes 1376256 | tf_op jit(solution)/shard_map/way_back/all_to_all | solution.py:375
  173.6 0.0 copy-done.14
  173.6 0.0 copy-done.12
  173.6 2.5 %combine.1 = (f32[224,128]{1,0:T(8,128)}, f32[8,128]{1,0:T(8,128)}) custom-call(s32[8,128]{1,0:T(8,128)S(1)} %bitcast.18, bf16[256,2688]{1,0:T(8,128)(2,1)S(1)} %copy-done.12, bf16[2688,144]{1,0:T(8,128)(2,1)S(1)} %copy-done.14, bf16[2688,128]{1,0:T(8,128)(2,1)S(1)} %bitcast.15), custom_call_target="tpu_custom_call" | custom-call | flops 1000000000 | bytes 1000000 | tf_op jit(solution)/shard_map/combine/pallas_call | solution.py:377
  (3 shorter events, 0.0 us)
Async XLA Ops:
  4.4 18.7 %copy-start.9 = (f32[2,2688]{1,0:T(2,128)S(1)}, f32[2,2688]{1,0:T(2,128)}, u32[]{:S(2)}) copy-start(f32[2,2688]{1,0:T(2,128)} %constant.7.clone.slots_ref) | copy-start | bytes 64516
  4.4 18.7 %copy-start.10 = (s32[128,8]{0,1:T(8,128)S(1)}, s32[128,8]{0,1:T(8,128)}, u32[]{:S(2)}) copy-start(s32[128,8]{0,1:T(8,128)} %param.11) | copy-start | bytes 12292
  4.4 48.7 %all-to-all-start = ((bf16[48,56,128]{2,1,0:T(8,128)(2,1)}), bf16[48,56,128]{2,1,0:T(8,128)(2,1)}, u32[]{:S(2)}, u32[]{:S(2)}) async-start(bf16[48,56,128]{2,1,0:T(8,128)(2,1)} %bitcast.20), calls=%async_computation | async-start | bytes 1376256 | tf_op jit(solution)/shard_map/dispatch/all_to_all | solution.py:326
  23.1 1.8 copy-start
  24.9 1.7 copy-start.5
  26.7 26.5 %copy-start.6 = (bf16[3,224,1024]{2,1,0:T(8,128)(2,1)S(1)}, bf16[3,224,1024]{2,1,0:T(8,128)(2,1)}, u32[]{:S(2)}) copy-start(bf16[3,224,1024]{2,1,0:T(8,128)(2,1)} %w_ref.3) | copy-start | bytes 4128772
  30.2 2.4 %copy-start.2 = (f32[3,432,1024]{2,1,0:T(8,128)}, f32[3,432,1024]{2,1,0:T(8,128)S(1)}, u32[]{:S(2)}) copy-start(f32[3,432,1024]{2,1,0:T(8,128)S(1)} %get-tuple-element.27.up_factor_ref) | copy-start | bytes 15925252
  32.6 2.4 %copy-start.3 = (f32[3,432,1024]{2,1,0:T(8,128)}, f32[3,432,1024]{2,1,0:T(8,128)S(1)}, u32[]{:S(2)}) copy-start(f32[3,432,1024]{2,1,0:T(8,128)S(1)} %get-tuple-element.28.gate_factor_ref) | copy-start | bytes 15925252
  35.0 1.1 copy-start.11
  36.1 1.1 copy-start.13
  56.7 5.0 %collective-permute-start = (bf16[8,656,128]{2,1,0:T(8,128)(2,1)S(1)}, bf16[8,656,128]{2,1,0:T(8,128)(2,1)S(1)}, u32[]{:S(2)}, u32[]{:S(2)}) collective-permute-start(bf16[8,656,128]{2,1,0:T(8,128)(2,1)S(1)} %get-tuple-element.26), channel_id=1, source_target_pairs={{0,48},{48,0},{1,49},{49,1},{2,50},{50,2},{3,51},{51,3},{4,52},{52... | collective-permute-start | bytes 4030472 | tf_op jit(solution)/shard_map/swap_cores/ppermute | solution.py:338
  61.7 69.3 %slice-start = ((s8[5308416]{0:T(1024)(128)(4,1)}), s8[1114112]{0:T(1024)(128)(4,1)S(1)}, s32[]{:S(2)}) async-start(s8[5308416]{0:T(1024)(128)(4,1)} %bitcast.12), calls=%async_computation.3 | async-start | bytes 2228224
  62.2 68.7 %copy-start.7 = (bf16[3,224,1024]{2,1,0:T(8,128)(2,1)S(1)}, bf16[3,224,1024]{2,1,0:T(8,128)(2,1)}, u32[]{:S(2)}) copy-start(bf16[3,224,1024]{2,1,0:T(8,128)(2,1)} %wg_ref.1) | copy-start | bytes 4128772
  62.2 68.7 %copy-start.8 = (bf16[3,224,1024]{2,1,0:T(8,128)(2,1)S(1)}, bf16[3,224,1024]{2,1,0:T(8,128)(2,1)}, u32[]{:S(2)}) copy-start(bf16[3,224,1024]{2,1,0:T(8,128)(2,1)} %wu_ref.1) | copy-start | bytes 4128772
  104.8 26.2 %copy-start.4 = (f32[3,432,1024]{2,1,0:T(8,128)S(1)}, f32[3,432,1024]{2,1,0:T(8,128)}, u32[]{:S(2)}) copy-start(f32[3,432,1024]{2,1,0:T(8,128)} %copy-done.3) | copy-start | bytes 15925252
  105.1 25.9 %slice-start.1 = ((s8[5308416]{0:T(1024)(128)(4,1)}), s8[4194304]{0:T(1024)(128)(4,1)S(1)}, s32[]{:S(2)}) async-start(s8[5308416]{0:T(1024)(128)(4,1)} %bitcast.12), calls=%async_computation.4 | async-start | bytes 8388608
  130.4 1.7 copy-start.1
  132.1 41.5 %copy-start.14 = (bf16[2688,144]{1,0:T(8,128)(2,1)S(1)}, bf16[2688,144]{1,0:T(8,128)(2,1)}, u32[]{:S(2)}) copy-start(bf16[2688,144]{1,0:T(8,128)(2,1)} %copy-done.13) | copy-start | bytes 2322436
  136.6 37.0 %copy-start.12 = (bf16[256,2688]{1,0:T(8,128)(2,1)S(1)}, bf16[256,2688]{1,0:T(8,128)(2,1)}, u32[]{:S(2)}) copy-start(bf16[256,2688]{1,0:T(8,128)(2,1)} %copy-done.11) | copy-start | bytes 4128772

commit v5 on v4

--- a/solution.py
+++ b/solution.py
@@ -106,7 +106,7 @@
         copy.wait()
 
 
-def down_half(half, share, rows_ref, w_ref, out_ref, plus_ref=None):
+def down_half(half, share, rows_ref, w_ref, out_ref, plus_ref=None, here=None):
     capacity = out_ref.shape[1] - share
     whole = half * (OWN - 1)
     width, hidden = w_ref.shape[1:]
@@ -122,7 +122,8 @@
             for m, piece in ((2 * n, a[:, :LANE]), (2 * n + 1, a[:, LANE:])):
                 if plus_ref is not None:
                     piece = piece + plus_ref[m, top : top + count, :].astype(F32)
-                out_ref[m, top : top + count, :] = piece.astype(BF16)
+                at = m if here is None else lax.rem(m + out_ref.shape[0] - here, out_ref.shape[0])
+                out_ref[at, top : top + count, :] = piece.astype(BF16)
 
 
 def unpack_kernel(share, half_ref, got_ref, w_ref, rows_ref, out_ref):
@@ -145,8 +146,24 @@
     down_half(1 - half_ref[0], share, rows_ref, w_ref, out_ref)
 
 
-def down_kernel(share, half_ref, rows_ref, w_ref, plus_ref, out_ref):
-    down_half(half_ref[0], share, rows_ref, w_ref, out_ref, plus_ref)
+def down_kernel(share, half_ref, rows_ref, w_ref, plus_ref, own_ref, right_ref, left_ref, right_far_ref, left_far_ref, ring):
+    down_half(half_ref[0], share, rows_ref, w_ref, ring, plus_ref, half_ref[1])
+    for out, distances in ((own_ref, (0, 2, 6)), (right_ref, (1, 3)), (left_ref, (7, 5))):
+        for i, k in enumerate(distances):
+            out[i] = ring[k]
+    near = right_far_ref.shape[0]
+    right_far_ref[...] = ring[4, 0:near, :]
+    left_far_ref[...] = ring[4, near:, :]
+
+
+def relay_kernel(own_ref, right_ref, left_ref, right_far_ref, left_far_ref, right_out, left_out):
+    near = right_far_ref.shape[0]
+    right = own_ref[1].astype(F32) + right_ref[1].astype(F32)
+    left = own_ref[2].astype(F32) + left_ref[1].astype(F32)
+    right_out[0:near, :] = (right[0:near] + right_far_ref[...].astype(F32)).astype(BF16)
+    right_out[near:, :] = right[near:].astype(BF16)
+    left_out[0:near, :] = left[0:near].astype(BF16)
+    left_out[near:, :] = (left[near:] + left_far_ref[...].astype(F32)).astype(BF16)
 
 
 def prepare_kernel(
@@ -183,11 +200,10 @@
     masks_ref[tokens:] = (rank_of == slots_ref[1:2, :]).astype(F32).astype(BF16)
 
 
-def sum_kernel(parts_ref, out_ref):
-    sources, rows, _ = parts_ref.shape
-    total = parts_ref[0].astype(F32)
-    for i in range(1, sources):
-        total = total + parts_ref[i].astype(F32)
+def sum_kernel(own_ref, right_ref, left_ref, right_two_ref, left_two_ref, out_ref):
+    rows = own_ref.shape[1]
+    total = own_ref[0].astype(F32) + right_ref[0].astype(F32) + left_ref[0].astype(F32)
+    total = total + right_two_ref[...].astype(F32) + left_two_ref[...].astype(F32)
     largest = jnp.max(jnp.max(jnp.abs(total), axis=0, keepdims=True), axis=1, keepdims=True)
     largest = jnp.broadcast_to(jnp.maximum(largest, 1e-35), (16, LANE))
     power = jnp.clip(jnp.floor(jnp.log2(largest)), -100.0, 100.0)
@@ -279,7 +295,7 @@
     share = -(-capacity // 32) * 16
     blocks = hidden // LANE
     packed = homes * PAIR
-    here = lax.axis_index("core").astype(jnp.int32)[None]
+    here = jnp.stack([lax.axis_index("core"), lax.axis_index("y")]).astype(jnp.int32)
     half_shape = jax.ShapeDtypeStruct((blocks, capacity + share, LANE), BF16)
     rows_shape = jax.ShapeDtypeStruct((OWN, 2 * share, 2 * LANE), BF16)
 
@@ -337,24 +353,43 @@
     with jax.named_scope("swap_cores"):
         swapped = lax.ppermute(other, "core", [(0, 1), (1, 0)])
     with jax.named_scope("down_own"):
-        chip = pl.pallas_call(
+        tall = capacity + share
+        near = -(-tall // 32) * 16
+        own, right, left, right_far, left_far = pl.pallas_call(
             functools.partial(down_kernel, share),
-            out_shape=half_shape,
+            out_shape=[
+                jax.ShapeDtypeStruct(shape, BF16)
+                for shape in ((3, tall, LANE), (2, tall, LANE), (2, tall, LANE), (near, LANE), (tall - near, LANE))
+            ],
             in_specs=[SMEM, VMEM, VMEM, VMEM],
-            out_specs=VMEM,
+            out_specs=[VMEM] * 5,
+            scratch_shapes=[pltpu.VMEM(half_shape.shape, BF16)],
             compiler_params=PARAMS,
             cost_estimate=cost(10**9, 4 * 10**6),
         )(here, rows, w_down, swapped)
     with jax.named_scope("sum_over_y"):
-        parts = lax.all_to_all(chip, "y", 0, 0, tiled=True)
+        def shifted(value, by):
+            return lax.ppermute(value, "y", [(i, (i + by) % blocks) for i in range(blocks)])
+
+        right, left = shifted(right, 1), shifted(left, -1)
+        right_far, left_far = shifted(right_far, 2), shifted(left_far, -2)
+        right_two, left_two = pl.pallas_call(
+            relay_kernel,
+            out_shape=[jax.ShapeDtypeStruct((tall, LANE), BF16)] * 2,
+            in_specs=[VMEM] * 5,
+            out_specs=[VMEM] * 2,
+            compiler_params=PARAMS,
+            cost_estimate=cost(10**6, 2 * 10**6),
+        )(own, right, left, right_far, left_far)
+        right_two, left_two = shifted(right_two, 2), shifted(left_two, -2)
         scaled = pl.pallas_call(
             sum_kernel,
             out_shape=jax.ShapeDtypeStruct((capacity + share + 16, LANE), F32),
-            in_specs=[VMEM],
+            in_specs=[VMEM] * 5,
             out_specs=VMEM,
             compiler_params=PARAMS,
             cost_estimate=cost(10**6, 3 * 10**6),
-        )(parts)
+        )(own, right, left, right_two, left_two)
     with jax.named_scope("gather_hidden"):
         grad = lax.all_gather(scaled.astype(jnp.float16), ("y", "core"), axis=0).astype(F32)
     with jax.named_scope("back"):

time: 177 us -> 172 us (0.972)
  blocking collectives: 105 us -> 61.7 us
  starting transfers between devices: 20.6 us -> 43.7 us
  waiting for transfers between devices: 19 us -> 31.1 us
  local copies, waits for them, and re-layouts: 11.6 us -> 13.4 us
    all_to_all x1 -> x0, blocking collectives: 42.5 us -> none  [on_device(): parts = lax.all_to_all(chip, 'y', 0, 0, tiled=True)]
    ppermute x0 -> x6, starting transfers between devices: none -> 23.2 us  [shifted(): lax.ppermute(value, 'y', [(i, (i + by) % blocks) for i in range(blocks)])]
    ppermute x0 -> x6, waiting for transfers between devices: none -> 12.2 us  [shifted(): lax.ppermute(value, 'y', [(i, (i + by) % blocks) for i in range(blocks)])]
  transfers between devices with their start and end apart: 2 -> 8, of which waited for: 2 -> 5; matrix products, arithmetic and copies ran while one was open for 0% -> 0% of each run, Pallas kernels for 2% -> 2%
where the time goes in v5:
time: 172 us; the launch traced here: 170 us
  blocking collectives  61.7 us (36%)
  starting transfers between devices  43.7 us (25%)
  waiting for transfers between devices  31.1 us (18%)
  Pallas kernels  19.1 us (11%)
  local copies, waits for them, and re-layouts  13.4 us (8%)
    all_to_all x1, blocking collectives, on_device(): lax.all_to_all(back.reshape(homes, PAIR, LANE), ('x', 'z'), 0, 0, tiled=T...  36.9 us
    all_gather x1, blocking collectives, on_device(): lax.all_gather(scaled.astype(jnp.float16), ('y', 'core'), axis=0)  24.8 us
    ppermute x6, starting transfers between devices, shifted(): lax.ppermute(value, 'y', [(i, (i + by) % blocks) for i in range(blocks)])  23.2 us
    all_to_all x1, starting transfers between devices, on_device(): lax.all_to_all(send.reshape(homes, PAIR, LANE), ('x', 'z'), 0, 0, tiled=T...  18.6 us
    all_to_all x1, waiting for transfers between devices, on_device(): lax.all_to_all(send.reshape(homes, PAIR, LANE), ('x', 'z'), 0, 0, tiled=T...  15.9 us
    unnamed x34, local copies, waits for them, and re-layouts  13.4 us
    ppermute x6, waiting for transfers between devices, shifted(): lax.ppermute(value, 'y', [(i, (i + by) % blocks) for i in range(blocks)])  12.2 us
    pallas_call x1, Pallas kernels, on_device(): pl.pallas_call(functools.partial(back_kernel, share), out_shape=jax.Shape...  4.67 us
  transfers between devices with their start and end apart: 8, of which 5 were waited for; matrix products, arithmetic and copies ran while one was open for 0% of the time, Pallas kernels for 2%

profile of v5, /device:TPU:6, one launch (start us, length us, event | category | flops | bytes accessed | tf_op | source)
XLA Modules:
  0.0 170.5 jit_solution(16982871173527952389)
XLA Ops:
  0.6 0.0 copy-start.8
  0.6 0.0 copy-start.9
  0.7 3.8 %send_rows.1 = bf16[2688,128]{1,0:T(8,128)(2,1)} custom-call(s32[8,128]{1,0:T(8,128)} %bitcast.18, f32[8,128]{1,0:T(8,128)} %bitcast.24, f32[224,128]{1,0:T(8,128)} %bitcast.23), custom_call_target="tpu_custom_call" | custom-call | flops 1000000000 | bytes 1000000 | tf_op jit(solution)/shard_map/send_rows/pallas_call | solution.py:303
  4.5 18.6 %all-to-all-start = ((bf16[48,56,128]{2,1,0:T(8,128)(2,1)}), bf16[48,56,128]{2,1,0:T(8,128)(2,1)S(1)}, u32[]{:S(2)}, u32[]{:S(2)}) async-start(bf16[48,56,128]{2,1,0:T(8,128)(2,1)} %bitcast.22), calls=%async_computation | async-start | bytes 1376256 | tf_op jit(solution)/shard_map/dispatch/all_to_all | solution.py:342
  23.0 0.0 copy-done.8
  23.0 0.0 copy-done.9
  23.1 0.0 copy-start
  23.1 1.7 %copy-done = bf16[3,432,1024]{2,1,0:T(8,128)(2,1)S(1)} copy-done((bf16[3,432,1024]{2,1,0:T(8,128)(2,1)S(1)}, bf16[3,432,1024]{2,1,0:T(8,128)(2,1)}, u32[]{:S(2)}) %copy-start) | copy-done | bytes 2654232
  24.8 1.7 %copy-done.5 = bf16[3,432,1024]{2,1,0:T(8,128)(2,1)S(1)} copy-done((bf16[3,432,1024]{2,1,0:T(8,128)(2,1)S(1)}, bf16[3,432,1024]{2,1,0:T(8,128)(2,1)}, u32[]{:S(2)}) %copy-start.5) | copy-done | bytes 2654232
  26.6 3.6 %prepare.1 = (f32[3,432,1024]{2,1,0:T(8,128)S(1)}, f32[3,432,1024]{2,1,0:T(8,128)S(1)}, bf16[896,864]{1,0:T(8,128)(2,1)S(1)}, bf16[256,2688]{1,0:T(8,128)(2,1)S(1)}, bf16[2688,144]{1,0:T(8,128)(2,1)S(1)}) custom-call(s32[8,128]{1,0:T(8,128)S(1)} %bitcast.19, f32[2,2688]{1,0:T(2,128)S(1)} %copy-done.8, bf16[3,432,1024]{2,1,0:T(8,128)(2,1)S(1)} %copy-done.5, ...), custom_call_target="tpu_custom_call" | custom-call | flops 20000000 | bytes 20000000 | tf_op jit(solution)/shard_map/prepare/pallas_call | solution.py:327
  30.1 0.0 copy-start.2
  30.2 2.3 %copy-done.2 = f32[3,432,1024]{2,1,0:T(8,128)} copy-done((f32[3,432,1024]{2,1,0:T(8,128)}, f32[3,432,1024]{2,1,0:T(8,128)S(1)}, u32[]{:S(2)}) %copy-start.2) | copy-done | bytes 5308440
  32.5 2.4 %copy-done.3 = f32[3,432,1024]{2,1,0:T(8,128)} copy-done((f32[3,432,1024]{2,1,0:T(8,128)}, f32[3,432,1024]{2,1,0:T(8,128)S(1)}, u32[]{:S(2)}) %copy-start.3) | copy-done | bytes 5308440
  34.9 1.1 copy-done.11
  36.0 1.2 copy-done.13
  37.1 0.1 pad_add_fusion.half_ref
  37.2 15.9 %all-to-all-done = bf16[48,56,128]{2,1,0:T(8,128)(2,1)S(1)} async-done(((bf16[48,56,128]{2,1,0:T(8,128)(2,1)}), bf16[48,56,128]{2,1,0:T(8,128)(2,1)S(1)}, u32[]{:S(2)}, u32[]{:S(2)}) %all-to-all-start) | async-done | bytes 688160 | tf_op jit(solution)/shard_map/dispatch/all_to_all | solution.py:342
  53.1 1.3 copy-done.10
  54.4 3.0 %down_other.1 = (bf16[3,448,256]{2,1,0:T(8,128)(2,1)S(1)}, bf16[8,656,128]{2,1,0:T(8,128)(2,1)S(1)}) custom-call(s32[2]{0:T(128)S(1)} %pad_add_fusion.half_ref, bf16[2688,128]{1,0:T(8,128)(2,1)S(1)} %bitcast.16, bf16[3,224,1024]{2,1,0:T(8,128)(2,1)S(1)} %copy-done.10), custom_call_target="tpu_custom_call" | custom-call | flops 1000000000 | bytes 4000000 | tf_op jit(solution)/shard_map/down_other/pallas_call | solution.py:345
  57.4 1.9 %collective-permute-start = (bf16[8,656,128]{2,1,0:T(8,128)(2,1)S(1)}, bf16[8,656,128]{2,1,0:T(8,128)(2,1)S(1)}, u32[]{:S(2)}, u32[]{:S(2)}) collective-permute-start(bf16[8,656,128]{2,1,0:T(8,128)(2,1)S(1)} %get-tuple-element.33), channel_id=1, source_target_pairs={{0,48},{48,0},{1,49},{49,1},{2,50},{50,2},{3,51},{51,3},{4,52},{52... | collective-permute-start | bytes 4030472 | tf_op jit(solution)/shard_map/swap_cores/ppermute | solution.py:354
  59.3 3.0 %collective-permute-done.plus_ref = bf16[8,656,128]{2,1,0:T(8,128)(2,1)S(1)} collective-permute-done((bf16[8,656,128]{2,1,0:T(8,128)(2,1)S(1)}, bf16[8,656,128]{2,1,0:T(8,128)(2,1)S(1)}, u32[]{:S(2)}, u32[]{:S(2)}) %collective-permute-start) | collective-permute-done | bytes 1343520 | tf_op jit(solution)/shard_map/swap_cores/ppermute | solution.py:354
  62.4 1.2 down_own.1
  63.6 3.5 %collective-permute-start.1 = (bf16[2,656,128]{2,1,0:T(8,128)(2,1)S(1)}, bf16[2,656,128]{2,1,0:T(8,128)(2,1)S(1)}, u32[]{:S(2)}, u32[]{:S(2)}) collective-permute-start(bf16[2,656,128]{2,1,0:T(8,128)(2,1)S(1)} %get-tuple-element.35), channel_id=1, source_target_pairs={{0,96},{96,192},{192,288},{288,384},{384,480},{480,576},{576,672},... | collective-permute-start | bytes 1007624 | tf_op jit(solution)/shard_map/sum_over_y/ppermute | solution.py:372
  67.1 3.8 %collective-permute-start.2 = (bf16[2,656,128]{2,1,0:T(8,128)(2,1)S(1)}, bf16[2,656,128]{2,1,0:T(8,128)(2,1)S(1)}, u32[]{:S(2)}, u32[]{:S(2)}) collective-permute-start(bf16[2,656,128]{2,1,0:T(8,128)(2,1)S(1)} %get-tuple-element.36), channel_id=1, source_target_pairs={{0,672},{96,0},{192,96},{288,192},{384,288},{480,384},{576,480},{6... | collective-permute-start | bytes 1007624 | tf_op jit(solution)/shard_map/sum_over_y/ppermute | solution.py:372
  70.9 3.0 %collective-permute-start.3 = (bf16[336,128]{1,0:T(8,128)(2,1)S(1)}, bf16[336,128]{1,0:T(8,128)(2,1)S(1)}, u32[]{:S(2)}, u32[]{:S(2)}) collective-permute-start(bf16[336,128]{1,0:T(8,128)(2,1)S(1)} %get-tuple-element.37), channel_id=1, source_target_pairs={{0,192},{96,288},{192,384},{288,480},{384,576},{480,672},{576,0},{... | collective-permute-start | bytes 258056 | tf_op jit(solution)/shard_map/sum_over_y/ppermute | solution.py:372
  74.0 4.9 %collective-permute-start.4 = (bf16[320,128]{1,0:T(8,128)(2,1)S(1)}, bf16[320,128]{1,0:T(8,128)(2,1)S(1)}, u32[]{:S(2)}, u32[]{:S(2)}) collective-permute-start(bf16[320,128]{1,0:T(8,128)(2,1)S(1)} %get-tuple-element.38), channel_id=1, source_target_pairs={{0,576},{96,672},{192,0},{288,96},{384,192},{480,288},{576,384},{6... | collective-permute-start | bytes 245768 | tf_op jit(solution)/shard_map/sum_over_y/ppermute | solution.py:372
  78.9 5.6 %collective-permute-done.4.left_far_ref = bf16[320,128]{1,0:T(8,128)(2,1)S(1)} collective-permute-done((bf16[320,128]{1,0:T(8,128)(2,1)S(1)}, bf16[320,128]{1,0:T(8,128)(2,1)S(1)}, u32[]{:S(2)}, u32[]{:S(2)}) %collective-permute-start.4) | collective-permute-done | bytes 81952 | tf_op jit(solution)/shard_map/sum_over_y/ppermute | solution.py:372
  84.5 0.0 collective-permute-done.3.right_far_ref
  84.5 0.0 collective-permute-done.1.right_ref
  84.5 0.0 collective-permute-done.2.left_ref
  84.5 0.1 sum_over_y.2
  84.6 5.6 %collective-permute-start.5 = (bf16[656,128]{1,0:T(8,128)(2,1)S(1)}, bf16[656,128]{1,0:T(8,128)(2,1)S(1)}, u32[]{:S(2)}, u32[]{:S(2)}) collective-permute-start(bf16[656,128]{1,0:T(8,128)(2,1)S(1)} %get-tuple-element.39), channel_id=1, source_target_pairs={{0,192},{96,288},{192,384},{288,480},{384,576},{480,672},{576,0},{... | collective-permute-start | bytes 503816 | tf_op jit(solution)/shard_map/sum_over_y/ppermute | solution.py:372
  90.2 2.4 %collective-permute-start.6 = (bf16[656,128]{1,0:T(8,128)(2,1)S(1)}, bf16[656,128]{1,0:T(8,128)(2,1)S(1)}, u32[]{:S(2)}, u32[]{:S(2)}) collective-permute-start(bf16[656,128]{1,0:T(8,128)(2,1)S(1)} %get-tuple-element.40), channel_id=1, source_target_pairs={{0,576},{96,672},{192,0},{288,96},{384,192},{480,288},{576,384},{6... | collective-permute-start | bytes 503816 | tf_op jit(solution)/shard_map/sum_over_y/ppermute | solution.py:372
  92.6 3.2 %collective-permute-done.5.right_two_ref = bf16[656,128]{1,0:T(8,128)(2,1)S(1)} collective-permute-done((bf16[656,128]{1,0:T(8,128)(2,1)S(1)}, bf16[656,128]{1,0:T(8,128)(2,1)S(1)}, u32[]{:S(2)}, u32[]{:S(2)}) %collective-permute-start.5) | collective-permute-done | bytes 167968 | tf_op jit(solution)/shard_map/sum_over_y/ppermute | solution.py:372
  95.8 3.4 %collective-permute-done.6.left_two_ref = bf16[656,128]{1,0:T(8,128)(2,1)S(1)} collective-permute-done((bf16[656,128]{1,0:T(8,128)(2,1)S(1)}, bf16[656,128]{1,0:T(8,128)(2,1)S(1)}, u32[]{:S(2)}, u32[]{:S(2)}) %collective-permute-start.6) | collective-permute-done | bytes 167968 | tf_op jit(solution)/shard_map/sum_over_y/ppermute | solution.py:372
  99.2 0.2 sum_over_y.3
  99.4 0.0 slice-start.1
  99.5 24.8 %all-gather.2 = f16[10752,128]{1,0:T(8,128)(2,1)S(1)} all-gather(f16[672,128]{1,0:T(8,128)(2,1)S(1)} %convert_element_type.6), channel_id=2, replica_groups=mesh['y'=8,'core'=2,'x'=4,'z'=12] {'y','core'}, dimensions={0}, use_global_device_ids=true | all-gather | bytes 2924544 | tf_op jit(solution)/shard_map/gather_hidden/all_gather | solution.py:394
  124.2 0.5 convert.grad_ref
  124.8 0.0 slice-done
  124.8 0.0 copy-done.7
  124.8 0.0 copy-done.4
  124.8 0.0 slice-done.1
  124.8 1.2 copy-done.1
  126.0 0.4 copy-done.6
  126.4 4.7 %back.1 = bf16[2688,128]{1,0:T(8,128)(2,1)S(1)} custom-call(f32[16,672,128]{2,1,0:T(8,128)S(1)} %convert.grad_ref, bf16[3,448,256]{2,1,0:T(8,128)(2,1)S(1)} %get-tuple-element.32.rows_ref, bf16[3,432,1024]{2,1,0:T(8,128)(2,1)S(1)} %copy-done.1, f32[3,432,1024]{2,1,0:T(8,128)S(1)} %bitcast.14, f32[3,432,1024]{2,1,0:T(8,128)S(1)} %copy-done.4, ...), custom_call_target="tpu_custom_call" | custom-call | flops 2000000000 | bytes 10000000 | tf_op jit(solution)/shard_map/back/pallas_call | solution.py:396
  131.1 36.9 %all_to_all.10 = bf16[48,56,128]{2,1,0:T(8,128)(2,1)S(1)} all-to-all(bf16[48,56,128]{2,1,0:T(8,128)(2,1)S(1)} %bitcast.15), channel_id=1, replica_groups=mesh['y'=8,'core'=2,'x'=4,'z'=12] {'x','z'}, dimensions={0} | all-to-all | bytes 1376256 | tf_op jit(solution)/shard_map/way_back/all_to_all | solution.py:410
  167.9 2.5 %combine.1 = (f32[224,128]{1,0:T(8,128)}, f32[8,128]{1,0:T(8,128)}) custom-call(s32[8,128]{1,0:T(8,128)S(1)} %bitcast.20, bf16[256,2688]{1,0:T(8,128)(2,1)S(1)} %copy-done.12, bf16[2688,144]{1,0:T(8,128)(2,1)S(1)} %copy-done.14, bf16[2688,128]{1,0:T(8,128)(2,1)S(1)} %bitcast.17), custom_call_target="tpu_custom_call" | custom-call | flops 1000000000 | bytes 1000000 | tf_op jit(solution)/shard_map/combine/pallas_call | solution.py:412
  (16 shorter events, 0.0 us)
Async XLA Ops:
  0.6 22.4 %copy-start.8 = (f32[2,2688]{1,0:T(2,128)S(1)}, f32[2,2688]{1,0:T(2,128)}, u32[]{:S(2)}) copy-start(f32[2,2688]{1,0:T(2,128)} %constant.12.clone.slots_ref) | copy-start | bytes 64516
  0.6 22.4 %copy-start.9 = (s32[128,8]{0,1:T(8,128)S(1)}, s32[128,8]{0,1:T(8,128)}, u32[]{:S(2)}) copy-start(s32[128,8]{0,1:T(8,128)} %param.11) | copy-start | bytes 12292
  4.5 48.6 %all-to-all-start = ((bf16[48,56,128]{2,1,0:T(8,128)(2,1)}), bf16[48,56,128]{2,1,0:T(8,128)(2,1)S(1)}, u32[]{:S(2)}, u32[]{:S(2)}) async-start(bf16[48,56,128]{2,1,0:T(8,128)(2,1)} %bitcast.22), calls=%async_computation | async-start | bytes 1376256 | tf_op jit(solution)/shard_map/dispatch/all_to_all | solution.py:342
  23.1 1.8 %copy-start = (bf16[3,432,1024]{2,1,0:T(8,128)(2,1)S(1)}, bf16[3,432,1024]{2,1,0:T(8,128)(2,1)}, u32[]{:S(2)}) copy-start(bf16[3,432,1024]{2,1,0:T(8,128)(2,1)} %up_ref.3) | copy-start | bytes 7962628
  24.8 1.7 %copy-start.5 = (bf16[3,432,1024]{2,1,0:T(8,128)(2,1)S(1)}, bf16[3,432,1024]{2,1,0:T(8,128)(2,1)}, u32[]{:S(2)}) copy-start(bf16[3,432,1024]{2,1,0:T(8,128)(2,1)} %gate_ref.1) | copy-start | bytes 7962628
  30.1 2.4 %copy-start.2 = (f32[3,432,1024]{2,1,0:T(8,128)}, f32[3,432,1024]{2,1,0:T(8,128)S(1)}, u32[]{:S(2)}) copy-start(f32[3,432,1024]{2,1,0:T(8,128)S(1)} %get-tuple-element.41.up_factor_ref) | copy-start | bytes 15925252
  32.5 2.4 %copy-start.3 = (f32[3,432,1024]{2,1,0:T(8,128)}, f32[3,432,1024]{2,1,0:T(8,128)S(1)}, u32[]{:S(2)}) copy-start(f32[3,432,1024]{2,1,0:T(8,128)S(1)} %get-tuple-element.42.gate_factor_ref) | copy-start | bytes 15925252
  34.9 1.1 copy-start.11
  36.0 1.2 copy-start.13
  53.1 1.3 copy-start.10
  57.4 5.0 %collective-permute-start = (bf16[8,656,128]{2,1,0:T(8,128)(2,1)S(1)}, bf16[8,656,128]{2,1,0:T(8,128)(2,1)S(1)}, u32[]{:S(2)}, u32[]{:S(2)}) collective-permute-start(bf16[8,656,128]{2,1,0:T(8,128)(2,1)S(1)} %get-tuple-element.33), channel_id=1, source_target_pairs={{0,48},{48,0},{1,49},{49,1},{2,50},{50,2},{3,51},{51,3},{4,52},{52... | collective-permute-start | bytes 4030472 | tf_op jit(solution)/shard_map/swap_cores/ppermute | solution.py:354
  62.4 62.4 %slice-start = ((s8[5308416]{0:T(1024)(128)(4,1)}), s8[1114112]{0:T(1024)(128)(4,1)S(1)}, s32[]{:S(2)}) async-start(s8[5308416]{0:T(1024)(128)(4,1)} %bitcast.13), calls=%async_computation.2 | async-start | bytes 2228224
  62.4 62.4 %copy-start.7 = (bf16[3,224,1024]{2,1,0:T(8,128)(2,1)S(1)}, bf16[3,224,1024]{2,1,0:T(8,128)(2,1)}, u32[]{:S(2)}) copy-start(bf16[3,224,1024]{2,1,0:T(8,128)(2,1)} %wu_ref.1) | copy-start | bytes 4128772
  63.6 20.9 %collective-permute-start.1 = (bf16[2,656,128]{2,1,0:T(8,128)(2,1)S(1)}, bf16[2,656,128]{2,1,0:T(8,128)(2,1)S(1)}, u32[]{:S(2)}, u32[]{:S(2)}) collective-permute-start(bf16[2,656,128]{2,1,0:T(8,128)(2,1)S(1)} %get-tuple-element.35), channel_id=1, source_target_pairs={{0,96},{96,192},{192,288},{288,384},{384,480},{480,576},{576,672},... | collective-permute-start | bytes 1007624 | tf_op jit(solution)/shard_map/sum_over_y/ppermute | solution.py:372
  67.1 17.4 %collective-permute-start.2 = (bf16[2,656,128]{2,1,0:T(8,128)(2,1)S(1)}, bf16[2,656,128]{2,1,0:T(8,128)(2,1)S(1)}, u32[]{:S(2)}, u32[]{:S(2)}) collective-permute-start(bf16[2,656,128]{2,1,0:T(8,128)(2,1)S(1)} %get-tuple-element.36), channel_id=1, source_target_pairs={{0,672},{96,0},{192,96},{288,192},{384,288},{480,384},{576,480},{6... | collective-permute-start | bytes 1007624 | tf_op jit(solution)/shard_map/sum_over_y/ppermute | solution.py:372
  70.9 13.6 %collective-permute-start.3 = (bf16[336,128]{1,0:T(8,128)(2,1)S(1)}, bf16[336,128]{1,0:T(8,128)(2,1)S(1)}, u32[]{:S(2)}, u32[]{:S(2)}) collective-permute-start(bf16[336,128]{1,0:T(8,128)(2,1)S(1)} %get-tuple-element.37), channel_id=1, source_target_pairs={{0,192},{96,288},{192,384},{288,480},{384,576},{480,672},{576,0},{... | collective-permute-start | bytes 258056 | tf_op jit(solution)/shard_map/sum_over_y/ppermute | solution.py:372
  74.0 10.5 %collective-permute-start.4 = (bf16[320,128]{1,0:T(8,128)(2,1)S(1)}, bf16[320,128]{1,0:T(8,128)(2,1)S(1)}, u32[]{:S(2)}, u32[]{:S(2)}) collective-permute-start(bf16[320,128]{1,0:T(8,128)(2,1)S(1)} %get-tuple-element.38), channel_id=1, source_target_pairs={{0,576},{96,672},{192,0},{288,96},{384,192},{480,288},{576,384},{6... | collective-permute-start | bytes 245768 | tf_op jit(solution)/shard_map/sum_over_y/ppermute | solution.py:372
  84.6 11.2 %collective-permute-start.5 = (bf16[656,128]{1,0:T(8,128)(2,1)S(1)}, bf16[656,128]{1,0:T(8,128)(2,1)S(1)}, u32[]{:S(2)}, u32[]{:S(2)}) collective-permute-start(bf16[656,128]{1,0:T(8,128)(2,1)S(1)} %get-tuple-element.39), channel_id=1, source_target_pairs={{0,192},{96,288},{192,384},{288,480},{384,576},{480,672},{576,0},{... | collective-permute-start | bytes 503816 | tf_op jit(solution)/shard_map/sum_over_y/ppermute | solution.py:372
  90.2 9.0 %collective-permute-start.6 = (bf16[656,128]{1,0:T(8,128)(2,1)S(1)}, bf16[656,128]{1,0:T(8,128)(2,1)S(1)}, u32[]{:S(2)}, u32[]{:S(2)}) collective-permute-start(bf16[656,128]{1,0:T(8,128)(2,1)S(1)} %get-tuple-element.40), channel_id=1, source_target_pairs={{0,576},{96,672},{192,0},{288,96},{384,192},{480,288},{576,384},{6... | collective-permute-start | bytes 503816 | tf_op jit(solution)/shard_map/sum_over_y/ppermute | solution.py:372
  99.2 25.6 %copy-start.4 = (f32[3,432,1024]{2,1,0:T(8,128)S(1)}, f32[3,432,1024]{2,1,0:T(8,128)}, u32[]{:S(2)}) copy-start(f32[3,432,1024]{2,1,0:T(8,128)} %copy-done.3) | copy-start | bytes 15925252
  99.4 25.4 %slice-start.1 = ((s8[5308416]{0:T(1024)(128)(4,1)}), s8[4194304]{0:T(1024)(128)(4,1)S(1)}, s32[]{:S(2)}) async-start(s8[5308416]{0:T(1024)(128)(4,1)} %bitcast.13), calls=%async_computation.3 | async-start | bytes 8388608
  124.2 1.7 %copy-start.1 = (bf16[3,432,1024]{2,1,0:T(8,128)(2,1)S(1)}, bf16[3,432,1024]{2,1,0:T(8,128)(2,1)}, u32[]{:S(2)}) copy-start(bf16[3,432,1024]{2,1,0:T(8,128)(2,1)} %up_ref.3) | copy-start | bytes 7962628
  124.2 2.1 %copy-start.6 = (bf16[3,224,1024]{2,1,0:T(8,128)(2,1)S(1)}, bf16[3,224,1024]{2,1,0:T(8,128)(2,1)}, u32[]{:S(2)}) copy-start(bf16[3,224,1024]{2,1,0:T(8,128)(2,1)} %wg_ref.1) | copy-start | bytes 4128772
  126.4 41.6 %copy-start.12 = (bf16[256,2688]{1,0:T(8,128)(2,1)S(1)}, bf16[256,2688]{1,0:T(8,128)(2,1)}, u32[]{:S(2)}) copy-start(bf16[256,2688]{1,0:T(8,128)(2,1)} %copy-done.11) | copy-start | bytes 4128772
  126.4 41.6 %copy-start.14 = (bf16[2688,144]{1,0:T(8,128)(2,1)S(1)}, bf16[2688,144]{1,0:T(8,128)(2,1)}, u32[]{:S(2)}) copy-start(bf16[2688,144]{1,0:T(8,128)(2,1)} %copy-done.13) | copy-start | bytes 2322436

commit v6 on v5

--- a/solution.py
+++ b/solution.py
@@ -146,24 +146,18 @@
     down_half(1 - half_ref[0], share, rows_ref, w_ref, out_ref)
 
 
-def down_kernel(share, half_ref, rows_ref, w_ref, plus_ref, own_ref, right_ref, left_ref, right_far_ref, left_far_ref, ring):
+def down_kernel(share, half_ref, rows_ref, w_ref, plus_ref, own_ref, right_ref, left_ref, far_ref, ring):
     down_half(half_ref[0], share, rows_ref, w_ref, ring, plus_ref, half_ref[1])
     for out, distances in ((own_ref, (0, 2, 6)), (right_ref, (1, 3)), (left_ref, (7, 5))):
         for i, k in enumerate(distances):
             out[i] = ring[k]
-    near = right_far_ref.shape[0]
-    right_far_ref[...] = ring[4, 0:near, :]
-    left_far_ref[...] = ring[4, near:, :]
-
-
-def relay_kernel(own_ref, right_ref, left_ref, right_far_ref, left_far_ref, right_out, left_out):
-    near = right_far_ref.shape[0]
-    right = own_ref[1].astype(F32) + right_ref[1].astype(F32)
-    left = own_ref[2].astype(F32) + left_ref[1].astype(F32)
-    right_out[0:near, :] = (right[0:near] + right_far_ref[...].astype(F32)).astype(BF16)
-    right_out[near:, :] = right[near:].astype(BF16)
-    left_out[0:near, :] = left[0:near].astype(BF16)
-    left_out[near:, :] = (left[near:] + left_far_ref[...].astype(F32)).astype(BF16)
+    far_ref[...] = ring[4]
+
+
+def relay_kernel(own_ref, right_ref, left_ref, far_ref, right_out, left_out):
+    right = own_ref[1].astype(F32) + right_ref[1].astype(F32) + far_ref[...].astype(F32)
+    right_out[...] = right.astype(BF16)
+    left_out[...] = (own_ref[2].astype(F32) + left_ref[1].astype(F32)).astype(BF16)
 
 
 def prepare_kernel(
@@ -354,15 +348,14 @@
         swapped = lax.ppermute(other, "core", [(0, 1), (1, 0)])
     with jax.named_scope("down_own"):
         tall = capacity + share
-        near = -(-tall // 32) * 16
-        own, right, left, right_far, left_far = pl.pallas_call(
+        own, right, left, far = pl.pallas_call(
             functools.partial(down_kernel, share),
             out_shape=[
                 jax.ShapeDtypeStruct(shape, BF16)
-                for shape in ((3, tall, LANE), (2, tall, LANE), (2, tall, LANE), (near, LANE), (tall - near, LANE))
+                for shape in ((3, tall, LANE), (2, tall, LANE), (2, tall, LANE), (tall, LANE))
             ],
             in_specs=[SMEM, VMEM, VMEM, VMEM],
-            out_specs=[VMEM] * 5,
+            out_specs=[VMEM] * 4,
             scratch_shapes=[pltpu.VMEM(half_shape.shape, BF16)],
             compiler_params=PARAMS,
             cost_estimate=cost(10**9, 4 * 10**6),
@@ -371,16 +364,15 @@
         def shifted(value, by):
             return lax.ppermute(value, "y", [(i, (i + by) % blocks) for i in range(blocks)])
 
-        right, left = shifted(right, 1), shifted(left, -1)
-        right_far, left_far = shifted(right_far, 2), shifted(left_far, -2)
+        right, left, far = shifted(right, 1), shifted(left, -1), shifted(far, 2)
         right_two, left_two = pl.pallas_call(
             relay_kernel,
             out_shape=[jax.ShapeDtypeStruct((tall, LANE), BF16)] * 2,
-            in_specs=[VMEM] * 5,
+            in_specs=[VMEM] * 4,
             out_specs=[VMEM] * 2,
             compiler_params=PARAMS,
             cost_estimate=cost(10**6, 2 * 10**6),
-        )(own, right, left, right_far, left_far)
+        )(own, right, left, far)
         right_two, left_two = shifted(right_two, 2), shifted(left_two, -2)
         scaled = pl.pallas_call(
             sum_kernel,

time: 172 us -> 175 us (1.017)
  waiting for transfers between devices: 31.1 us -> 37.7 us
  starting transfers between devices: 43.7 us -> 38.8 us
  blocking collectives: 61.7 us -> 64 us
    ppermute x6 -> x5, waiting for transfers between devices: 12.2 us -> 18.8 us  [shifted(): lax.ppermute(value, 'y', [(i, (i + by) % blocks) for i in range(blocks)])]
    ppermute x6 -> x5, starting transfers between devices: 23.2 us -> 18.3 us  [shifted(): lax.ppermute(value, 'y', [(i, (i + by) % blocks) for i in range(blocks)])]
    all_gather x1, blocking collectives: 24.8 us -> 27.1 us  [on_device(): lax.all_gather(scaled.astype(jnp.float16), ('y', 'core'), axis=0)]
  transfers between devices with their start and end apart: 8 -> 7, of which waited for: 5 -> 5; matrix products, arithmetic and copies ran while one was open for 0% -> 0% of each run, Pallas kernels for 2% -> 2%
where the time goes in v6:
time: 175 us; the launch traced here: 174 us
  blocking collectives  64 us (37%)
  starting transfers between devices  38.8 us (22%)
  waiting for transfers between devices  37.7 us (22%)
  Pallas kernels  19.1 us (11%)
  local copies, waits for them, and re-layouts  13.4 us (8%)
    all_to_all x1, blocking collectives, on_device(): lax.all_to_all(back.reshape(homes, PAIR, LANE), ('x', 'z'), 0, 0, tiled=T...  36.9 us
    all_gather x1, blocking collectives, on_device(): lax.all_gather(scaled.astype(jnp.float16), ('y', 'core'), axis=0)  27.1 us
    ppermute x5, waiting for transfers between devices, shifted(): lax.ppermute(value, 'y', [(i, (i + by) % blocks) for i in range(blocks)])  18.8 us
    all_to_all x1, starting transfers between devices, on_device(): lax.all_to_all(send.reshape(homes, PAIR, LANE), ('x', 'z'), 0, 0, tiled=T...  18.6 us
    ppermute x5, starting transfers between devices, shifted(): lax.ppermute(value, 'y', [(i, (i + by) % blocks) for i in range(blocks)])  18.3 us
    all_to_all x1, waiting for transfers between devices, on_device(): lax.all_to_all(send.reshape(homes, PAIR, LANE), ('x', 'z'), 0, 0, tiled=T...  15.8 us
    unnamed x34, local copies, waits for them, and re-layouts  13.4 us
    pallas_call x1, Pallas kernels, on_device(): pl.pallas_call(functools.partial(back_kernel, share), out_shape=jax.Shape...  4.67 us
  transfers between devices with their start and end apart: 7, of which 5 were waited for; matrix products, arithmetic and copies ran while one was open for 0% of the time, Pallas kernels for 2%

profile of v6, /device:TPU:6, one launch (start us, length us, event | category | flops | bytes accessed | tf_op | source)
XLA Modules:
  0.0 174.4 jit_solution(1475278720422740592)
XLA Ops:
  0.6 0.0 copy-start.8
  0.6 0.0 copy-start.9
  0.7 3.8 %send_rows.1 = bf16[2688,128]{1,0:T(8,128)(2,1)} custom-call(s32[8,128]{1,0:T(8,128)} %bitcast.18, f32[8,128]{1,0:T(8,128)} %bitcast.24, f32[224,128]{1,0:T(8,128)} %bitcast.23), custom_call_target="tpu_custom_call" | custom-call | flops 1000000000 | bytes 1000000 | tf_op jit(solution)/shard_map/send_rows/pallas_call | solution.py:297
  4.4 18.6 %all-to-all-start = ((bf16[48,56,128]{2,1,0:T(8,128)(2,1)}), bf16[48,56,128]{2,1,0:T(8,128)(2,1)S(1)}, u32[]{:S(2)}, u32[]{:S(2)}) async-start(bf16[48,56,128]{2,1,0:T(8,128)(2,1)} %bitcast.22), calls=%async_computation | async-start | bytes 1376256 | tf_op jit(solution)/shard_map/dispatch/all_to_all | solution.py:336
  23.0 0.0 copy-done.8
  23.0 0.0 copy-done.9
  23.0 0.0 copy-start
  23.1 1.7 copy-done
  24.8 1.7 %copy-done.5 = bf16[3,432,1024]{2,1,0:T(8,128)(2,1)S(1)} copy-done((bf16[3,432,1024]{2,1,0:T(8,128)(2,1)S(1)}, bf16[3,432,1024]{2,1,0:T(8,128)(2,1)}, u32[]{:S(2)}) %copy-start.5) | copy-done | bytes 2654232
  26.6 3.6 %prepare.1 = (f32[3,432,1024]{2,1,0:T(8,128)S(1)}, f32[3,432,1024]{2,1,0:T(8,128)S(1)}, bf16[896,864]{1,0:T(8,128)(2,1)S(1)}, bf16[256,2688]{1,0:T(8,128)(2,1)S(1)}, bf16[2688,144]{1,0:T(8,128)(2,1)S(1)}) custom-call(s32[8,128]{1,0:T(8,128)S(1)} %bitcast.19, f32[2,2688]{1,0:T(2,128)S(1)} %copy-done.8, bf16[3,432,1024]{2,1,0:T(8,128)(2,1)S(1)} %copy-done.5, ...), custom_call_target="tpu_custom_call" | custom-call | flops 20000000 | bytes 20000000 | tf_op jit(solution)/shard_map/prepare/pallas_call | solution.py:321
  30.1 0.0 copy-start.2
  30.2 2.3 %copy-done.2 = f32[3,432,1024]{2,1,0:T(8,128)} copy-done((f32[3,432,1024]{2,1,0:T(8,128)}, f32[3,432,1024]{2,1,0:T(8,128)S(1)}, u32[]{:S(2)}) %copy-start.2) | copy-done | bytes 5308440
  32.5 2.4 %copy-done.3 = f32[3,432,1024]{2,1,0:T(8,128)} copy-done((f32[3,432,1024]{2,1,0:T(8,128)}, f32[3,432,1024]{2,1,0:T(8,128)S(1)}, u32[]{:S(2)}) %copy-start.3) | copy-done | bytes 5308440
  34.9 1.1 copy-done.11
  36.0 1.2 copy-done.13
  37.1 0.1 pad_add_fusion.half_ref
  37.2 15.8 %all-to-all-done = bf16[48,56,128]{2,1,0:T(8,128)(2,1)S(1)} async-done(((bf16[48,56,128]{2,1,0:T(8,128)(2,1)}), bf16[48,56,128]{2,1,0:T(8,128)(2,1)S(1)}, u32[]{:S(2)}, u32[]{:S(2)}) %all-to-all-start) | async-done | bytes 688160 | tf_op jit(solution)/shard_map/dispatch/all_to_all | solution.py:336
  53.1 1.3 copy-done.10
  54.4 3.0 %down_other.1 = (bf16[3,448,256]{2,1,0:T(8,128)(2,1)S(1)}, bf16[8,656,128]{2,1,0:T(8,128)(2,1)S(1)}) custom-call(s32[2]{0:T(128)S(1)} %pad_add_fusion.half_ref, bf16[2688,128]{1,0:T(8,128)(2,1)S(1)} %bitcast.16, bf16[3,224,1024]{2,1,0:T(8,128)(2,1)S(1)} %copy-done.10), custom_call_target="tpu_custom_call" | custom-call | flops 1000000000 | bytes 4000000 | tf_op jit(solution)/shard_map/down_other/pallas_call | solution.py:339
  57.4 1.9 %collective-permute-start = (bf16[8,656,128]{2,1,0:T(8,128)(2,1)S(1)}, bf16[8,656,128]{2,1,0:T(8,128)(2,1)S(1)}, u32[]{:S(2)}, u32[]{:S(2)}) collective-permute-start(bf16[8,656,128]{2,1,0:T(8,128)(2,1)S(1)} %get-tuple-element.32), channel_id=1, source_target_pairs={{0,48},{48,0},{1,49},{49,1},{2,50},{50,2},{3,51},{51,3},{4,52},{52... | collective-permute-start | bytes 4030472 | tf_op jit(solution)/shard_map/swap_cores/ppermute | solution.py:348
  59.3 3.0 %collective-permute-done.plus_ref = bf16[8,656,128]{2,1,0:T(8,128)(2,1)S(1)} collective-permute-done((bf16[8,656,128]{2,1,0:T(8,128)(2,1)S(1)}, bf16[8,656,128]{2,1,0:T(8,128)(2,1)S(1)}, u32[]{:S(2)}, u32[]{:S(2)}) %collective-permute-start) | collective-permute-done | bytes 1343520 | tf_op jit(solution)/shard_map/swap_cores/ppermute | solution.py:348
  62.4 1.2 down_own.1
  63.6 3.5 %collective-permute-start.1 = (bf16[2,656,128]{2,1,0:T(8,128)(2,1)S(1)}, bf16[2,656,128]{2,1,0:T(8,128)(2,1)S(1)}, u32[]{:S(2)}, u32[]{:S(2)}) collective-permute-start(bf16[2,656,128]{2,1,0:T(8,128)(2,1)S(1)} %get-tuple-element.34), channel_id=1, source_target_pairs={{0,96},{96,192},{192,288},{288,384},{384,480},{480,576},{576,672},... | collective-permute-start | bytes 1007624 | tf_op jit(solution)/shard_map/sum_over_y/ppermute | solution.py:365
  67.1 3.8 %collective-permute-start.2 = (bf16[2,656,128]{2,1,0:T(8,128)(2,1)S(1)}, bf16[2,656,128]{2,1,0:T(8,128)(2,1)S(1)}, u32[]{:S(2)}, u32[]{:S(2)}) collective-permute-start(bf16[2,656,128]{2,1,0:T(8,128)(2,1)S(1)} %get-tuple-element.35), channel_id=1, source_target_pairs={{0,672},{96,0},{192,96},{288,192},{384,288},{480,384},{576,480},{6... | collective-permute-start | bytes 1007624 | tf_op jit(solution)/shard_map/sum_over_y/ppermute | solution.py:365
  70.9 3.0 %collective-permute-start.3 = (bf16[656,128]{1,0:T(8,128)(2,1)S(1)}, bf16[656,128]{1,0:T(8,128)(2,1)S(1)}, u32[]{:S(2)}, u32[]{:S(2)}) collective-permute-start(bf16[656,128]{1,0:T(8,128)(2,1)S(1)} %get-tuple-element.36), channel_id=1, source_target_pairs={{0,192},{96,288},{192,384},{288,480},{384,576},{480,672},{576,0},{... | collective-permute-start | bytes 503816 | tf_op jit(solution)/shard_map/sum_over_y/ppermute | solution.py:365
  74.0 9.6 %collective-permute-done.3.far_ref = bf16[656,128]{1,0:T(8,128)(2,1)S(1)} collective-permute-done((bf16[656,128]{1,0:T(8,128)(2,1)S(1)}, bf16[656,128]{1,0:T(8,128)(2,1)S(1)}, u32[]{:S(2)}, u32[]{:S(2)}) %collective-permute-start.3) | collective-permute-done | bytes 167968 | tf_op jit(solution)/shard_map/sum_over_y/ppermute | solution.py:365
  83.5 0.0 collective-permute-done.1.right_ref
  83.5 0.0 collective-permute-done.2.left_ref
  83.5 0.1 sum_over_y.2
  83.7 4.0 %collective-permute-start.4 = (bf16[656,128]{1,0:T(8,128)(2,1)S(1)}, bf16[656,128]{1,0:T(8,128)(2,1)S(1)}, u32[]{:S(2)}, u32[]{:S(2)}) collective-permute-start(bf16[656,128]{1,0:T(8,128)(2,1)S(1)} %get-tuple-element.37), channel_id=1, source_target_pairs={{0,192},{96,288},{192,384},{288,480},{384,576},{480,672},{576,0},{... | collective-permute-start | bytes 503816 | tf_op jit(solution)/shard_map/sum_over_y/ppermute | solution.py:365
  87.6 4.0 %collective-permute-start.5 = (bf16[656,128]{1,0:T(8,128)(2,1)S(1)}, bf16[656,128]{1,0:T(8,128)(2,1)S(1)}, u32[]{:S(2)}, u32[]{:S(2)}) collective-permute-start(bf16[656,128]{1,0:T(8,128)(2,1)S(1)} %get-tuple-element.38), channel_id=1, source_target_pairs={{0,576},{96,672},{192,0},{288,96},{384,192},{480,288},{576,384},{6... | collective-permute-start | bytes 503816 | tf_op jit(solution)/shard_map/sum_over_y/ppermute | solution.py:365
  91.6 2.1 %collective-permute-done.4.right_two_ref = bf16[656,128]{1,0:T(8,128)(2,1)S(1)} collective-permute-done((bf16[656,128]{1,0:T(8,128)(2,1)S(1)}, bf16[656,128]{1,0:T(8,128)(2,1)S(1)}, u32[]{:S(2)}, u32[]{:S(2)}) %collective-permute-start.4) | collective-permute-done | bytes 167968 | tf_op jit(solution)/shard_map/sum_over_y/ppermute | solution.py:365
  93.7 7.1 %collective-permute-done.5.left_two_ref = bf16[656,128]{1,0:T(8,128)(2,1)S(1)} collective-permute-done((bf16[656,128]{1,0:T(8,128)(2,1)S(1)}, bf16[656,128]{1,0:T(8,128)(2,1)S(1)}, u32[]{:S(2)}, u32[]{:S(2)}) %collective-permute-start.5) | collective-permute-done | bytes 167968 | tf_op jit(solution)/shard_map/sum_over_y/ppermute | solution.py:365
  100.9 0.2 sum_over_y.3
  101.1 0.0 slice-start.1
  101.1 27.1 %all-gather.2 = f16[10752,128]{1,0:T(8,128)(2,1)S(1)} all-gather(f16[672,128]{1,0:T(8,128)(2,1)S(1)} %convert_element_type.6), channel_id=2, replica_groups=mesh['y'=8,'core'=2,'x'=4,'z'=12] {'y','core'}, dimensions={0}, use_global_device_ids=true | all-gather | bytes 2924544 | tf_op jit(solution)/shard_map/gather_hidden/all_gather | solution.py:386
  128.2 0.5 convert.grad_ref
  128.8 0.0 slice-done
  128.8 0.0 copy-done.7
  128.8 0.0 copy-done.4
  128.8 0.0 slice-done.1
  128.8 1.2 copy-done.1
  130.0 0.4 copy-done.6
  130.4 4.7 %back.1 = bf16[2688,128]{1,0:T(8,128)(2,1)S(1)} custom-call(f32[16,672,128]{2,1,0:T(8,128)S(1)} %convert.grad_ref, bf16[3,448,256]{2,1,0:T(8,128)(2,1)S(1)} %get-tuple-element.31.rows_ref, bf16[3,432,1024]{2,1,0:T(8,128)(2,1)S(1)} %copy-done.1, f32[3,432,1024]{2,1,0:T(8,128)S(1)} %bitcast.14, f32[3,432,1024]{2,1,0:T(8,128)S(1)} %copy-done.4, ...), custom_call_target="tpu_custom_call" | custom-call | flops 2000000000 | bytes 10000000 | tf_op jit(solution)/shard_map/back/pallas_call | solution.py:388
  135.0 36.9 %all_to_all.10 = bf16[48,56,128]{2,1,0:T(8,128)(2,1)S(1)} all-to-all(bf16[48,56,128]{2,1,0:T(8,128)(2,1)S(1)} %bitcast.15), channel_id=1, replica_groups=mesh['y'=8,'core'=2,'x'=4,'z'=12] {'x','z'}, dimensions={0} | all-to-all | bytes 1376256 | tf_op jit(solution)/shard_map/way_back/all_to_all | solution.py:402
  171.9 0.0 copy-done.12
  171.9 0.0 copy-done.14
  171.9 2.5 %combine.1 = (f32[224,128]{1,0:T(8,128)}, f32[8,128]{1,0:T(8,128)}) custom-call(s32[8,128]{1,0:T(8,128)S(1)} %bitcast.20, bf16[256,2688]{1,0:T(8,128)(2,1)S(1)} %copy-done.12, bf16[2688,144]{1,0:T(8,128)(2,1)S(1)} %copy-done.14, bf16[2688,128]{1,0:T(8,128)(2,1)S(1)} %bitcast.17), custom_call_target="tpu_custom_call" | custom-call | flops 1000000000 | bytes 1000000 | tf_op jit(solution)/shard_map/combine/pallas_call | solution.py:404
  (14 shorter events, 0.0 us)
Async XLA Ops:
  0.6 22.4 %copy-start.8 = (f32[2,2688]{1,0:T(2,128)S(1)}, f32[2,2688]{1,0:T(2,128)}, u32[]{:S(2)}) copy-start(f32[2,2688]{1,0:T(2,128)} %constant.12.clone.slots_ref) | copy-start | bytes 64516
  0.6 22.4 %copy-start.9 = (s32[128,8]{0,1:T(8,128)S(1)}, s32[128,8]{0,1:T(8,128)}, u32[]{:S(2)}) copy-start(s32[128,8]{0,1:T(8,128)} %param.11) | copy-start | bytes 12292
  4.4 48.6 %all-to-all-start = ((bf16[48,56,128]{2,1,0:T(8,128)(2,1)}), bf16[48,56,128]{2,1,0:T(8,128)(2,1)S(1)}, u32[]{:S(2)}, u32[]{:S(2)}) async-start(bf16[48,56,128]{2,1,0:T(8,128)(2,1)} %bitcast.22), calls=%async_computation | async-start | bytes 1376256 | tf_op jit(solution)/shard_map/dispatch/all_to_all | solution.py:336
  23.0 1.8 %copy-start = (bf16[3,432,1024]{2,1,0:T(8,128)(2,1)S(1)}, bf16[3,432,1024]{2,1,0:T(8,128)(2,1)}, u32[]{:S(2)}) copy-start(bf16[3,432,1024]{2,1,0:T(8,128)(2,1)} %up_ref.3) | copy-start | bytes 7962628
  24.8 1.7 %copy-start.5 = (bf16[3,432,1024]{2,1,0:T(8,128)(2,1)S(1)}, bf16[3,432,1024]{2,1,0:T(8,128)(2,1)}, u32[]{:S(2)}) copy-start(bf16[3,432,1024]{2,1,0:T(8,128)(2,1)} %gate_ref.1) | copy-start | bytes 7962628
  30.1 2.4 %copy-start.2 = (f32[3,432,1024]{2,1,0:T(8,128)}, f32[3,432,1024]{2,1,0:T(8,128)S(1)}, u32[]{:S(2)}) copy-start(f32[3,432,1024]{2,1,0:T(8,128)S(1)} %get-tuple-element.39.up_factor_ref) | copy-start | bytes 15925252
  32.5 2.4 %copy-start.3 = (f32[3,432,1024]{2,1,0:T(8,128)}, f32[3,432,1024]{2,1,0:T(8,128)S(1)}, u32[]{:S(2)}) copy-start(f32[3,432,1024]{2,1,0:T(8,128)S(1)} %get-tuple-element.40.gate_factor_ref) | copy-start | bytes 15925252
  34.9 1.1 copy-start.11
  36.0 1.2 copy-start.13
  53.1 1.3 copy-start.10
  57.4 5.0 %collective-permute-start = (bf16[8,656,128]{2,1,0:T(8,128)(2,1)S(1)}, bf16[8,656,128]{2,1,0:T(8,128)(2,1)S(1)}, u32[]{:S(2)}, u32[]{:S(2)}) collective-permute-start(bf16[8,656,128]{2,1,0:T(8,128)(2,1)S(1)} %get-tuple-element.32), channel_id=1, source_target_pairs={{0,48},{48,0},{1,49},{49,1},{2,50},{50,2},{3,51},{51,3},{4,52},{52... | collective-permute-start | bytes 4030472 | tf_op jit(solution)/shard_map/swap_cores/ppermute | solution.py:348
  62.4 66.4 %slice-start = ((s8[5308416]{0:T(1024)(128)(4,1)}), s8[1114112]{0:T(1024)(128)(4,1)S(1)}, s32[]{:S(2)}) async-start(s8[5308416]{0:T(1024)(128)(4,1)} %bitcast.13), calls=%async_computation.2 | async-start | bytes 2228224
  62.4 66.4 %copy-start.7 = (bf16[3,224,1024]{2,1,0:T(8,128)(2,1)S(1)}, bf16[3,224,1024]{2,1,0:T(8,128)(2,1)}, u32[]{:S(2)}) copy-start(bf16[3,224,1024]{2,1,0:T(8,128)(2,1)} %wu_ref.1) | copy-start | bytes 4128772
  63.6 19.9 %collective-permute-start.1 = (bf16[2,656,128]{2,1,0:T(8,128)(2,1)S(1)}, bf16[2,656,128]{2,1,0:T(8,128)(2,1)S(1)}, u32[]{:S(2)}, u32[]{:S(2)}) collective-permute-start(bf16[2,656,128]{2,1,0:T(8,128)(2,1)S(1)} %get-tuple-element.34), channel_id=1, source_target_pairs={{0,96},{96,192},{192,288},{288,384},{384,480},{480,576},{576,672},... | collective-permute-start | bytes 1007624 | tf_op jit(solution)/shard_map/sum_over_y/ppermute | solution.py:365
  67.1 16.4 %collective-permute-start.2 = (bf16[2,656,128]{2,1,0:T(8,128)(2,1)S(1)}, bf16[2,656,128]{2,1,0:T(8,128)(2,1)S(1)}, u32[]{:S(2)}, u32[]{:S(2)}) collective-permute-start(bf16[2,656,128]{2,1,0:T(8,128)(2,1)S(1)} %get-tuple-element.35), channel_id=1, source_target_pairs={{0,672},{96,0},{192,96},{288,192},{384,288},{480,384},{576,480},{6... | collective-permute-start | bytes 1007624 | tf_op jit(solution)/shard_map/sum_over_y/ppermute | solution.py:365
  70.9 12.6 %collective-permute-start.3 = (bf16[656,128]{1,0:T(8,128)(2,1)S(1)}, bf16[656,128]{1,0:T(8,128)(2,1)S(1)}, u32[]{:S(2)}, u32[]{:S(2)}) collective-permute-start(bf16[656,128]{1,0:T(8,128)(2,1)S(1)} %get-tuple-element.36), channel_id=1, source_target_pairs={{0,192},{96,288},{192,384},{288,480},{384,576},{480,672},{576,0},{... | collective-permute-start | bytes 503816 | tf_op jit(solution)/shard_map/sum_over_y/ppermute | solution.py:365
  83.7 10.1 %collective-permute-start.4 = (bf16[656,128]{1,0:T(8,128)(2,1)S(1)}, bf16[656,128]{1,0:T(8,128)(2,1)S(1)}, u32[]{:S(2)}, u32[]{:S(2)}) collective-permute-start(bf16[656,128]{1,0:T(8,128)(2,1)S(1)} %get-tuple-element.37), channel_id=1, source_target_pairs={{0,192},{96,288},{192,384},{288,480},{384,576},{480,672},{576,0},{... | collective-permute-start | bytes 503816 | tf_op jit(solution)/shard_map/sum_over_y/ppermute | solution.py:365
  87.6 13.2 %collective-permute-start.5 = (bf16[656,128]{1,0:T(8,128)(2,1)S(1)}, bf16[656,128]{1,0:T(8,128)(2,1)S(1)}, u32[]{:S(2)}, u32[]{:S(2)}) collective-permute-start(bf16[656,128]{1,0:T(8,128)(2,1)S(1)} %get-tuple-element.38), channel_id=1, source_target_pairs={{0,576},{96,672},{192,0},{288,96},{384,192},{480,288},{576,384},{6... | collective-permute-start | bytes 503816 | tf_op jit(solution)/shard_map/sum_over_y/ppermute | solution.py:365
  100.9 27.9 %copy-start.4 = (f32[3,432,1024]{2,1,0:T(8,128)S(1)}, f32[3,432,1024]{2,1,0:T(8,128)}, u32[]{:S(2)}) copy-start(f32[3,432,1024]{2,1,0:T(8,128)} %copy-done.3) | copy-start | bytes 15925252
  101.1 27.7 %slice-start.1 = ((s8[5308416]{0:T(1024)(128)(4,1)}), s8[4194304]{0:T(1024)(128)(4,1)S(1)}, s32[]{:S(2)}) async-start(s8[5308416]{0:T(1024)(128)(4,1)} %bitcast.13), calls=%async_computation.3 | async-start | bytes 8388608
  128.2 1.7 %copy-start.1 = (bf16[3,432,1024]{2,1,0:T(8,128)(2,1)S(1)}, bf16[3,432,1024]{2,1,0:T(8,128)(2,1)}, u32[]{:S(2)}) copy-start(bf16[3,432,1024]{2,1,0:T(8,128)(2,1)} %up_ref.3) | copy-start | bytes 7962628
  128.2 2.1 %copy-start.6 = (bf16[3,224,1024]{2,1,0:T(8,128)(2,1)S(1)}, bf16[3,224,1024]{2,1,0:T(8,128)(2,1)}, u32[]{:S(2)}) copy-start(bf16[3,224,1024]{2,1,0:T(8,128)(2,1)} %wg_ref.1) | copy-start | bytes 4128772
  130.4 41.6 %copy-start.12 = (bf16[256,2688]{1,0:T(8,128)(2,1)S(1)}, bf16[256,2688]{1,0:T(8,128)(2,1)}, u32[]{:S(2)}) copy-start(bf16[256,2688]{1,0:T(8,128)(2,1)} %copy-done.11) | copy-start | bytes 4128772
  130.4 41.6 %copy-start.14 = (bf16[2688,144]{1,0:T(8,128)(2,1)S(1)}, bf16[2688,144]{1,0:T(8,128)(2,1)}, u32[]{:S(2)}) copy-start(bf16[2688,144]{1,0:T(8,128)(2,1)} %copy-done.13) | copy-start | bytes 2322436
